TPU v7x, 32 devices: a whole 2x2x4 slice. The times are simulated.
32 devices in a mesh: groups: 2 (over x), row: 4 (over z), col: 4 (over y, core).
Axes of the slice: x: 2, y: 2, z: 4, core: 2. Of those that a mesh axis runs over, the one named last changes fastest.
Arguments:
- tokens: bfloat16 [1024, 6144], P(('groups', 'row'), 'col'), parts along dimension 0, may hold values from -6 to 6
- cotangent: bfloat16 [1024, 6144], P(('groups', 'row'), 'col'), parts along dimension 0, may hold values from -0.625 to 0.625
- up_weight: bfloat16 [6144, 24576], P('col', 'row'), may hold values from -0.078125 to 0.078125
- down_weight: bfloat16 [24576, 6144], P('row', 'col'), may hold values from -0.0390625 to 0.0390625
- up_mask: int32 [48, 192], P('col', 'row'), may hold values from 0 to 1, as said below
- down_mask: int32 [192, 48], P('row', 'col'), may hold values from 0 to 1, as said below
Outputs:
- up_grad: bfloat16 [12288, 24576], P(('groups', 'col'), 'row'), parts along dimension 0
- down_grad: bfloat16 [49152, 6144], P(('groups', 'row'), 'col'), parts along dimension 0
There are 2 independent parts, one for each index of `groups`. A program takes and returns all parts, laid end to end along the dimension named above; an argument that names none is the same for every part. Nothing has to cross between parts.
Inputs may be any that keep to these rules, and one draw needn't show every extreme that they name: `up_mask`: 1 keeps a 128 x 128 block of up_weight, 0 prunes it; the share kept differs from block row to block row and block column to block column. `down_mask`: 1 keeps a 128 x 128 block of down_weight, 0 prunes it; the share kept differs from block row to block row and block column to block column.
All inputs are finite; a program needn't handle non-finite values.
Results may differ from a plain program's by a relative error of at most 0.015.
Values may be sent and summed in bfloat16 or wider, within the bound.
No kernel may reach another device: no remote copies, remote signals or barrier semaphores. Data moves between devices by JAX's collectives and lax.ppermute only.
A program may use at most 320 MiB of HBM per device.

v0:
```python
import functools

import jax
import jax.numpy as jnp
from jax import lax
from jax.experimental import pallas as pl
from jax.experimental.pallas import tpu as pltpu
from jax.sharding import PartitionSpec as P

BLOCK = 128
CORES = 2
VMEM_BYTES = 20 * 1024 * 1024

SQRT_HALF = 0.7071067811865476
INV_ROOT_TWO_PI = 0.3989422804014327

ANY = pl.BlockSpec(memory_space=pl.ANY)
VMEM = pl.BlockSpec(memory_space=pltpu.VMEM)

TICKET = jax.ShapeDtypeStruct((8, 128), jnp.float32)

BRIEF = pl.CostEstimate(flops=10**10, bytes_accessed=0, transcendentals=0)


CUTS = {
    "h0": (2, 2, 4),
    "h0s": (2, 2, 4),
    "g0": (4, 4),
    "g0s": (4, 4),
    "h1": (2, 2, 4),
    "h1s": (2, 2, 4),
    "g1": (2, 2, 2, 1, 1),
    "g1s": (2, 2, 2, 2),
    "a": (2, 2, 4),
    "e": (2, 2, 2, 1, 1),
}

ORDER = [
    ("send", "h0s", 0),
    ("turn", "x", 0),
    ("turn", "x", 1),
    ("send", "h0s", 1),
    ("add", "h0", 0),
    ("send", "h0s", 2),
    ("add", "h0", 1),
    ("send", "g0s", 0, ("x", 1)),
    ("turn", "x", 2),
    ("add", "h0", 2),
    ("send", "g0s", 1, ("h0", 0)),
    ("add", "g0", 0),
    ("add", "g0", 1, ("x", 0)),
    ("stack", "x", 0, ("h0", 2)),
    ("turn", "c", 0),
    ("send", "h1s", 0),
    ("send", "h1s", 2),
    ("send", "h1s", 1, ("g0", 0), ("h0", 1)),
    ("add", "h1", 0),
    ("turn", "c", 2),
    ("turn", "c", 1),
    ("add", "h1", 1),
    ("add", "h1", 2, ("g0", 1)),
    ("act", "a", 0),
    ("act", "a", 1, ("c", 0)),
    ("stack", "c", 0),
    ("send", "g1s", 0),
    ("down", "a", 0),
    ("add", "g1", 0),
    ("send", "g1s", 1),
    ("down", "a", 1),
    ("add", "g1", 1),
    ("send", "g1s", 2),
    ("send", "g1s", 3),
    ("act", "a", 2),
    ("add", "g1", 2),
    ("add", "g1", 3),
    ("add", "g1", 4),
    ("down", "a", 2),
    ("hidden", "e", 0),
    ("hidden", "e", 1),
    ("up", "e", 0),
    ("up", "e", 1),
    ("hidden", "e", 2),
    ("upmine", "e", 2),
    ("upother", "e", 2),
    ("hidden", "e", 3),
    ("upmine", "e", 3),
    ("upother", "e", 3),
    ("hidden", "e", 4),
    ("upmine", "e", 4),
    ("upother", "e", 4),
]


def tile_of(extent, most, *offsets):
    return max(
        width
        for width in range(BLOCK, most + 1, BLOCK)
        if all(size % width == 0 for size in (extent, *offsets))
    )


def spread_mask(mask, rows, columns):
    tall, wide = mask.shape
    bits = mask[...].astype(jnp.bfloat16)
    if rows[1] != tall:
        at = (rows[1], tall)
        pick = lax.broadcasted_iota(jnp.int32, at, 0) + rows[0] == lax.broadcasted_iota(jnp.int32, at, 1)
        bits = jnp.dot(pick.astype(jnp.bfloat16), bits, preferred_element_type=jnp.float32).astype(jnp.bfloat16)
    at = (wide, columns[1] * BLOCK)
    pick = lax.broadcasted_iota(jnp.int32, at, 1) // BLOCK + columns[0] == lax.broadcasted_iota(jnp.int32, at, 0)
    return jnp.dot(bits, pick.astype(jnp.bfloat16), preferred_element_type=jnp.float32).astype(jnp.bfloat16)


def units_at(down, first, width):
    run = pl.ds(first, width)
    return (run, slice(None)) if down else (slice(None), run)


def project_kernel(fresh, down, summed, waits, span, start, offset, skip, tile, half, *refs):
    refs = list(refs)
    rows = refs.pop(0)
    source = refs.pop(0)
    mask = refs.pop(0) if fresh else None
    arrived = refs.pop(0) if summed else None
    refs = refs[waits:]
    out = refs.pop(0)
    kept, sems = (refs[0], refs[-1]) if fresh else (source, None)
    steps = out.shape[1] // tile
    begin = half[0] * span + start

    def copy(step):
        here = pl.multiple_of(begin + step * tile, BLOCK)
        there = kept.at[units_at(down, pl.multiple_of(step * tile, BLOCK), tile)]
        return pltpu.make_async_copy(source.at[units_at(down, here, tile)], there, sems.at[step])

    for step in range(steps if fresh else 0):
        copy(step).start()
    inputs = rows[pl.ds(rows.shape[0] - out.shape[0], out.shape[0]), :]

    def chunk(step, carry):
        first = skip + step * tile
        if steps > 1:
            first = pl.multiple_of(first, BLOCK)
        if fresh:
            run = ((begin + step * tile) // BLOCK, tile // BLOCK)
            bits = spread_mask(mask, run, (0, mask.shape[1])) if down else spread_mask(mask, (0, mask.shape[0]), run)
            copy(step).wait()
            for i in range(bits.shape[0]):
                if down:
                    at = (pl.ds(first + i * BLOCK, BLOCK), slice(None))
                else:
                    at = (pl.ds(i * BLOCK, BLOCK), pl.ds(first, tile))
                kept[at] = kept[at] * bits[i : i + 1, :]
        total = lax.dot_general(
            inputs,
            kept[units_at(down, first, tile)],
            (((1,), (1 if down else 0,)), ((), ())),
            preferred_element_type=jnp.float32,
        )
        here = step * tile if steps == 1 else pl.multiple_of(step * tile, BLOCK)
        if summed:
            total = total + arrived[:, pl.ds(pl.multiple_of(offset + here, BLOCK), tile)].astype(jnp.float32)
        out[:, pl.ds(here, tile)] = total.astype(out.dtype)
        return carry

    if steps == 1:
        chunk(0, 0)
    else:
        lax.fori_loop(0, steps, chunk, 0)


def project(inputs, count, weight, mask, down, half, span, start, skip, width, arrived, before):
    fresh = mask is not None
    tile = tile_of(width, 768)
    if fresh:
        given = [inputs, pltpu.with_memory_space_constraint(weight, pltpu.HBM), mask]
        specs = [VMEM, ANY, VMEM]
    else:
        given = [inputs, pltpu.with_memory_space_constraint(weight, pltpu.VMEM)]
        specs = [VMEM, VMEM]
    if arrived:
        given.append(arrived[0])
        specs.append(VMEM)
    shapes = [jax.ShapeDtypeStruct((count, width), jnp.bfloat16)]
    if fresh:
        model = weight.shape[1 if down else 0]
        shapes.append(pltpu.VMEM((width, model) if down else (model, width), weight.dtype))
    offset = arrived[1] if arrived else 0
    return pl.pallas_call(
        functools.partial(
            project_kernel, fresh, down, bool(arrived), len(before), span, start, offset, skip, tile
        ),
        out_shape=(*shapes, TICKET),
        in_specs=[pl.BlockSpec(memory_space=pltpu.SMEM)] + specs + [ANY] * len(before),
        out_specs=(VMEM,) * len(shapes) + (ANY,),
        scratch_shapes=[pltpu.SemaphoreType.DMA((width // tile,))] if fresh else [],
        compiler_params=pltpu.CompilerParams(vmem_limit_bytes=12 * 1024 * 1024),
        cost_estimate=BRIEF,
        name="project_down" if down else "project_up",
    )(half, *given, *before)


def activate_kernel(groups, *refs):
    pairs, (act, slope, _) = refs[: 2 * groups], refs[-3:]
    top = 0
    for i in range(groups):
        mine, other = pairs[2 * i], pairs[2 * i + 1]
        at = pl.ds(top, mine.shape[0])
        value = mine[...].astype(jnp.float32) + other[...].astype(jnp.float32)
        gate = 0.5 * (1.0 + lax.erf(value * SQRT_HALF))
        act[at, :] = (value * gate).astype(act.dtype)
        slope[at, :] = gate + value * jnp.exp(-0.5 * value * value) * INV_ROOT_TWO_PI
        top += mine.shape[0]


def backward_kernel(groups, *refs):
    pairs, slope, out = refs[: 2 * groups], refs[2 * groups], refs[-2]
    top = 0
    for i in range(groups):
        mine, other = pairs[2 * i], pairs[2 * i + 1]
        at = pl.ds(top, mine.shape[0])
        value = mine[...].astype(jnp.float32) + other[...].astype(jnp.float32)
        out[at, :] = (value * slope[at, :]).astype(out.dtype)
        top += mine.shape[0]


def column_spec(array, tile, offset):
    return pl.BlockSpec((array.shape[0], tile), lambda step: (0, offset // tile + step))


def pointwise(pairs, width, slope, before):
    offsets = [at for _, _, at in pairs] + ([slope[1]] if slope else [])
    tile = tile_of(width, 384, *offsets)
    count = sum(mine.shape[0] for mine, _, _ in pairs)
    given, specs = [], []
    for mine, other, at in pairs:
        given += [mine, other]
        specs += [column_spec(mine, tile, at)] * 2
    whole = pl.BlockSpec((count, tile), lambda step: (0, step))
    result = jax.ShapeDtypeStruct((count, width), jnp.bfloat16)
    if slope:
        given.append(slope[0])
        specs.append(column_spec(slope[0], tile, slope[1]))
        kernel, shapes, outs = backward_kernel, (result, TICKET), (whole, ANY)
    else:
        kernel = activate_kernel
        shapes = (result, jax.ShapeDtypeStruct((count, width), jnp.float32), TICKET)
        outs = (whole, whole, ANY)
    return pl.pallas_call(
        functools.partial(kernel, len(pairs)),
        out_shape=shapes,
        grid=(width // tile,),
        in_specs=specs + [ANY] * len(before),
        out_specs=outs,
        compiler_params=pltpu.CompilerParams(vmem_limit_bytes=10 * 1024 * 1024),
        cost_estimate=BRIEF,
        name="hidden_gradient" if slope else "activation",
    )(*given, *before)


def stack_kernel(pieces, transposed, *refs):
    outs = refs[-3:] if transposed else refs[-2:]
    top = 0
    for piece in refs[:pieces]:
        at = pl.ds(top, piece.shape[0])
        outs[0][at, :] = piece[...]
        if transposed:
            outs[1][:, at] = piece[...].T
        top += piece.shape[0]


def stack(pieces, transposed, before):
    count, model = sum(piece.shape[0] for piece in pieces), pieces[0].shape[1]
    shapes = [(count, model), (model, count)] if transposed else [(count, model)]
    return pl.pallas_call(
        functools.partial(stack_kernel, len(pieces), transposed),
        out_shape=(*(jax.ShapeDtypeStruct(shape, pieces[0].dtype) for shape in shapes), TICKET),
        in_specs=[VMEM] * len(pieces) + [ANY] * len(before),
        out_specs=(VMEM,) * len(shapes) + (ANY,),
        compiler_params=pltpu.CompilerParams(vmem_limit_bytes=12 * 1024 * 1024),
        cost_estimate=BRIEF,
        name="stack",
    )(*pieces, *before)


def begin_kernel(*refs):
    pass


def begin(scalars, arrays):
    return pl.pallas_call(
        begin_kernel,
        out_shape=TICKET,
        in_specs=[pl.BlockSpec(memory_space=pltpu.SMEM)] * len(scalars) + [ANY] * len(arrays),
        out_specs=ANY,
        compiler_params=pltpu.CompilerParams(vmem_limit_bytes=1024 * 1024),
        cost_estimate=BRIEF,
        name="begin",
    )(*scalars, *arrays)


def copy_kernel(source, *refs):
    refs[-2][...] = source[...]


def late(source, before):
    return pl.pallas_call(
        copy_kernel,
        out_shape=(jax.ShapeDtypeStruct(source.shape, source.dtype), TICKET),
        in_specs=[VMEM] + [ANY] * len(before),
        out_specs=(VMEM, ANY),
        compiler_params=pltpu.CompilerParams(vmem_limit_bytes=4 * 1024 * 1024),
        cost_estimate=BRIEF,
        name="late",
    )(source, *before)


def gradient_kernel(down, parts, span, start, half, mask, *refs):
    fixed, *moving = refs[: 1 + parts]
    out = refs[-2]
    part, step = pl.program_id(0), pl.program_id(1)
    tile = out.shape[0 if down else 1]
    first = ((half[0] ^ part) * span + start + step * tile) // BLOCK

    whole = out.shape[0]
    part_rows = tile_of(whole, 768 if down else 1536)

    def unit_columns(*at):
        if parts == 1:
            return moving[0][at]
        return jnp.where(part == 0, moving[0][at], moving[1][at])

    def rows(i, carry):
        at = pl.ds(pl.multiple_of(i * part_rows, BLOCK), part_rows)
        blocks = part_rows // BLOCK
        if down:
            left, right, dims = unit_columns(slice(None), at), fixed[...], (((0,), (0,)), ((), ()))
            bits = spread_mask(mask, (first + i * blocks, blocks), (0, mask.shape[1]))
        else:
            left, right, dims = fixed[at, :], unit_columns(slice(None), slice(None)), (((1,), (0,)), ((), ()))
            bits = spread_mask(mask, (i * blocks, blocks), (first, tile // BLOCK))
        value = lax.dot_general(left, right, dims, preferred_element_type=jnp.float32)
        for j in range(blocks):
            block = value[j * BLOCK : (j + 1) * BLOCK, :].astype(out.dtype)
            here = pl.multiple_of(i * part_rows + j * BLOCK, BLOCK)
            out[pl.ds(here, BLOCK), :] = block * bits[j : j + 1, :]
        return carry

    lax.fori_loop(0, whole // part_rows, rows, 0)


def gradient(fixed, moving, mask, down, half, start, units, out, before):
    span = units // CORES
    count, width = moving[0].shape
    parts = len(moving)
    model = fixed.shape[1 if down else 0]
    tile = tile_of(width, 768, start)
    steps = width // tile
    shape = (units, model) if down else (model, units)

    def unit_block(part, step, half):
        return (half[0] ^ part) * (span // tile) + start // tile + step

    specs = [pl.BlockSpec(array.shape, lambda *at: (0, 0)) for array in (mask, fixed)]
    for i in range(parts):
        rest = 0 if i else steps - 1

        def place(part, step, half, i=i, rest=rest):
            return (0, jnp.where(part == i, step, rest))

        specs.append(pl.BlockSpec((count, tile), place))
    if down:
        out_spec = pl.BlockSpec((tile, model), lambda *at: (unit_block(*at), 0))
    else:
        out_spec = pl.BlockSpec((model, tile), lambda *at: (0, unit_block(*at)))
    given = [mask, fixed, *moving]
    aliases = {}
    if out is not None:
        given.append(out)
        specs.append(ANY)
        aliases = {1 + 2 + parts: 0}
    return pl.pallas_call(
        functools.partial(gradient_kernel, down, parts, span, start),
        out_shape=(jax.ShapeDtypeStruct(shape, jnp.bfloat16), TICKET),
        grid_spec=pltpu.PrefetchScalarGridSpec(
            num_scalar_prefetch=1,
            grid=(parts, steps),
            in_specs=specs + [ANY] * len(before),
            out_specs=(out_spec, ANY),
        ),
        input_output_aliases=aliases,
        compiler_params=pltpu.CompilerParams(vmem_limit_bytes=VMEM_BYTES),
        cost_estimate=BRIEF,
        name="down_gradient" if down else "up_gradient",
    )(half, *given, *before)


def on_device(n_row, n_col, tokens, cotangent, up_weight, down_weight, up_mask, down_mask):
    units = up_weight.shape[1]
    span = units // CORES
    chips = n_col // CORES
    core = lax.axis_index("col") % CORES
    mine = core.astype(jnp.int32).reshape(1)
    other = 1 - mine

    def turn(value, by):
        return lax.ppermute(value, "row", [(i, (i + by) % n_row) for i in range(n_row)])

    def core_swap(value):
        return lax.ppermute(value, "col", [(i, i ^ 1) for i in range(n_col)])

    def chip_swap(value):
        hop = 1
        while 2 * hop < chips:
            value = value + lax.ppermute(value, "col", [(i, i ^ (CORES * hop)) for i in range(n_col)])
            hop *= 2
        if chips == 1:
            return value, jnp.zeros_like(value)
        return value, lax.ppermute(value, "col", [(i, i ^ (CORES * hop)) for i in range(n_col)])

    lanes = span // BLOCK

    def cuts(eighths):
        if any(lanes * size % 8 for size in eighths):
            eighths = [*eighths[:-2], eighths[-2] + eighths[-1]]
        ends = [span * sum(eighths[: i + 1]) // 8 for i in range(len(eighths))]
        return [(end - span * size // 8, span * size // 8) for size, end in zip(eighths, ends)]

    chunks = {name: cuts(eighths) for name, eighths in CUTS.items()}
    own = tokens.shape[0]
    inputs = {"h0": (tokens, own), "g0": (cotangent, own)}
    weights = {"h": (up_weight, up_mask), "g": (down_weight, down_mask)}
    near = sorted({1, n_row - 1} - {0}) if n_row > 1 else []
    turns = [near[:1], near[1:], [by for by in range(1, n_row) if by not in near]]
    shards = {"x": tokens, "c": cotangent}
    moves, sent, sums, stored, slopes, acts, hidden, grads = {}, {}, {}, [], [], {}, {}, {}
    before = [begin([mine, other], [up_mask, down_mask])]

    def step(call, *args):
        nonlocal before
        *results, ticket = call(*args, before)
        before = [ticket]
        return results[0] if len(results) == 1 else results

    def covering(found, start, width):
        return next(one for one in found if one[0] <= start and start + width <= one[0] + one[1])

    def product(key, side, start, width, arrived):
        rows, count = inputs[key]
        half, down = (mine, other)[side], key[0] == "g"
        if key[1] == "0":
            weight, mask = weights[key[0]]
            result, kept = step(project, rows, count, weight, mask, down, half, span, start, 0, width, arrived)
            stored.append((start, width, key[0], side, kept))
            return result
        at, _, _, _, kept = covering([one for one in stored if one[2:4] == (key[0], side)], start, width)
        return step(project, rows, count, kept, None, down, half, span, start, start - at, width, arrived)

    def pairs(kind, start, width):
        found = []
        for key in (kind + "0", kind + "1") if n_row > 1 else (kind + "0",):
            at, _, value, arrived = covering(sums[key], start, width)
            found.append((value, arrived, start - at))
        return found

    def run(action, name, at):
        if action == "turn":
            if turns[at]:
                source = step(late, shards[name])
                moves[name, at] = [turn(source, by) for by in turns[at]]
            else:
                moves[name, at] = []
            return
        if action == "stack":
            pieces = [shards[name], *(piece for i in range(3) for piece in moves[name, i])]
            if name == "x":
                inputs["h1"], stacks["x"] = step(stack, pieces, True)
                inputs["h1"] = (inputs["h1"], own * (n_row - 1))
            else:
                stacks["c"] = step(stack, pieces, False)
                inputs["g1"] = (stacks["c"], own * (n_row - 1))
            return
        if name not in chunks or at >= len(chunks[name]):
            return
        if n_row == 1 and name[1:] == "1":
            return
        start, width = chunks[name][at]
        if action == "send":
            value = product(name[:2], 1, start, width, None)
            sent.setdefault(name[:2], []).append((start, width, core_swap(value)))
        elif action == "add":
            first, _, arrived = covering(sent[name], start, width)
            value, arrived = chip_swap(product(name, 0, start, width, (arrived, start - first)))
            sums.setdefault(name, []).append((start, width, value, arrived))
            moves[name, at] = [arrived]
        elif action == "act":
            act, slope = step(pointwise, pairs("h", start, width), width, None)
            slopes.append((start, width, slope))
            acts[at] = act, core_swap(act)
        elif action == "down":
            grads["down"] = step(
                gradient, stacks["c"], acts[at], down_mask, True, mine, start, units, grads.get("down")
            )
        elif action == "hidden":
            first, _, slope = covering(slopes, start, width)
            value = step(pointwise, pairs("g", start, width), width, (slope, start - first))
            hidden[at] = value, core_swap(value)
        else:
            moving = {"up": hidden[at], "upmine": hidden[at][:1], "upother": hidden[at][1:]}[action]
            half = other if action == "upother" else mine
            grads["up"] = step(gradient, stacks["x"], moving, up_mask, False, half, start, units, grads.get("up"))

    stacks = {}
    for action, name, at, *ended in ORDER:
        for transfer in ended:
            before += moves.get(transfer, [])
        run(action, name, at)
    return grads["up"], grads["down"]


def solution(mesh):
    placed = (
        P(("groups", "row"), "col"),
        P(("groups", "row"), "col"),
        P("col", "row"),
        P("row", "col"),
        P("col", "row"),
        P("row", "col"),
    )
    return jax.shard_map(
        functools.partial(on_device, mesh.shape["row"], mesh.shape["col"]),
        mesh=mesh,
        in_specs=placed,
        out_specs=(P(("groups", "col"), "row"), P(("groups", "row"), "col")),
        check_vma=False,
    )
```

profile of v0, /device:TPU:0, one launch (start us, length us, event | category | flops | bytes accessed | tf_op | source)
XLA Modules:
  0.0 171.0 jit_solution(11658913929063982716)
XLA Ops:
  0.6 0.8 copy.17.refs_3_.refs_2_.mask
  1.4 0.7 copy-done.14
  2.1 1.0 copy-done
  3.1 2.3 %project_up.12 = (bf16[128,768]{1,0:T(8,128)(2,1)S(1)}, bf16[1536,768]{1,0:T(8,128)(2,1)S(1)}, f32[8,128]{1,0:T(8,128)S(1)}) custom-call(s32[1]{0:T(128)S(6)} %sub.3.refs_1_.half, bf16[128,1536]{1,0:T(8,128)(2,1)S(1)} %copy-done, bf16[1536,6144]{1,0:T(8,128)(2,1)} %refs_1_.16, s32[12,48]{1,0:T(8,128)S(1)} %copy-done.15, f32[8,128]{1,0:T(8,128)S(1)} %begin.1.refs_3_), custom_call_target="tpu_custom_call" | custom-call | flops 10000000000 | tf_op jit(solution)/shard_map/project_up/pallas_call | solution.py:189
  6.0 2.2 %project_up.13 = (bf16[128,768]{1,0:T(8,128)(2,1)S(1)}, bf16[1536,768]{1,0:T(8,128)(2,1)S(1)}, f32[8,128]{1,0:T(8,128)S(1)}) custom-call(s32[1]{0:T(128)S(6)} %sub.3.refs_1_.half, bf16[128,1536]{1,0:T(8,128)(2,1)S(1)} %copy-done, bf16[1536,6144]{1,0:T(8,128)(2,1)} %refs_1_.16, s32[12,48]{1,0:T(8,128)S(1)} %copy-done.15, f32[8,128]{1,0:T(8,128)S(1)} %get-tuple-element.123.refs_3_), custom_call_target="tpu_custom_call" | custom-call | flops 10000000000 | tf_op jit(solution)/shard_map/project_up/pallas_call | solution.py:189
  8.2 1.4 copy-done.17
  9.7 5.0 %collective-permute-start.1 = (bf16[128,1536]{1,0:T(8,128)(2,1)S(1)}, bf16[128,1536]{1,0:T(8,128)(2,1)S(1)}, u32[]{:S(2)}, u32[]{:S(2)}) collective-permute-start(bf16[128,1536]{1,0:T(8,128)(2,1)S(1)} %get-tuple-element.122), channel_id=1, source_target_pairs={{0,12},{4,0},{8,4},{12,8},{1,13},{5,1},{9,5},{13,9},{2,14},{6,2},{... | collective-permute-start | bytes 1179656 | tf_op jit(solution)/shard_map/ppermute | solution.py:407
  14.7 2.3 %project_up.14 = (bf16[128,768]{1,0:T(8,128)(2,1)S(1)}, bf16[1536,768]{1,0:T(8,128)(2,1)S(1)}, f32[8,128]{1,0:T(8,128)S(1)}) custom-call(s32[1]{0:T(128)} %bitcast.refs_0_.half, bf16[128,1536]{1,0:T(8,128)(2,1)S(1)} %copy-done, bf16[1536,6144]{1,0:T(8,128)(2,1)} %refs_1_.16, s32[12,48]{1,0:T(8,128)S(1)} %copy-done.15, ...), custom_call_target="tpu_custom_call" | custom-call | flops 10000000000 | tf_op jit(solution)/shard_map/project_up/pallas_call | solution.py:189
  17.0 3.0 %project_up.15 = (bf16[128,1536]{1,0:T(8,128)(2,1)S(1)}, bf16[1536,1536]{1,0:T(8,128)(2,1)S(1)}, f32[8,128]{1,0:T(8,128)S(1)}) custom-call(s32[1]{0:T(128)S(6)} %sub.3.refs_1_.half, bf16[128,1536]{1,0:T(8,128)(2,1)S(1)} %copy-done, bf16[1536,6144]{1,0:T(8,128)(2,1)} %refs_1_.16, s32[12,48]{1,0:T(8,128)S(1)} %copy-done.15, ...), custom_call_target="tpu_custom_call" | custom-call | flops 10000000000 | tf_op jit(solution)/shard_map/project_up/pallas_call | solution.py:189
  20.0 1.6 collective-permute-start.6
  21.6 2.3 %project_up.16 = (bf16[128,768]{1,0:T(8,128)(2,1)S(1)}, bf16[1536,768]{1,0:T(8,128)(2,1)S(1)}, f32[8,128]{1,0:T(8,128)S(1)}) custom-call(s32[1]{0:T(128)} %bitcast.refs_0_.half, bf16[128,1536]{1,0:T(8,128)(2,1)S(1)} %copy-done, bf16[1536,6144]{1,0:T(8,128)(2,1)} %refs_1_.16, s32[12,48]{1,0:T(8,128)S(1)} %copy-done.15, ...), custom_call_target="tpu_custom_call" | custom-call | flops 10000000000 | tf_op jit(solution)/shard_map/project_up/pallas_call | solution.py:189
  24.5 4.0 %project_down.13 = (bf16[128,1536]{1,0:T(8,128)(2,1)S(1)}, bf16[1536,1536]{1,0:T(8,128)(2,1)S(1)}, f32[8,128]{1,0:T(8,128)S(1)}) custom-call(s32[1]{0:T(128)S(6)} %sub.3.refs_1_.half, bf16[128,1536]{1,0:T(8,128)(2,1)S(1)} %copy-done.1, bf16[6144,1536]{1,0:T(8,128)(2,1)} %refs_1_.19, s32[48,12]{1,0:T(8,128)S(1)} %copy.17.refs_3_.refs_2_.mask, ...), custom_call_target="tpu_custom_call" | custom-call | flops 10000000000 | tf_op jit(solution)/shard_map/project_down/pallas_call | solution.py:189
  28.7 1.2 collective-permute-start.4
  29.9 3.0 %project_up.17 = (bf16[128,1536]{1,0:T(8,128)(2,1)S(1)}, bf16[1536,1536]{1,0:T(8,128)(2,1)S(1)}, f32[8,128]{1,0:T(8,128)S(1)}) custom-call(s32[1]{0:T(128)} %bitcast.refs_0_.half, bf16[128,1536]{1,0:T(8,128)(2,1)S(1)} %copy-done, bf16[1536,6144]{1,0:T(8,128)(2,1)} %refs_1_.16, s32[12,48]{1,0:T(8,128)S(1)} %copy-done.15, ...), custom_call_target="tpu_custom_call" | custom-call | flops 10000000000 | tf_op jit(solution)/shard_map/project_up/pallas_call | solution.py:189
  32.9 4.2 %project_down.14 = (bf16[128,1536]{1,0:T(8,128)(2,1)S(1)}, bf16[1536,1536]{1,0:T(8,128)(2,1)S(1)}, f32[8,128]{1,0:T(8,128)S(1)}) custom-call(s32[1]{0:T(128)S(6)} %sub.3.refs_1_.half, bf16[128,1536]{1,0:T(8,128)(2,1)S(1)} %copy-done.1, bf16[6144,1536]{1,0:T(8,128)(2,1)} %refs_1_.19, s32[48,12]{1,0:T(8,128)S(1)} %copy.17.refs_3_.refs_2_.mask, ...), custom_call_target="tpu_custom_call" | custom-call | flops 10000000000 | tf_op jit(solution)/shard_map/project_down/pallas_call | solution.py:189
  37.3 1.5 collective-permute-start.9
  38.8 4.0 %project_down.15 = (bf16[128,1536]{1,0:T(8,128)(2,1)S(1)}, bf16[1536,1536]{1,0:T(8,128)(2,1)S(1)}, f32[8,128]{1,0:T(8,128)S(1)}) custom-call(s32[1]{0:T(128)} %bitcast.refs_0_.half, bf16[128,1536]{1,0:T(8,128)(2,1)S(1)} %copy-done.1, bf16[6144,1536]{1,0:T(8,128)(2,1)} %refs_1_.19, s32[48,12]{1,0:T(8,128)S(1)} %copy.17.refs_3_.refs_2_.mask, ...), custom_call_target="tpu_custom_call" | custom-call | flops 10000000000 | tf_op jit(solution)/shard_map/project_down/pallas_call | solution.py:189
  43.5 4.0 %project_down.16 = (bf16[128,1536]{1,0:T(8,128)(2,1)S(1)}, bf16[1536,1536]{1,0:T(8,128)(2,1)S(1)}, f32[8,128]{1,0:T(8,128)S(1)}) custom-call(s32[1]{0:T(128)} %bitcast.refs_0_.half, bf16[128,1536]{1,0:T(8,128)(2,1)S(1)} %copy-done.1, bf16[6144,1536]{1,0:T(8,128)(2,1)} %refs_1_.19, s32[48,12]{1,0:T(8,128)S(1)} %copy.17.refs_3_.refs_2_.mask, ...), custom_call_target="tpu_custom_call" | custom-call | flops 10000000000 | tf_op jit(solution)/shard_map/project_down/pallas_call | solution.py:189
  47.5 2.0 %collective-permute-done.4.refs_3_ = bf16[128,1536]{1,0:T(8,128)(2,1)S(1)} collective-permute-done((bf16[128,1536]{1,0:T(8,128)(2,1)S(1)}, bf16[128,1536]{1,0:T(8,128)(2,1)S(1)}, u32[]{:S(2)}, u32[]{:S(2)}) %collective-permute-start.4) | collective-permute-done | bytes 393248 | tf_op jit(solution)/shard_map/ppermute | solution.py:407
  50.3 1.1 project_up.18
  51.5 2.3 %project_up.19 = (bf16[384,1536]{1,0:T(8,128)(2,1)S(1)}, f32[8,128]{1,0:T(8,128)S(1)}) custom-call(s32[1]{0:T(128)S(6)} %sub.3.refs_1_.half, bf16[512,1536]{1,0:T(8,128)(2,1)S(1)} %get-tuple-element.146.refs_0_, bf16[1536,1536]{1,0:T(8,128)(2,1)S(1)} %get-tuple-element.152.refs_1_, f32[8,128]{1,0:T(8,128)S(1)} %get-tuple-element.153.refs_2_), custom_call_target="tpu_custom_call" | custom-call | flops 10000000000 | tf_op jit(solution)/shard_map/project_up/pallas_call | solution.py:189
  54.3 1.5 collective-permute-start.10
  55.9 3.1 %collective-permute-start.11 = (bf16[128,1536]{1,0:T(8,128)(2,1)S(1)}, bf16[128,1536]{1,0:T(8,128)(2,1)S(1)}, u32[]{:S(2)}, u32[]{:S(2)}) collective-permute-start(bf16[128,1536]{1,0:T(8,128)(2,1)S(1)} %get-tuple-element.145), channel_id=1, source_target_pairs={{0,4},{4,8},{8,12},{12,0},{1,5},{5,9},{9,13},{13,1},{2,6},{6,10},{... | collective-permute-start | bytes 1179656 | tf_op jit(solution)/shard_map/ppermute | solution.py:407
  59.0 1.1 project_up.20
  60.2 1.1 project_up.21
  62.2 1.8 %collective-permute-start.15 = (bf16[128,1536]{1,0:T(8,128)(2,1)S(1)}, bf16[128,1536]{1,0:T(8,128)(2,1)S(1)}, u32[]{:S(2)}, u32[]{:S(2)}) collective-permute-start(bf16[128,1536]{1,0:T(8,128)(2,1)S(1)} %get-tuple-element.160), channel_id=1, source_target_pairs={{0,12},{4,0},{8,4},{12,8},{1,13},{5,1},{9,5},{13,9},{2,14},{6,2},{... | collective-permute-start | bytes 1179656 | tf_op jit(solution)/shard_map/ppermute | solution.py:407
  63.9 1.1 project_up.22
  65.0 1.3 collective-permute-done.10.refs_4_.refs_1_
  66.3 1.5 collective-permute-start.16
  67.8 1.5 collective-permute-start.18
  69.3 2.3 %project_up.23 = (bf16[384,1536]{1,0:T(8,128)(2,1)S(1)}, f32[8,128]{1,0:T(8,128)S(1)}) custom-call(s32[1]{0:T(128)} %bitcast.refs_0_.half, bf16[512,1536]{1,0:T(8,128)(2,1)S(1)} %copy-done.20, bf16[1536,1536]{1,0:T(8,128)(2,1)S(1)} %get-tuple-element.167.refs_1_, bf16[384,1536]{1,0:T(8,128)(2,1)S(1)} %collective-permute-done.20.refs_2_, ...), custom_call_target="tpu_custom_call" | custom-call | flops 10000000000 | tf_op jit(solution)/shard_map/project_up/pallas_call | solution.py:189
  71.6 7.3 %collective-permute-done.19.refs_3_ = bf16[384,768]{1,0:T(8,128)(2,1)S(1)} collective-permute-done((bf16[384,768]{1,0:T(8,128)(2,1)S(1)}, bf16[384,768]{1,0:T(8,128)(2,1)S(1)}, u32[]{:S(2)}, u32[]{:S(2)}) %collective-permute-start.19) | collective-permute-done | bytes 589856 | tf_op jit(solution)/shard_map/ppermute | solution.py:419
  79.0 1.2 activation.3
  80.3 1.6 collective-permute-start.27
  81.8 9.8 %collective-permute-done.18.refs_3_ = bf16[384,768]{1,0:T(8,128)(2,1)S(1)} collective-permute-done((bf16[384,768]{1,0:T(8,128)(2,1)S(1)}, bf16[384,768]{1,0:T(8,128)(2,1)S(1)}, u32[]{:S(2)}, u32[]{:S(2)}) %collective-permute-start.18) | collective-permute-done | bytes 589856 | tf_op jit(solution)/shard_map/ppermute | solution.py:419
  91.6 1.2 activation.4
  92.8 1.0 collective-permute-done.16.refs_3_
  93.9 1.1 project_down.17
  95.6 4.5 %down_gradient.3 = (bf16[6144,1536]{1,0:T(8,128)(2,1)}, f32[8,128]{1,0:T(8,128)S(1)}) custom-call(s32[1]{0:T(128)} %bitcast.refs_0_.half, s32[48,12]{1,0:T(8,128)S(1)} %copy.17.refs_3_.refs_2_.mask, bf16[512,1536]{1,0:T(8,128)(2,1)S(1)} %get-tuple-element.173.refs_0_, bf16[512,768]{1,0:T(8,128)(2,1)S(1)} %get-tuple-element.180.refs_1_, ...), custom_call_target="tpu_custom_call" | custom-call | flops 10000000000 | tf_op jit(solution)/shard_map/down_gradient/pallas_call | solution.py:382
  100.1 1.1 project_down.18
  101.2 1.1 project_down.19
  103.1 4.5 %down_gradient.4 = (bf16[6144,1536]{1,0:T(8,128)(2,1)}, f32[8,128]{1,0:T(8,128)S(1)}) custom-call(s32[1]{0:T(128)} %bitcast.refs_0_.half, s32[48,12]{1,0:T(8,128)S(1)} %copy.17.refs_3_.refs_2_.mask, bf16[512,1536]{1,0:T(8,128)(2,1)S(1)} %get-tuple-element.173.refs_0_, ...), custom_call_target="tpu_custom_call", output_to_operand_aliasing={{0}: (5, {})} | custom-call | flops 10000000000 | tf_op jit(solution)/shard_map/down_gradient/pallas_call | solution.py:382
  107.6 1.1 project_down.20
  108.7 1.1 project_down.21
  110.0 1.1 project_down.22
  111.1 5.7 %collective-permute-done.27.refs_3_ = bf16[384,1536]{1,0:T(8,128)(2,1)S(1)} collective-permute-done((bf16[384,1536]{1,0:T(8,128)(2,1)S(1)}, bf16[384,1536]{1,0:T(8,128)(2,1)S(1)}, u32[]{:S(2)}, u32[]{:S(2)}) %collective-permute-start.27) | collective-permute-done | bytes 1179680 | tf_op jit(solution)/shard_map/ppermute | solution.py:419
  116.9 2.4 %activation.5 = (bf16[512,1536]{1,0:T(8,128)(2,1)S(1)}, f32[512,1536]{1,0:T(8,128)S(1)}, f32[8,128]{1,0:T(8,128)S(1)}) custom-call(bf16[128,1536]{1,0:T(8,128)(2,1)S(1)} %copy-done.11, bf16[128,1536]{1,0:T(8,128)(2,1)S(1)} %copy-done.13, bf16[384,1536]{1,0:T(8,128)(2,1)S(1)} %get-tuple-element.193.refs_2_, ...), custom_call_target="tpu_custom_call" | custom-call | flops 10000000000 | tf_op jit(solution)/shard_map/activation/pallas_call | solution.py:249
  119.8 1.5 collective-permute-start.31
  121.4 1.1 project_down.23
  123.6 0.8 project_down.24
  124.4 1.6 collective-permute-start.29
  126.0 0.8 project_down.25
  127.4 7.9 %down_gradient.5 = (bf16[6144,1536]{1,0:T(8,128)(2,1)}, f32[8,128]{1,0:T(8,128)S(1)}) custom-call(s32[1]{0:T(128)} %bitcast.refs_0_.half, s32[48,12]{1,0:T(8,128)S(1)} %copy.17.refs_3_.refs_2_.mask, bf16[512,1536]{1,0:T(8,128)(2,1)S(1)} %get-tuple-element.173.refs_0_, ...), custom_call_target="tpu_custom_call", output_to_operand_aliasing={{0}: (5, {})} | custom-call | flops 10000000000 | tf_op jit(solution)/shard_map/down_gradient/pallas_call | solution.py:382
  135.3 0.7 hidden_gradient.5
  136.1 6.1 %collective-permute-done.31.refs_3_ = bf16[384,768]{1,0:T(8,128)(2,1)S(1)} collective-permute-done((bf16[384,768]{1,0:T(8,128)(2,1)S(1)}, bf16[384,768]{1,0:T(8,128)(2,1)S(1)}, u32[]{:S(2)}, u32[]{:S(2)}) %collective-permute-start.31) | collective-permute-done | bytes 589856 | tf_op jit(solution)/shard_map/ppermute | solution.py:419
  142.9 4.3 %up_gradient.8 = (bf16[1536,6144]{1,0:T(8,128)(2,1)}, f32[8,128]{1,0:T(8,128)S(1)}) custom-call(s32[1]{0:T(128)} %bitcast.refs_0_.half, s32[12,48]{1,0:T(8,128)S(1)} %copy-done.16, bf16[1536,512]{1,0:T(8,128)(2,1)S(1)} %get-tuple-element.142.refs_0_, bf16[512,768]{1,0:T(8,128)(2,1)S(1)} %get-tuple-element.212.refs_1_, ...), custom_call_target="tpu_custom_call" | custom-call | flops 10000000000 | tf_op jit(solution)/shard_map/up_gradient/pallas_call | solution.py:382
  147.3 4.3 %up_gradient.9 = (bf16[1536,6144]{1,0:T(8,128)(2,1)}, f32[8,128]{1,0:T(8,128)S(1)}) custom-call(s32[1]{0:T(128)} %bitcast.refs_0_.half, s32[12,48]{1,0:T(8,128)S(1)} %copy-done.16, bf16[1536,512]{1,0:T(8,128)(2,1)S(1)} %get-tuple-element.142.refs_0_, bf16[512,768]{1,0:T(8,128)(2,1)S(1)} %get-tuple-element.211.refs_1_, ...), custom_call_target="tpu_custom_call", output_to_operand_aliasing={{0}: (5, {})} | custom-call | flops 10000000000 | tf_op jit(solution)/shard_map/up_gradient/pallas_call | solution.py:382
  151.6 3.2 %collective-permute-done.30.refs_3_ = bf16[384,768]{1,0:T(8,128)(2,1)S(1)} collective-permute-done((bf16[384,768]{1,0:T(8,128)(2,1)S(1)}, bf16[384,768]{1,0:T(8,128)(2,1)S(1)}, u32[]{:S(2)}, u32[]{:S(2)}) %collective-permute-start.30) | collective-permute-done | bytes 589856 | tf_op jit(solution)/shard_map/ppermute | solution.py:419
  155.5 2.8 %up_gradient.10 = (bf16[1536,6144]{1,0:T(8,128)(2,1)}, f32[8,128]{1,0:T(8,128)S(1)}) custom-call(s32[1]{0:T(128)} %bitcast.refs_0_.half, s32[12,48]{1,0:T(8,128)S(1)} %copy-done.16, bf16[1536,512]{1,0:T(8,128)(2,1)S(1)} %get-tuple-element.142.refs_0_, bf16[512,768]{1,0:T(8,128)(2,1)S(1)} %get-tuple-element.217.refs_1_, ...), custom_call_target="tpu_custom_call", output_to_operand_aliasing={{0}: (4, {})} | custom-call | flops 10000000000 | tf_op jit(solution)/shard_map/up_gradient/pallas_call | solution.py:382
  158.4 2.8 %up_gradient.11 = (bf16[1536,6144]{1,0:T(8,128)(2,1)}, f32[8,128]{1,0:T(8,128)S(1)}) custom-call(s32[1]{0:T(128)S(6)} %sub.3.refs_1_.half, s32[12,48]{1,0:T(8,128)S(1)} %copy-done.16, bf16[1536,512]{1,0:T(8,128)(2,1)S(1)} %get-tuple-element.142.refs_0_, bf16[512,768]{1,0:T(8,128)(2,1)S(1)} %collective-permute-done.36.refs_1_, ...), custom_call_target="tpu_custom_call", output_to_operand_aliasing={{0}: (4, {})} | custom-call | flops 10000000000 | tf_op jit(solution)/shard_map/up_gradient/pallas_call | solution.py:382
  162.0 2.0 %up_gradient.12 = (bf16[1536,6144]{1,0:T(8,128)(2,1)}, f32[8,128]{1,0:T(8,128)S(1)}) custom-call(s32[1]{0:T(128)} %bitcast.refs_0_.half, s32[12,48]{1,0:T(8,128)S(1)} %copy-done.16, bf16[1536,512]{1,0:T(8,128)(2,1)S(1)} %get-tuple-element.142.refs_0_, bf16[512,384]{1,0:T(8,128)(2,1)S(1)} %get-tuple-element.223.refs_1_, ...), custom_call_target="tpu_custom_call", output_to_operand_aliasing={{0}: (4, {})} | custom-call | flops 10000000000 | tf_op jit(solution)/shard_map/up_gradient/pallas_call | solution.py:382
  164.0 2.0 %up_gradient.13 = (bf16[1536,6144]{1,0:T(8,128)(2,1)}, f32[8,128]{1,0:T(8,128)S(1)}) custom-call(s32[1]{0:T(128)S(6)} %sub.3.refs_1_.half, s32[12,48]{1,0:T(8,128)S(1)} %copy-done.16, bf16[1536,512]{1,0:T(8,128)(2,1)S(1)} %get-tuple-element.142.refs_0_, bf16[512,384]{1,0:T(8,128)(2,1)S(1)} %collective-permute-done.37.refs_1_, ...), custom_call_target="tpu_custom_call", output_to_operand_aliasing={{0}: (4, {})} | custom-call | flops 10000000000 | tf_op jit(solution)/shard_map/up_gradient/pallas_call | solution.py:382
  166.9 2.0 %up_gradient.14 = (bf16[1536,6144]{1,0:T(8,128)(2,1)}, f32[8,128]{1,0:T(8,128)S(1)}) custom-call(s32[1]{0:T(128)} %bitcast.refs_0_.half, s32[12,48]{1,0:T(8,128)S(1)} %copy-done.16, bf16[1536,512]{1,0:T(8,128)(2,1)S(1)} %get-tuple-element.142.refs_0_, bf16[512,384]{1,0:T(8,128)(2,1)S(1)} %get-tuple-element.229.refs_1_, ...), custom_call_target="tpu_custom_call", output_to_operand_aliasing={{0}: (4, {})} | custom-call | flops 10000000000 | tf_op jit(solution)/shard_map/up_gradient/pallas_call | solution.py:382
  169.0 2.0 %up_gradient.15 = (bf16[1536,6144]{1,0:T(8,128)(2,1)}, f32[8,128]{1,0:T(8,128)}) custom-call(s32[1]{0:T(128)S(6)} %sub.3.refs_1_.half, s32[12,48]{1,0:T(8,128)S(1)} %copy-done.16, bf16[1536,512]{1,0:T(8,128)(2,1)S(1)} %get-tuple-element.142.refs_0_, bf16[512,384]{1,0:T(8,128)(2,1)S(1)} %collective-permute-done.38.refs_1_, ...), custom_call_target="tpu_custom_call", output_to_operand_aliasing={{0}: (4, {})} | custom-call | flops 10000000000 | tf_op jit(solution)/shard_map/up_gradient/pallas_call | solution.py:382
  (110 shorter events, 11.8 us)
Async XLA Ops:
  1.4 0.7 copy-start.14
  2.1 1.0 copy-start
  2.1 1.0 copy-start.15
  5.4 9.3 %collective-permute-start.3 = (bf16[128,768]{1,0:T(8,128)(2,1)S(1)}, bf16[128,768]{1,0:T(8,128)(2,1)S(1)}, u32[]{:S(2)}, u32[]{:S(2)}) collective-permute-start(bf16[128,768]{1,0:T(8,128)(2,1)S(1)} %get-tuple-element.125), channel_id=1, source_target_pairs={{0,1},{1,0},{2,3},{3,2},{4,5},{5,4},{6,7},{7,6},{8,9},{9,8},{10,11... | collective-permute-start | bytes 589832 | tf_op jit(solution)/shard_map/ppermute | solution.py:410
  8.2 1.4 copy-start.17
  9.6 12.0 %collective-permute-start.2 = (bf16[128,768]{1,0:T(8,128)(2,1)S(1)}, bf16[128,768]{1,0:T(8,128)(2,1)S(1)}, u32[]{:S(2)}, u32[]{:S(2)}) collective-permute-start(bf16[128,768]{1,0:T(8,128)(2,1)S(1)} %get-tuple-element.124), channel_id=1, source_target_pairs={{0,1},{1,0},{2,3},{3,2},{4,5},{5,4},{6,7},{7,6},{8,9},{9,8},{10,11... | collective-permute-start | bytes 589832 | tf_op jit(solution)/shard_map/ppermute | solution.py:410
  9.7 14.9 %collective-permute-start.1 = (bf16[128,1536]{1,0:T(8,128)(2,1)S(1)}, bf16[128,1536]{1,0:T(8,128)(2,1)S(1)}, u32[]{:S(2)}, u32[]{:S(2)}) collective-permute-start(bf16[128,1536]{1,0:T(8,128)(2,1)S(1)} %get-tuple-element.122), channel_id=1, source_target_pairs={{0,12},{4,0},{8,4},{12,8},{1,13},{5,1},{9,5},{13,9},{2,14},{6,2},{... | collective-permute-start | bytes 1179656 | tf_op jit(solution)/shard_map/ppermute | solution.py:407
  14.7 28.2 %collective-permute-start = (bf16[128,1536]{1,0:T(8,128)(2,1)S(1)}, bf16[128,1536]{1,0:T(8,128)(2,1)S(1)}, u32[]{:S(2)}, u32[]{:S(2)}) collective-permute-start(bf16[128,1536]{1,0:T(8,128)(2,1)S(1)} %get-tuple-element.120), channel_id=1, source_target_pairs={{0,4},{4,8},{8,12},{12,0},{1,5},{5,9},{9,13},{13,1},{2,6},{6,10},{... | collective-permute-start | bytes 1179656 | tf_op jit(solution)/shard_map/ppermute | solution.py:407
  19.9 8.7 %collective-permute-start.5 = (bf16[128,1536]{1,0:T(8,128)(2,1)S(1)}, bf16[128,1536]{1,0:T(8,128)(2,1)S(1)}, u32[]{:S(2)}, u32[]{:S(2)}) collective-permute-start(bf16[128,1536]{1,0:T(8,128)(2,1)S(1)} %get-tuple-element.132), channel_id=1, source_target_pairs={{0,1},{1,0},{2,3},{3,2},{4,5},{5,4},{6,7},{7,6},{8,9},{9,8},{10,11... | collective-permute-start | bytes 1179656 | tf_op jit(solution)/shard_map/ppermute | solution.py:410
  20.0 12.9 %collective-permute-start.6 = (bf16[128,768]{1,0:T(8,128)(2,1)S(1)}, bf16[128,768]{1,0:T(8,128)(2,1)S(1)}, u32[]{:S(2)}, u32[]{:S(2)}) collective-permute-start(bf16[128,768]{1,0:T(8,128)(2,1)S(1)} %get-tuple-element.135.refs_0_), channel_id=1, source_target_pairs={{0,2},{1,3},{2,0},{3,1},{4,6},{5,7},{6,4},{7,5},{8,10},{9,11},{10,... | collective-permute-start | bytes 589832 | tf_op jit(solution)/shard_map/ppermute | solution.py:419
  21.6 2.9 %copy-start.1 = (bf16[128,1536]{1,0:T(8,128)(2,1)S(1)}, bf16[128,1536]{1,0:T(8,128)(2,1)}, u32[]{:S(2)}) copy-start(bf16[128,1536]{1,0:T(8,128)(2,1)} %refs_0_.23) | copy-start | bytes 1179652
  23.9 31.9 %collective-permute-start.14 = (bf16[128,768]{1,0:T(8,128)(2,1)S(1)}, bf16[128,768]{1,0:T(8,128)(2,1)S(1)}, u32[]{:S(2)}, u32[]{:S(2)}) collective-permute-start(bf16[128,768]{1,0:T(8,128)(2,1)S(1)} %get-tuple-element.156.refs_0_), channel_id=1, source_target_pairs={{0,2},{1,3},{2,0},{3,1},{4,6},{5,7},{6,4},{7,5},{8,10},{9,11},{10,... | collective-permute-start | bytes 589832 | tf_op jit(solution)/shard_map/ppermute | solution.py:419
  28.6 8.7 %collective-permute-start.8 = (bf16[128,1536]{1,0:T(8,128)(2,1)S(1)}, bf16[128,1536]{1,0:T(8,128)(2,1)S(1)}, u32[]{:S(2)}, u32[]{:S(2)}) collective-permute-start(bf16[128,1536]{1,0:T(8,128)(2,1)S(1)} %get-tuple-element.137), channel_id=1, source_target_pairs={{0,1},{1,0},{2,3},{3,2},{4,5},{5,4},{6,7},{7,6},{8,9},{9,8},{10,11... | collective-permute-start | bytes 1179656 | tf_op jit(solution)/shard_map/ppermute | solution.py:410
  28.7 20.8 %collective-permute-start.4 = (bf16[128,1536]{1,0:T(8,128)(2,1)S(1)}, bf16[128,1536]{1,0:T(8,128)(2,1)S(1)}, u32[]{:S(2)}, u32[]{:S(2)}) collective-permute-start(bf16[128,1536]{1,0:T(8,128)(2,1)S(1)} %get-tuple-element.131), channel_id=1, source_target_pairs={{0,8},{4,12},{8,0},{12,4},{1,9},{5,13},{9,1},{13,5},{2,10},{6,14},... | collective-permute-start | bytes 1179656 | tf_op jit(solution)/shard_map/ppermute | solution.py:407
  32.9 4.4 %copy-start.10 = (bf16[128,1536]{1,0:T(8,128)(2,1)}, bf16[128,1536]{1,0:T(8,128)(2,1)S(1)}, u32[]{:S(2)}) copy-start(bf16[128,1536]{1,0:T(8,128)(2,1)S(1)} %get-tuple-element.141.refs_0_) | copy-start | bytes 1179652
  37.1 6.4 %collective-permute-start.7 = (bf16[128,1536]{1,0:T(8,128)(2,1)S(1)}, bf16[128,1536]{1,0:T(8,128)(2,1)S(1)}, u32[]{:S(2)}, u32[]{:S(2)}) collective-permute-start(bf16[128,1536]{1,0:T(8,128)(2,1)S(1)} %get-tuple-element.136), channel_id=1, source_target_pairs={{0,1},{1,0},{2,3},{3,2},{4,5},{5,4},{6,7},{7,6},{8,9},{9,8},{10,11... | collective-permute-start | bytes 1179656 | tf_op jit(solution)/shard_map/ppermute | solution.py:410
  37.3 12.2 %collective-permute-start.9 = (bf16[128,1536]{1,0:T(8,128)(2,1)S(1)}, bf16[128,1536]{1,0:T(8,128)(2,1)S(1)}, u32[]{:S(2)}, u32[]{:S(2)}) collective-permute-start(bf16[128,1536]{1,0:T(8,128)(2,1)S(1)} %get-tuple-element.141.refs_0_), channel_id=1, source_target_pairs={{0,2},{1,3},{2,0},{3,1},{4,6},{5,7},{6,4},{7,5},{8,10},{9,11},{10,... | collective-permute-start | bytes 1179656 | tf_op jit(solution)/shard_map/ppermute | solution.py:419
  42.9 4.7 %copy-start.6 = (bf16[128,1536]{1,0:T(8,128)(2,1)}, bf16[128,1536]{1,0:T(8,128)(2,1)S(1)}, u32[]{:S(2)}) copy-start(bf16[128,1536]{1,0:T(8,128)(2,1)S(1)} %get-tuple-element.155.refs_0_) | copy-start | bytes 1179652
  42.9 16.1 %collective-permute-start.13 = (bf16[128,1536]{1,0:T(8,128)(2,1)S(1)}, bf16[128,1536]{1,0:T(8,128)(2,1)S(1)}, u32[]{:S(2)}, u32[]{:S(2)}) collective-permute-start(bf16[128,1536]{1,0:T(8,128)(2,1)S(1)} %get-tuple-element.155.refs_0_), channel_id=1, source_target_pairs={{0,2},{1,3},{2,0},{3,1},{4,6},{5,7},{6,4},{7,5},{8,10},{9,11},{10,... | collective-permute-start | bytes 1179656 | tf_op jit(solution)/shard_map/ppermute | solution.py:419
  47.5 6.8 %copy-start.2 = (bf16[128,1536]{1,0:T(8,128)(2,1)}, bf16[128,1536]{1,0:T(8,128)(2,1)S(1)}, u32[]{:S(2)}) copy-start(bf16[128,1536]{1,0:T(8,128)(2,1)S(1)} %get-tuple-element.143.refs_0_) | copy-start | bytes 1179652
  49.5 0.8 copy-start.12
  50.3 9.9 %copy-start.19 = (bf16[512,1536]{1,0:T(8,128)(2,1)}, bf16[512,1536]{1,0:T(8,128)(2,1)S(1)}, u32[]{:S(2)}) copy-start(bf16[512,1536]{1,0:T(8,128)(2,1)S(1)} %get-tuple-element.146.refs_0_) | copy-start | bytes 4718596
  51.4 8.8 %collective-permute-start.12 = (bf16[384,768]{1,0:T(8,128)(2,1)S(1)}, bf16[384,768]{1,0:T(8,128)(2,1)S(1)}, u32[]{:S(2)}, u32[]{:S(2)}) collective-permute-start(bf16[384,768]{1,0:T(8,128)(2,1)S(1)} %get-tuple-element.150), channel_id=1, source_target_pairs={{0,1},{1,0},{2,3},{3,2},{4,5},{5,4},{6,7},{7,6},{8,9},{9,8},{10,11... | collective-permute-start | bytes 1769480 | tf_op jit(solution)/shard_map/ppermute | solution.py:410
  51.5 7.5 %copy-start.18 = (bf16[1536,768]{1,0:T(8,128)(2,1)S(1)}, bf16[1536,768]{1,0:T(8,128)(2,1)}, u32[]{:S(2)}) copy-start(bf16[1536,768]{1,0:T(8,128)(2,1)} %copy-done.17) | copy-start | bytes 7077892
  53.8 14.0 %collective-permute-start.20 = (bf16[384,1536]{1,0:T(8,128)(2,1)S(1)}, bf16[384,1536]{1,0:T(8,128)(2,1)S(1)}, u32[]{:S(2)}, u32[]{:S(2)}) collective-permute-start(bf16[384,1536]{1,0:T(8,128)(2,1)S(1)} %get-tuple-element.168), channel_id=1, source_target_pairs={{0,1},{1,0},{2,3},{3,2},{4,5},{5,4},{6,7},{7,6},{8,9},{9,8},{10,11... | collective-permute-start | bytes 3538952 | tf_op jit(solution)/shard_map/ppermute | solution.py:410
  54.3 12.0 %collective-permute-start.10 = (bf16[128,1536]{1,0:T(8,128)(2,1)S(1)}, bf16[128,1536]{1,0:T(8,128)(2,1)S(1)}, u32[]{:S(2)}, u32[]{:S(2)}) collective-permute-start(bf16[128,1536]{1,0:T(8,128)(2,1)S(1)} %get-tuple-element.143.refs_0_), channel_id=1, source_target_pairs={{0,2},{1,3},{2,0},{3,1},{4,6},{5,7},{6,4},{7,5},{8,10},{9,11},{10,... | collective-permute-start | bytes 1179656 | tf_op jit(solution)/shard_map/ppermute | solution.py:419
  55.9 24.4 %collective-permute-start.11 = (bf16[128,1536]{1,0:T(8,128)(2,1)S(1)}, bf16[128,1536]{1,0:T(8,128)(2,1)S(1)}, u32[]{:S(2)}, u32[]{:S(2)}) collective-permute-start(bf16[128,1536]{1,0:T(8,128)(2,1)S(1)} %get-tuple-element.145), channel_id=1, source_target_pairs={{0,4},{4,8},{8,12},{12,0},{1,5},{5,9},{9,13},{13,1},{2,6},{6,10},{... | collective-permute-start | bytes 1179656 | tf_op jit(solution)/shard_map/ppermute | solution.py:407
  59.0 1.1 copy-start.8
  60.1 2.1 %collective-permute-start.17 = (bf16[384,768]{1,0:T(8,128)(2,1)S(1)}, bf16[384,768]{1,0:T(8,128)(2,1)S(1)}, u32[]{:S(2)}, u32[]{:S(2)}) collective-permute-start(bf16[384,768]{1,0:T(8,128)(2,1)S(1)} %get-tuple-element.163), channel_id=1, source_target_pairs={{0,1},{1,0},{2,3},{3,2},{4,5},{5,4},{6,7},{7,6},{8,9},{9,8},{10,11... | collective-permute-start | bytes 1769480 | tf_op jit(solution)/shard_map/ppermute | solution.py:410
  61.3 2.6 %copy-start.20 = (bf16[512,1536]{1,0:T(8,128)(2,1)S(1)}, bf16[512,1536]{1,0:T(8,128)(2,1)}, u32[]{:S(2)}) copy-start(bf16[512,1536]{1,0:T(8,128)(2,1)} %copy-done.19) | copy-start | bytes 4718596
  61.4 17.6 %collective-permute-start.19 = (bf16[384,768]{1,0:T(8,128)(2,1)S(1)}, bf16[384,768]{1,0:T(8,128)(2,1)S(1)}, u32[]{:S(2)}, u32[]{:S(2)}) collective-permute-start(bf16[384,768]{1,0:T(8,128)(2,1)S(1)} %get-tuple-element.166.refs_2_), channel_id=1, source_target_pairs={{0,2},{1,3},{2,0},{3,1},{4,6},{5,7},{6,4},{7,5},{8,10},{9,11},{10,... | collective-permute-start | bytes 1769480 | tf_op jit(solution)/shard_map/ppermute | solution.py:419
  62.2 30.6 %collective-permute-start.15 = (bf16[128,1536]{1,0:T(8,128)(2,1)S(1)}, bf16[128,1536]{1,0:T(8,128)(2,1)S(1)}, u32[]{:S(2)}, u32[]{:S(2)}) collective-permute-start(bf16[128,1536]{1,0:T(8,128)(2,1)S(1)} %get-tuple-element.160), channel_id=1, source_target_pairs={{0,12},{4,0},{8,4},{12,8},{1,13},{5,1},{9,5},{13,9},{2,14},{6,2},{... | collective-permute-start | bytes 1179656 | tf_op jit(solution)/shard_map/ppermute | solution.py:407
  66.3 5.3 %copy-start.4 = (bf16[128,1536]{1,0:T(8,128)(2,1)}, bf16[128,1536]{1,0:T(8,128)(2,1)S(1)}, u32[]{:S(2)}) copy-start(bf16[128,1536]{1,0:T(8,128)(2,1)S(1)} %collective-permute-done.10.refs_4_.refs_1_) | copy-start | bytes 1179652
  66.3 27.5 %collective-permute-start.16 = (bf16[128,1536]{1,0:T(8,128)(2,1)S(1)}, bf16[128,1536]{1,0:T(8,128)(2,1)S(1)}, u32[]{:S(2)}, u32[]{:S(2)}) collective-permute-start(bf16[128,1536]{1,0:T(8,128)(2,1)S(1)} %get-tuple-element.161), channel_id=1, source_target_pairs={{0,8},{4,12},{8,0},{12,4},{1,9},{5,13},{9,1},{13,5},{2,10},{6,14},... | collective-permute-start | bytes 1179656 | tf_op jit(solution)/shard_map/ppermute | solution.py:407
  67.8 23.8 %collective-permute-start.18 = (bf16[384,768]{1,0:T(8,128)(2,1)S(1)}, bf16[384,768]{1,0:T(8,128)(2,1)S(1)}, u32[]{:S(2)}, u32[]{:S(2)}) collective-permute-start(bf16[384,768]{1,0:T(8,128)(2,1)S(1)} %get-tuple-element.165.refs_2_), channel_id=1, source_target_pairs={{0,2},{1,3},{2,0},{3,1},{4,6},{5,7},{6,4},{7,5},{8,10},{9,11},{10,... | collective-permute-start | bytes 1769480 | tf_op jit(solution)/shard_map/ppermute | solution.py:419
  80.2 15.4 %collective-permute-start.22 = (bf16[512,768]{1,0:T(8,128)(2,1)S(1)}, bf16[512,768]{1,0:T(8,128)(2,1)S(1)}, u32[]{:S(2)}, u32[]{:S(2)}) collective-permute-start(bf16[512,768]{1,0:T(8,128)(2,1)S(1)} %get-tuple-element.180.refs_1_), channel_id=1, source_target_pairs={{0,1},{1,0},{2,3},{3,2},{4,5},{5,4},{6,7},{7,6},{8,9},{9,8},{10,11... | collective-permute-start | bytes 2359304 | tf_op jit(solution)/shard_map/ppermute | solution.py:410
  80.3 36.6 %collective-permute-start.27 = (bf16[384,1536]{1,0:T(8,128)(2,1)S(1)}, bf16[384,1536]{1,0:T(8,128)(2,1)S(1)}, u32[]{:S(2)}, u32[]{:S(2)}) collective-permute-start(bf16[384,1536]{1,0:T(8,128)(2,1)S(1)} %get-tuple-element.193.refs_2_), channel_id=1, source_target_pairs={{0,2},{1,3},{2,0},{3,1},{4,6},{5,7},{6,4},{7,5},{8,10},{9,11},{10,... | collective-permute-start | bytes 3538952 | tf_op jit(solution)/shard_map/ppermute | solution.py:419
  95.0 5.1 %collective-permute-start.21 = (bf16[384,768]{1,0:T(8,128)(2,1)S(1)}, bf16[384,768]{1,0:T(8,128)(2,1)S(1)}, u32[]{:S(2)}, u32[]{:S(2)}) collective-permute-start(bf16[384,768]{1,0:T(8,128)(2,1)S(1)} %get-tuple-element.179), channel_id=1, source_target_pairs={{0,1},{1,0},{2,3},{3,2},{4,5},{5,4},{6,7},{7,6},{8,9},{9,8},{10,11... | collective-permute-start | bytes 1769480 | tf_op jit(solution)/shard_map/ppermute | solution.py:410
  95.1 8.0 %collective-permute-start.24 = (bf16[512,768]{1,0:T(8,128)(2,1)S(1)}, bf16[512,768]{1,0:T(8,128)(2,1)S(1)}, u32[]{:S(2)}, u32[]{:S(2)}) collective-permute-start(bf16[512,768]{1,0:T(8,128)(2,1)S(1)} %get-tuple-element.185.refs_1_), channel_id=1, source_target_pairs={{0,1},{1,0},{2,3},{3,2},{4,5},{5,4},{6,7},{7,6},{8,9},{9,8},{10,11... | collective-permute-start | bytes 2359304 | tf_op jit(solution)/shard_map/ppermute | solution.py:410
  102.3 5.3 %collective-permute-start.23 = (bf16[384,768]{1,0:T(8,128)(2,1)S(1)}, bf16[384,768]{1,0:T(8,128)(2,1)S(1)}, u32[]{:S(2)}, u32[]{:S(2)}) collective-permute-start(bf16[384,768]{1,0:T(8,128)(2,1)S(1)} %get-tuple-element.184), channel_id=1, source_target_pairs={{0,1},{1,0},{2,3},{3,2},{4,5},{5,4},{6,7},{7,6},{8,9},{9,8},{10,11... | collective-permute-start | bytes 1769480 | tf_op jit(solution)/shard_map/ppermute | solution.py:410
  102.5 32.8 %collective-permute-start.32 = (bf16[384,768]{1,0:T(8,128)(2,1)S(1)}, bf16[384,768]{1,0:T(8,128)(2,1)S(1)}, u32[]{:S(2)}, u32[]{:S(2)}) collective-permute-start(bf16[384,768]{1,0:T(8,128)(2,1)S(1)} %get-tuple-element.204.refs_2_), channel_id=1, source_target_pairs={{0,2},{1,3},{2,0},{3,1},{4,6},{5,7},{6,4},{7,5},{8,10},{9,11},{10,... | collective-permute-start | bytes 1769480 | tf_op jit(solution)/shard_map/ppermute | solution.py:419
  109.8 11.6 %collective-permute-start.26 = (bf16[384,768]{1,0:T(8,128)(2,1)S(1)}, bf16[384,768]{1,0:T(8,128)(2,1)S(1)}, u32[]{:S(2)}, u32[]{:S(2)}) collective-permute-start(bf16[384,768]{1,0:T(8,128)(2,1)S(1)} %get-tuple-element.192), channel_id=1, source_target_pairs={{0,1},{1,0},{2,3},{3,2},{4,5},{5,4},{6,7},{7,6},{8,9},{9,8},{10,11... | collective-permute-start | bytes 1769480 | tf_op jit(solution)/shard_map/ppermute | solution.py:410
  110.0 6.8 %copy-start.11 = (bf16[128,1536]{1,0:T(8,128)(2,1)S(1)}, bf16[128,1536]{1,0:T(8,128)(2,1)}, u32[]{:S(2)}) copy-start(bf16[128,1536]{1,0:T(8,128)(2,1)} %copy-done.10) | copy-start | bytes 1179652
  110.0 6.8 %copy-start.13 = (bf16[128,1536]{1,0:T(8,128)(2,1)S(1)}, bf16[128,1536]{1,0:T(8,128)(2,1)}, u32[]{:S(2)}) copy-start(bf16[128,1536]{1,0:T(8,128)(2,1)} %copy-done.12) | copy-start | bytes 1179652
  119.3 7.5 %collective-permute-start.33 = (bf16[512,1536]{1,0:T(8,128)(2,1)S(1)}, bf16[512,1536]{1,0:T(8,128)(2,1)S(1)}, u32[]{:S(2)}, u32[]{:S(2)}) collective-permute-start(bf16[512,1536]{1,0:T(8,128)(2,1)S(1)} %get-tuple-element.206.refs_1_), channel_id=1, source_target_pairs={{0,1},{1,0},{2,3},{3,2},{4,5},{5,4},{6,7},{7,6},{8,9},{9,8},{10,11... | collective-permute-start | bytes 4718600 | tf_op jit(solution)/shard_map/ppermute | solution.py:410
  119.4 4.2 %collective-permute-start.25 = (bf16[384,768]{1,0:T(8,128)(2,1)S(1)}, bf16[384,768]{1,0:T(8,128)(2,1)S(1)}, u32[]{:S(2)}, u32[]{:S(2)}) collective-permute-start(bf16[384,768]{1,0:T(8,128)(2,1)S(1)} %get-tuple-element.191), channel_id=1, source_target_pairs={{0,1},{1,0},{2,3},{3,2},{4,5},{5,4},{6,7},{7,6},{8,9},{9,8},{10,11... | collective-permute-start | bytes 1769480 | tf_op jit(solution)/shard_map/ppermute | solution.py:410
  119.8 22.3 %collective-permute-start.31 = (bf16[384,768]{1,0:T(8,128)(2,1)S(1)}, bf16[384,768]{1,0:T(8,128)(2,1)S(1)}, u32[]{:S(2)}, u32[]{:S(2)}) collective-permute-start(bf16[384,768]{1,0:T(8,128)(2,1)S(1)} %get-tuple-element.202.refs_2_), channel_id=1, source_target_pairs={{0,2},{1,3},{2,0},{3,1},{4,6},{5,7},{6,4},{7,5},{8,10},{9,11},{10,... | collective-permute-start | bytes 1769480 | tf_op jit(solution)/shard_map/ppermute | solution.py:419
  122.5 32.3 %collective-permute-start.30 = (bf16[384,768]{1,0:T(8,128)(2,1)S(1)}, bf16[384,768]{1,0:T(8,128)(2,1)S(1)}, u32[]{:S(2)}, u32[]{:S(2)}) collective-permute-start(bf16[384,768]{1,0:T(8,128)(2,1)S(1)} %get-tuple-element.201.refs_2_), channel_id=1, source_target_pairs={{0,2},{1,3},{2,0},{3,1},{4,6},{5,7},{6,4},{7,5},{8,10},{9,11},{10,... | collective-permute-start | bytes 1769480 | tf_op jit(solution)/shard_map/ppermute | solution.py:419
  124.4 36.8 %collective-permute-start.29 = (bf16[384,384]{1,0:T(8,128)(2,1)S(1)}, bf16[384,384]{1,0:T(8,128)(2,1)S(1)}, u32[]{:S(2)}, u32[]{:S(2)}) collective-permute-start(bf16[384,384]{1,0:T(8,128)(2,1)S(1)} %get-tuple-element.200.refs_2_), channel_id=1, source_target_pairs={{0,2},{1,3},{2,0},{3,1},{4,6},{5,7},{6,4},{7,5},{8,10},{9,11},{10,... | collective-permute-start | bytes 884744 | tf_op jit(solution)/shard_map/ppermute | solution.py:419
  126.8 39.9 %collective-permute-start.28 = (bf16[384,384]{1,0:T(8,128)(2,1)S(1)}, bf16[384,384]{1,0:T(8,128)(2,1)S(1)}, u32[]{:S(2)}, u32[]{:S(2)}) collective-permute-start(bf16[384,384]{1,0:T(8,128)(2,1)S(1)} %get-tuple-element.198.refs_2_), channel_id=1, source_target_pairs={{0,2},{1,3},{2,0},{3,1},{4,6},{5,7},{6,4},{7,5},{8,10},{9,11},{10,... | collective-permute-start | bytes 884744 | tf_op jit(solution)/shard_map/ppermute | solution.py:419
  127.4 8.0 %copy-start.7 = (bf16[128,1536]{1,0:T(8,128)(2,1)S(1)}, bf16[128,1536]{1,0:T(8,128)(2,1)}, u32[]{:S(2)}) copy-start(bf16[128,1536]{1,0:T(8,128)(2,1)} %copy-done.6) | copy-start | bytes 1179652
  127.4 8.0 %copy-start.9 = (bf16[128,1536]{1,0:T(8,128)(2,1)S(1)}, bf16[128,1536]{1,0:T(8,128)(2,1)}, u32[]{:S(2)}) copy-start(bf16[128,1536]{1,0:T(8,128)(2,1)} %copy-done.8) | copy-start | bytes 1179652
  136.0 6.9 %collective-permute-start.35 = (bf16[512,768]{1,0:T(8,128)(2,1)S(1)}, bf16[512,768]{1,0:T(8,128)(2,1)S(1)}, u32[]{:S(2)}, u32[]{:S(2)}) collective-permute-start(bf16[512,768]{1,0:T(8,128)(2,1)S(1)} %get-tuple-element.212.refs_1_), channel_id=1, source_target_pairs={{0,1},{1,0},{2,3},{3,2},{4,5},{5,4},{6,7},{7,6},{8,9},{9,8},{10,11... | collective-permute-start | bytes 2359304 | tf_op jit(solution)/shard_map/ppermute | solution.py:410
  142.2 0.8 copy-start.16
  142.8 4.4 %collective-permute-start.34 = (bf16[512,768]{1,0:T(8,128)(2,1)S(1)}, bf16[512,768]{1,0:T(8,128)(2,1)S(1)}, u32[]{:S(2)}, u32[]{:S(2)}) collective-permute-start(bf16[512,768]{1,0:T(8,128)(2,1)S(1)} %get-tuple-element.211.refs_1_), channel_id=1, source_target_pairs={{0,1},{1,0},{2,3},{3,2},{4,5},{5,4},{6,7},{7,6},{8,9},{9,8},{10,11... | collective-permute-start | bytes 2359304 | tf_op jit(solution)/shard_map/ppermute | solution.py:410
  147.3 7.5 %copy-start.3 = (bf16[128,1536]{1,0:T(8,128)(2,1)S(1)}, bf16[128,1536]{1,0:T(8,128)(2,1)}, u32[]{:S(2)}) copy-start(bf16[128,1536]{1,0:T(8,128)(2,1)} %copy-done.2) | copy-start | bytes 1179652
  147.3 7.5 %copy-start.5 = (bf16[128,1536]{1,0:T(8,128)(2,1)S(1)}, bf16[128,1536]{1,0:T(8,128)(2,1)}, u32[]{:S(2)}) copy-start(bf16[128,1536]{1,0:T(8,128)(2,1)} %copy-done.4) | copy-start | bytes 1179652
  155.5 2.9 %collective-permute-start.36 = (bf16[512,768]{1,0:T(8,128)(2,1)S(1)}, bf16[512,768]{1,0:T(8,128)(2,1)S(1)}, u32[]{:S(2)}, u32[]{:S(2)}) collective-permute-start(bf16[512,768]{1,0:T(8,128)(2,1)S(1)} %get-tuple-element.217.refs_1_), channel_id=1, source_target_pairs={{0,1},{1,0},{2,3},{3,2},{4,5},{5,4},{6,7},{7,6},{8,9},{9,8},{10,11... | collective-permute-start | bytes 2359304 | tf_op jit(solution)/shard_map/ppermute | solution.py:410
  161.4 2.6 %collective-permute-start.37 = (bf16[512,384]{1,0:T(8,128)(2,1)S(1)}, bf16[512,384]{1,0:T(8,128)(2,1)S(1)}, u32[]{:S(2)}, u32[]{:S(2)}) collective-permute-start(bf16[512,384]{1,0:T(8,128)(2,1)S(1)} %get-tuple-element.223.refs_1_), channel_id=1, source_target_pairs={{0,1},{1,0},{2,3},{3,2},{4,5},{5,4},{6,7},{7,6},{8,9},{9,8},{10,11... | collective-permute-start | bytes 1179656 | tf_op jit(solution)/shard_map/ppermute | solution.py:410
  166.9 2.1 %collective-permute-start.38 = (bf16[512,384]{1,0:T(8,128)(2,1)S(1)}, bf16[512,384]{1,0:T(8,128)(2,1)S(1)}, u32[]{:S(2)}, u32[]{:S(2)}) collective-permute-start(bf16[512,384]{1,0:T(8,128)(2,1)S(1)} %get-tuple-element.229.refs_1_), channel_id=1, source_target_pairs={{0,1},{1,0},{2,3},{3,2},{4,5},{5,4},{6,7},{7,6},{8,9},{9,8},{10,11... | collective-permute-start | bytes 1179656 | tf_op jit(solution)/shard_map/ppermute | solution.py:410
where the time goes:
time: 172 us; the launch traced here: 171 us
  Pallas kernels  96.8 us (56%)
  waiting for transfers between devices  37.8 us (22%)
  starting transfers between devices  31 us (18%)
  local copies, waits for them, and re-layouts  4.18 us (2%)
    pallas_call x25, Pallas kernels, project(): pl.pallas_call(functools.partial(project_kernel, fresh, down, bool(arrive...  49.4 us
    pallas_call x11, Pallas kernels, gradient(): pl.pallas_call(functools.partial(gradient_kernel, down, parts, span, star...  39.4 us
    ppermute x13, waiting for transfers between devices, chip_swap(): lax.ppermute(value, 'col', [(i, i ^ CORES * hop) for i in range(n_col)])  34.1 us
    ppermute x13, starting transfers between devices, chip_swap(): lax.ppermute(value, 'col', [(i, i ^ CORES * hop) for i in range(n_col)])  14.3 us
    ppermute x6, starting transfers between devices, turn(): lax.ppermute(value, 'row', [(i, (i + by) % n_row) for i in range(n_row)])  12.6 us
    pallas_call x8, Pallas kernels, pointwise(): pl.pallas_call(functools.partial(kernel, len(pairs)), out_shape=shapes, g...  7.19 us
    unnamed x43, local copies, waits for them, and re-layouts  4.18 us
    ppermute x20, starting transfers between devices, core_swap(): return lax.ppermute(value, 'col', [(i, i ^ 1) for i in range(n_col)])  4.06 us
  transfers between devices with their start and end apart: 39, of which 11 were waited for; matrix products, arithmetic and copies ran while one was open for 0% of the time, Pallas kernels for 54%

commit v1 on v0

--- a/solution.py
+++ b/solution.py
@@ -99,13 +99,14 @@
     )
 
 
-def spread_mask(mask, rows, columns):
-    tall, wide = mask.shape
+def spread_mask(mask, down, rows, columns):
+    wide, tall = mask.shape if down else mask.shape[::-1]
     bits = mask[...].astype(jnp.bfloat16)
-    if rows[1] != tall:
+    if down or rows[1] != tall:
         at = (rows[1], tall)
         pick = lax.broadcasted_iota(jnp.int32, at, 0) + rows[0] == lax.broadcasted_iota(jnp.int32, at, 1)
-        bits = jnp.dot(pick.astype(jnp.bfloat16), bits, preferred_element_type=jnp.float32).astype(jnp.bfloat16)
+        dims = (((1,), (1 if down else 0,)), ((), ()))
+        bits = lax.dot_general(pick.astype(jnp.bfloat16), bits, dims, preferred_element_type=jnp.float32).astype(jnp.bfloat16)
     at = (wide, columns[1] * BLOCK)
     pick = lax.broadcasted_iota(jnp.int32, at, 1) // BLOCK + columns[0] == lax.broadcasted_iota(jnp.int32, at, 0)
     return jnp.dot(bits, pick.astype(jnp.bfloat16), preferred_element_type=jnp.float32).astype(jnp.bfloat16)
@@ -116,7 +117,7 @@
     return (run, slice(None)) if down else (slice(None), run)
 
 
-def project_kernel(fresh, down, summed, waits, span, start, offset, skip, tile, half, *refs):
+def project_kernel(opening, fresh, down, summed, waits, span, start, offset, skip, tile, half, *refs):
     refs = list(refs)
     rows = refs.pop(0)
     source = refs.pop(0)
@@ -124,7 +125,17 @@
     arrived = refs.pop(0) if summed else None
     refs = refs[waits:]
     out = refs.pop(0)
-    kept, sems = (refs[0], refs[-1]) if fresh else (source, None)
+    kept = refs[0] if fresh else source
+    sems = refs[2] if fresh and not opening else refs[3] if opening else None
+    if opening:
+        echo, held, more = refs[1], *refs[4:]
+        small = [
+            pltpu.make_async_copy(rows, echo, more.at[0]),
+            pltpu.make_async_copy(mask, held, more.at[1]),
+        ]
+        for one in small:
+            one.start()
+        rows, mask = echo, held
     steps = out.shape[1] // tile
     begin = half[0] * span + start
 
@@ -135,6 +146,8 @@
 
     for step in range(steps if fresh else 0):
         copy(step).start()
+    for one in small if opening else []:
+        one.wait()
     inputs = rows[pl.ds(rows.shape[0] - out.shape[0], out.shape[0]), :]
 
     def chunk(step, carry):
@@ -143,7 +156,8 @@
             first = pl.multiple_of(first, BLOCK)
         if fresh:
             run = ((begin + step * tile) // BLOCK, tile // BLOCK)
-            bits = spread_mask(mask, run, (0, mask.shape[1])) if down else spread_mask(mask, (0, mask.shape[0]), run)
+            every = (0, mask.shape[0])
+            bits = spread_mask(mask, down, run, every) if down else spread_mask(mask, down, every, run)
             copy(step).wait()
             for i in range(bits.shape[0]):
                 if down:
@@ -169,12 +183,15 @@
         lax.fori_loop(0, steps, chunk, 0)
 
 
-def project(inputs, count, weight, mask, down, half, span, start, skip, width, arrived, before):
+def project(inputs, count, weight, mask, down, opening, half, span, start, skip, width, arrived, before):
     fresh = mask is not None
     tile = tile_of(width, 768)
     if fresh:
         given = [inputs, pltpu.with_memory_space_constraint(weight, pltpu.HBM), mask]
         specs = [VMEM, ANY, VMEM]
+        if opening:
+            given = [pltpu.with_memory_space_constraint(array, pltpu.HBM) for array in (inputs, weight, mask)]
+            specs = [ANY] * 3
     else:
         given = [inputs, pltpu.with_memory_space_constraint(weight, pltpu.VMEM)]
         specs = [VMEM, VMEM]
@@ -185,15 +202,19 @@
     if fresh:
         model = weight.shape[1 if down else 0]
         shapes.append(pltpu.VMEM((width, model) if down else (model, width), weight.dtype))
+    scratch = [pltpu.SemaphoreType.DMA((width // tile,))] if fresh else []
+    if opening:
+        shapes.append(jax.ShapeDtypeStruct(inputs.shape, inputs.dtype))
+        scratch += [pltpu.VMEM(mask.shape, mask.dtype), pltpu.SemaphoreType.DMA((2,))]
     offset = arrived[1] if arrived else 0
     return pl.pallas_call(
         functools.partial(
-            project_kernel, fresh, down, bool(arrived), len(before), span, start, offset, skip, tile
+            project_kernel, opening, fresh, down, bool(arrived), len(before), span, start, offset, skip, tile
         ),
         out_shape=(*shapes, TICKET),
         in_specs=[pl.BlockSpec(memory_space=pltpu.SMEM)] + specs + [ANY] * len(before),
         out_specs=(VMEM,) * len(shapes) + (ANY,),
-        scratch_shapes=[pltpu.SemaphoreType.DMA((width // tile,))] if fresh else [],
+        scratch_shapes=scratch,
         compiler_params=pltpu.CompilerParams(vmem_limit_bytes=12 * 1024 * 1024),
         cost_estimate=BRIEF,
         name="project_down" if down else "project_up",
@@ -335,10 +356,10 @@
         blocks = part_rows // BLOCK
         if down:
             left, right, dims = unit_columns(slice(None), at), fixed[...], (((0,), (0,)), ((), ()))
-            bits = spread_mask(mask, (first + i * blocks, blocks), (0, mask.shape[1]))
+            bits = spread_mask(mask, down, (first + i * blocks, blocks), (0, mask.shape[0]))
         else:
             left, right, dims = fixed[at, :], unit_columns(slice(None), slice(None)), (((1,), (0,)), ((), ()))
-            bits = spread_mask(mask, (i * blocks, blocks), (first, tile // BLOCK))
+            bits = spread_mask(mask, down, (i * blocks, blocks), (first, tile // BLOCK))
         value = lax.dot_general(left, right, dims, preferred_element_type=jnp.float32)
         for j in range(blocks):
             block = value[j * BLOCK : (j + 1) * BLOCK, :].astype(out.dtype)
@@ -429,12 +450,12 @@
     chunks = {name: cuts(eighths) for name, eighths in CUTS.items()}
     own = tokens.shape[0]
     inputs = {"h0": (tokens, own), "g0": (cotangent, own)}
-    weights = {"h": (up_weight, up_mask), "g": (down_weight, down_mask)}
+    weights = {"h": (up_weight, up_mask), "g": (down_weight, down_mask.T)}
     near = sorted({1, n_row - 1} - {0}) if n_row > 1 else []
     turns = [near[:1], near[1:], [by for by in range(1, n_row) if by not in near]]
     shards = {"x": tokens, "c": cotangent}
     moves, sent, sums, stored, slopes, acts, hidden, grads = {}, {}, {}, [], [], {}, {}, {}
-    before = [begin([mine, other], [up_mask, down_mask])]
+    before = [begin([mine, other], [])]
 
     def step(call, *args):
         nonlocal before
@@ -450,11 +471,14 @@
         half, down = (mine, other)[side], key[0] == "g"
         if key[1] == "0":
             weight, mask = weights[key[0]]
-            result, kept = step(project, rows, count, weight, mask, down, half, span, start, 0, width, arrived)
+            opening = not stored and key == "h0"
+            result, kept, *echo = step(project, rows, count, weight, mask, down, opening, half, span, start, 0, width, arrived)
+            if opening:
+                shards["echo"] = echo[0]
             stored.append((start, width, key[0], side, kept))
             return result
         at, _, _, _, kept = covering([one for one in stored if one[2:4] == (key[0], side)], start, width)
-        return step(project, rows, count, kept, None, down, half, span, start, start - at, width, arrived)
+        return step(project, rows, count, kept, None, down, False, half, span, start, start - at, width, arrived)
 
     def pairs(kind, start, width):
         found = []
@@ -466,7 +490,7 @@
     def run(action, name, at):
         if action == "turn":
             if turns[at]:
-                source = step(late, shards[name])
+                source = shards["echo"] if name == "x" and at < 2 else step(late, shards[name])
                 moves[name, at] = [turn(source, by) for by in turns[at]]
             else:
                 moves[name, at] = []
@@ -499,7 +523,7 @@
             acts[at] = act, core_swap(act)
         elif action == "down":
             grads["down"] = step(
-                gradient, stacks["c"], acts[at], down_mask, True, mine, start, units, grads.get("down")
+                gradient, stacks["c"], acts[at], down_mask.T, True, mine, start, units, grads.get("down")
             )
         elif action == "hidden":
             first, _, slope = covering(slopes, start, width)

time: 172 us -> 169 us (0.983)
  local copies, waits for them, and re-layouts: 4.18 us -> 2.08 us
    unnamed x43 -> x42, local copies, waits for them, and re-layouts: 4.18 us -> 2.08 us
  transfers between devices with their start and end apart: 39 -> 39, of which waited for: 11 -> 11; matrix products, arithmetic and copies ran while one was open for 0% -> 0% of each run, Pallas kernels for 54% -> 55%
where the time goes in v1:
time: 169 us; the launch traced here: 168 us
  Pallas kernels  97 us (57%)
  waiting for transfers between devices  38.2 us (23%)
  starting transfers between devices  29.9 us (18%)
  local copies, waits for them, and re-layouts  2.08 us (1%)
    pallas_call x25, Pallas kernels, project(): pl.pallas_call(functools.partial(project_kernel, opening, fresh, down, bo...  49.7 us
    pallas_call x11, Pallas kernels, gradient(): pl.pallas_call(functools.partial(gradient_kernel, down, parts, span, star...  39.4 us
    ppermute x13, waiting for transfers between devices, chip_swap(): lax.ppermute(value, 'col', [(i, i ^ CORES * hop) for i in range(n_col)])  34.4 us
    ppermute x13, starting transfers between devices, chip_swap(): lax.ppermute(value, 'col', [(i, i ^ CORES * hop) for i in range(n_col)])  14.3 us
    ppermute x6, starting transfers between devices, turn(): lax.ppermute(value, 'row', [(i, (i + by) % n_row) for i in range(n_row)])  11.5 us
    pallas_call x8, Pallas kernels, pointwise(): pl.pallas_call(functools.partial(kernel, len(pairs)), out_shape=shapes, g...  7.19 us
    ppermute x20, starting transfers between devices, core_swap(): return lax.ppermute(value, 'col', [(i, i ^ 1) for i in range(n_col)])  4.09 us
  transfers between devices with their start and end apart: 39, of which 11 were waited for; matrix products, arithmetic and copies ran while one was open for 0% of the time, Pallas kernels for 55%

profile of v1, /device:TPU:0, one launch (start us, length us, event | category | flops | bytes accessed | tf_op | source)
XLA Modules:
  0.0 168.4 jit_solution(15154760784781923615)
XLA Ops:
  0.7 2.5 %project_up.12 = (bf16[128,768]{1,0:T(8,128)(2,1)S(1)}, bf16[1536,768]{1,0:T(8,128)(2,1)S(1)}, bf16[128,1536]{1,0:T(8,128)(2,1)S(1)}, f32[8,128]{1,0:T(8,128)S(1)}) custom-call(s32[1]{0:T(128)S(6)} %sub.3.refs_1_.half, bf16[128,1536]{1,0:T(8,128)(2,1)} %refs_0_.22, bf16[1536,6144]{1,0:T(8,128)(2,1)} %refs_1_.16, s32[12,48]{1,0:T(8,128)} %mask.15, ...), custom_call_target="tpu_custom_call" | custom-call | flops 10000000000 | tf_op jit(solution)/shard_map/project_up/pallas_call | solution.py:210
  3.1 5.1 %collective-permute-start.1 = (bf16[128,1536]{1,0:T(8,128)(2,1)S(1)}, bf16[128,1536]{1,0:T(8,128)(2,1)S(1)}, u32[]{:S(2)}, u32[]{:S(2)}) collective-permute-start(bf16[128,1536]{1,0:T(8,128)(2,1)S(1)} %get-tuple-element.116), channel_id=1, source_target_pairs={{0,12},{4,0},{8,4},{12,8},{1,13},{5,1},{9,5},{13,9},{2,14},{6,2},{... | collective-permute-start | bytes 1179656 | tf_op jit(solution)/shard_map/ppermute | solution.py:428
  8.3 2.3 %project_up.13 = (bf16[128,768]{1,0:T(8,128)(2,1)S(1)}, bf16[1536,768]{1,0:T(8,128)(2,1)S(1)}, f32[8,128]{1,0:T(8,128)S(1)}) custom-call(s32[1]{0:T(128)S(6)} %sub.3.refs_1_.half, bf16[128,1536]{1,0:T(8,128)(2,1)S(1)} %copy-done, bf16[1536,6144]{1,0:T(8,128)(2,1)} %refs_1_.16, s32[12,48]{1,0:T(8,128)S(1)} %copy-done.15, f32[8,128]{1,0:T(8,128)S(1)} %get-tuple-element.117.refs_3_), custom_call_target="tpu_custom_call" | custom-call | flops 10000000000 | tf_op jit(solution)/shard_map/project_up/pallas_call | solution.py:210
  11.1 2.3 %project_up.14 = (bf16[128,768]{1,0:T(8,128)(2,1)S(1)}, bf16[1536,768]{1,0:T(8,128)(2,1)S(1)}, f32[8,128]{1,0:T(8,128)S(1)}) custom-call(s32[1]{0:T(128)} %bitcast.refs_0_.half, bf16[128,1536]{1,0:T(8,128)(2,1)S(1)} %copy-done, bf16[1536,6144]{1,0:T(8,128)(2,1)} %refs_1_.16, s32[12,48]{1,0:T(8,128)S(1)} %copy-done.15, ...), custom_call_target="tpu_custom_call" | custom-call | flops 10000000000 | tf_op jit(solution)/shard_map/project_up/pallas_call | solution.py:210
  13.4 3.0 %project_up.15 = (bf16[128,1536]{1,0:T(8,128)(2,1)S(1)}, bf16[1536,1536]{1,0:T(8,128)(2,1)S(1)}, f32[8,128]{1,0:T(8,128)S(1)}) custom-call(s32[1]{0:T(128)S(6)} %sub.3.refs_1_.half, bf16[128,1536]{1,0:T(8,128)(2,1)S(1)} %copy-done, bf16[1536,6144]{1,0:T(8,128)(2,1)} %refs_1_.16, s32[12,48]{1,0:T(8,128)S(1)} %copy-done.15, ...), custom_call_target="tpu_custom_call" | custom-call | flops 10000000000 | tf_op jit(solution)/shard_map/project_up/pallas_call | solution.py:210
  16.5 1.6 collective-permute-start.6
  18.0 2.3 %project_up.16 = (bf16[128,768]{1,0:T(8,128)(2,1)S(1)}, bf16[1536,768]{1,0:T(8,128)(2,1)S(1)}, f32[8,128]{1,0:T(8,128)S(1)}) custom-call(s32[1]{0:T(128)} %bitcast.refs_0_.half, bf16[128,1536]{1,0:T(8,128)(2,1)S(1)} %copy-done, bf16[1536,6144]{1,0:T(8,128)(2,1)} %refs_1_.16, s32[12,48]{1,0:T(8,128)S(1)} %copy-done.15, ...), custom_call_target="tpu_custom_call" | custom-call | flops 10000000000 | tf_op jit(solution)/shard_map/project_up/pallas_call | solution.py:210
  20.9 4.0 %project_down.13 = (bf16[128,1536]{1,0:T(8,128)(2,1)S(1)}, bf16[1536,1536]{1,0:T(8,128)(2,1)S(1)}, f32[8,128]{1,0:T(8,128)S(1)}) custom-call(s32[1]{0:T(128)S(6)} %sub.3.refs_1_.half, bf16[128,1536]{1,0:T(8,128)(2,1)S(1)} %copy-done.1, bf16[6144,1536]{1,0:T(8,128)(2,1)} %refs_1_.19, s32[12,48]{1,0:T(8,128)S(1)} %bitcast.2, ...), custom_call_target="tpu_custom_call" | custom-call | flops 10000000000 | tf_op jit(solution)/shard_map/project_down/pallas_call | solution.py:210
  25.1 1.1 collective-permute-start.4
  26.2 3.0 %project_up.17 = (bf16[128,1536]{1,0:T(8,128)(2,1)S(1)}, bf16[1536,1536]{1,0:T(8,128)(2,1)S(1)}, f32[8,128]{1,0:T(8,128)S(1)}) custom-call(s32[1]{0:T(128)} %bitcast.refs_0_.half, bf16[128,1536]{1,0:T(8,128)(2,1)S(1)} %copy-done, bf16[1536,6144]{1,0:T(8,128)(2,1)} %refs_1_.16, s32[12,48]{1,0:T(8,128)S(1)} %copy-done.15, ...), custom_call_target="tpu_custom_call" | custom-call | flops 10000000000 | tf_op jit(solution)/shard_map/project_up/pallas_call | solution.py:210
  29.2 4.2 %project_down.14 = (bf16[128,1536]{1,0:T(8,128)(2,1)S(1)}, bf16[1536,1536]{1,0:T(8,128)(2,1)S(1)}, f32[8,128]{1,0:T(8,128)S(1)}) custom-call(s32[1]{0:T(128)S(6)} %sub.3.refs_1_.half, bf16[128,1536]{1,0:T(8,128)(2,1)S(1)} %copy-done.1, bf16[6144,1536]{1,0:T(8,128)(2,1)} %refs_1_.19, s32[12,48]{1,0:T(8,128)S(1)} %bitcast.3, ...), custom_call_target="tpu_custom_call" | custom-call | flops 10000000000 | tf_op jit(solution)/shard_map/project_down/pallas_call | solution.py:210
  33.6 1.5 collective-permute-start.9
  35.2 4.0 %project_down.15 = (bf16[128,1536]{1,0:T(8,128)(2,1)S(1)}, bf16[1536,1536]{1,0:T(8,128)(2,1)S(1)}, f32[8,128]{1,0:T(8,128)S(1)}) custom-call(s32[1]{0:T(128)} %bitcast.refs_0_.half, bf16[128,1536]{1,0:T(8,128)(2,1)S(1)} %copy-done.1, bf16[6144,1536]{1,0:T(8,128)(2,1)} %refs_1_.19, s32[12,48]{1,0:T(8,128)S(1)} %bitcast.4, ...), custom_call_target="tpu_custom_call" | custom-call | flops 10000000000 | tf_op jit(solution)/shard_map/project_down/pallas_call | solution.py:210
  39.8 4.0 %project_down.16 = (bf16[128,1536]{1,0:T(8,128)(2,1)S(1)}, bf16[1536,1536]{1,0:T(8,128)(2,1)S(1)}, f32[8,128]{1,0:T(8,128)S(1)}) custom-call(s32[1]{0:T(128)} %bitcast.refs_0_.half, bf16[128,1536]{1,0:T(8,128)(2,1)S(1)} %copy-done.1, bf16[6144,1536]{1,0:T(8,128)(2,1)} %refs_1_.19, s32[12,48]{1,0:T(8,128)S(1)} %bitcast.5, ...), custom_call_target="tpu_custom_call" | custom-call | flops 10000000000 | tf_op jit(solution)/shard_map/project_down/pallas_call | solution.py:210
  43.9 2.1 %collective-permute-done.4.refs_3_ = bf16[128,1536]{1,0:T(8,128)(2,1)S(1)} collective-permute-done((bf16[128,1536]{1,0:T(8,128)(2,1)S(1)}, bf16[128,1536]{1,0:T(8,128)(2,1)S(1)}, u32[]{:S(2)}, u32[]{:S(2)}) %collective-permute-start.4) | collective-permute-done | bytes 393248 | tf_op jit(solution)/shard_map/ppermute | solution.py:428
  46.8 1.1 copy-done.17
  47.9 1.1 project_up.18
  49.0 2.3 %project_up.19 = (bf16[384,1536]{1,0:T(8,128)(2,1)S(1)}, f32[8,128]{1,0:T(8,128)S(1)}) custom-call(s32[1]{0:T(128)S(6)} %sub.3.refs_1_.half, bf16[512,1536]{1,0:T(8,128)(2,1)S(1)} %get-tuple-element.140.refs_0_, bf16[1536,1536]{1,0:T(8,128)(2,1)S(1)} %get-tuple-element.146.refs_1_, f32[8,128]{1,0:T(8,128)S(1)} %get-tuple-element.147.refs_2_), custom_call_target="tpu_custom_call" | custom-call | flops 10000000000 | tf_op jit(solution)/shard_map/project_up/pallas_call | solution.py:210
  51.9 1.5 collective-permute-start.10
  53.4 3.0 %collective-permute-start.11 = (bf16[128,1536]{1,0:T(8,128)(2,1)S(1)}, bf16[128,1536]{1,0:T(8,128)(2,1)S(1)}, u32[]{:S(2)}, u32[]{:S(2)}) collective-permute-start(bf16[128,1536]{1,0:T(8,128)(2,1)S(1)} %get-tuple-element.139), channel_id=1, source_target_pairs={{0,4},{4,8},{8,12},{12,0},{1,5},{5,9},{9,13},{13,1},{2,6},{6,10},{... | collective-permute-start | bytes 1179656 | tf_op jit(solution)/shard_map/ppermute | solution.py:428
  56.4 1.1 project_up.20
  57.6 1.1 project_up.21
  59.5 0.9 collective-permute-start.15
  60.4 1.1 project_up.22
  61.5 2.4 %collective-permute-done.10.refs_4_.refs_1_ = bf16[128,1536]{1,0:T(8,128)(2,1)S(1)} collective-permute-done((bf16[128,1536]{1,0:T(8,128)(2,1)S(1)}, bf16[128,1536]{1,0:T(8,128)(2,1)S(1)}, u32[]{:S(2)}, u32[]{:S(2)}) %collective-permute-start.10) | collective-permute-done | bytes 393248 | tf_op jit(solution)/shard_map/ppermute | solution.py:440
  63.8 1.5 collective-permute-start.16
  65.4 1.5 collective-permute-start.18
  66.9 2.3 %project_up.23 = (bf16[384,1536]{1,0:T(8,128)(2,1)S(1)}, f32[8,128]{1,0:T(8,128)S(1)}) custom-call(s32[1]{0:T(128)} %bitcast.refs_0_.half, bf16[512,1536]{1,0:T(8,128)(2,1)S(1)} %copy-done.20, bf16[1536,1536]{1,0:T(8,128)(2,1)S(1)} %get-tuple-element.161.refs_1_, bf16[384,1536]{1,0:T(8,128)(2,1)S(1)} %collective-permute-done.20.refs_2_, ...), custom_call_target="tpu_custom_call" | custom-call | flops 10000000000 | tf_op jit(solution)/shard_map/project_up/pallas_call | solution.py:210
  69.2 7.3 %collective-permute-done.19.refs_3_ = bf16[384,768]{1,0:T(8,128)(2,1)S(1)} collective-permute-done((bf16[384,768]{1,0:T(8,128)(2,1)S(1)}, bf16[384,768]{1,0:T(8,128)(2,1)S(1)}, u32[]{:S(2)}, u32[]{:S(2)}) %collective-permute-start.19) | collective-permute-done | bytes 589856 | tf_op jit(solution)/shard_map/ppermute | solution.py:440
  76.5 1.2 activation.3
  77.8 1.6 collective-permute-start.27
  79.4 9.7 %collective-permute-done.18.refs_3_ = bf16[384,768]{1,0:T(8,128)(2,1)S(1)} collective-permute-done((bf16[384,768]{1,0:T(8,128)(2,1)S(1)}, bf16[384,768]{1,0:T(8,128)(2,1)S(1)}, u32[]{:S(2)}, u32[]{:S(2)}) %collective-permute-start.18) | collective-permute-done | bytes 589856 | tf_op jit(solution)/shard_map/ppermute | solution.py:440
  89.1 1.2 activation.4
  90.3 1.0 collective-permute-done.16.refs_3_
  91.4 1.1 project_down.17
  93.1 4.5 %down_gradient.3 = (bf16[6144,1536]{1,0:T(8,128)(2,1)}, f32[8,128]{1,0:T(8,128)S(1)}) custom-call(s32[1]{0:T(128)} %bitcast.refs_0_.half, s32[12,48]{1,0:T(8,128)S(1)} %bitcast.6, bf16[512,1536]{1,0:T(8,128)(2,1)S(1)} %get-tuple-element.167.refs_0_, bf16[512,768]{1,0:T(8,128)(2,1)S(1)} %get-tuple-element.174.refs_1_, ...), custom_call_target="tpu_custom_call" | custom-call | flops 10000000000 | tf_op jit(solution)/shard_map/down_gradient/pallas_call | solution.py:403
  97.7 1.1 project_down.18
  98.8 1.1 project_down.19
  100.6 4.5 %down_gradient.4 = (bf16[6144,1536]{1,0:T(8,128)(2,1)}, f32[8,128]{1,0:T(8,128)S(1)}) custom-call(s32[1]{0:T(128)} %bitcast.refs_0_.half, s32[12,48]{1,0:T(8,128)S(1)} %bitcast.7, bf16[512,1536]{1,0:T(8,128)(2,1)S(1)} %get-tuple-element.167.refs_0_, bf16[512,768]{1,0:T(8,128)(2,1)S(1)} %get-tuple-element.179.refs_1_, ...), custom_call_target="tpu_custom_call", output_to_operand_aliasing={{0}: (5, {})} | custom-call | flops 10000000000 | tf_op jit(solution)/shard_map/down_gradient/pallas_call | solution.py:403
  105.1 1.1 project_down.20
  106.2 1.1 project_down.21
  107.6 1.1 project_down.22
  108.7 5.7 %collective-permute-done.27.refs_3_ = bf16[384,1536]{1,0:T(8,128)(2,1)S(1)} collective-permute-done((bf16[384,1536]{1,0:T(8,128)(2,1)S(1)}, bf16[384,1536]{1,0:T(8,128)(2,1)S(1)}, u32[]{:S(2)}, u32[]{:S(2)}) %collective-permute-start.27) | collective-permute-done | bytes 1179680 | tf_op jit(solution)/shard_map/ppermute | solution.py:440
  114.4 2.4 %activation.5 = (bf16[512,1536]{1,0:T(8,128)(2,1)S(1)}, f32[512,1536]{1,0:T(8,128)S(1)}, f32[8,128]{1,0:T(8,128)S(1)}) custom-call(bf16[128,1536]{1,0:T(8,128)(2,1)S(1)} %copy-done.11, bf16[128,1536]{1,0:T(8,128)(2,1)S(1)} %copy-done.13, bf16[384,1536]{1,0:T(8,128)(2,1)S(1)} %get-tuple-element.187.refs_2_, ...), custom_call_target="tpu_custom_call" | custom-call | flops 10000000000 | tf_op jit(solution)/shard_map/activation/pallas_call | solution.py:270
  117.4 1.5 collective-permute-start.31
  118.9 1.1 project_down.23
  121.1 0.8 project_down.24
  121.9 1.6 collective-permute-start.29
  123.5 0.8 project_down.25
  124.9 7.9 %down_gradient.5 = (bf16[6144,1536]{1,0:T(8,128)(2,1)}, f32[8,128]{1,0:T(8,128)S(1)}) custom-call(s32[1]{0:T(128)} %bitcast.refs_0_.half, s32[12,48]{1,0:T(8,128)S(1)} %bitcast.8, bf16[512,1536]{1,0:T(8,128)(2,1)S(1)} %get-tuple-element.167.refs_0_, bf16[512,1536]{1,0:T(8,128)(2,1)S(1)} %get-tuple-element.200.refs_1_, ...), custom_call_target="tpu_custom_call", output_to_operand_aliasing={{0}: (5, {})} | custom-call | flops 10000000000 | tf_op jit(solution)/shard_map/down_gradient/pallas_call | solution.py:403
  132.8 0.7 hidden_gradient.5
  133.6 6.1 %collective-permute-done.31.refs_3_ = bf16[384,768]{1,0:T(8,128)(2,1)S(1)} collective-permute-done((bf16[384,768]{1,0:T(8,128)(2,1)S(1)}, bf16[384,768]{1,0:T(8,128)(2,1)S(1)}, u32[]{:S(2)}, u32[]{:S(2)}) %collective-permute-start.31) | collective-permute-done | bytes 589856 | tf_op jit(solution)/shard_map/ppermute | solution.py:440
  139.7 0.7 hidden_gradient.6
  140.5 0.7 copy-done.18
  141.1 4.3 %up_gradient.8 = (bf16[1536,6144]{1,0:T(8,128)(2,1)}, f32[8,128]{1,0:T(8,128)S(1)}) custom-call(s32[1]{0:T(128)} %bitcast.refs_0_.half, s32[12,48]{1,0:T(8,128)S(1)} %copy-done.16, bf16[1536,512]{1,0:T(8,128)(2,1)S(1)} %copy-done.18, bf16[512,768]{1,0:T(8,128)(2,1)S(1)} %get-tuple-element.206.refs_1_, bf16[512,768]{1,0:T(8,128)(2,1)S(1)} %collective-permute-done.35.refs_2_, ...), custom_call_target="tpu_custom_call" | custom-call | flops 10000000000 | tf_op jit(solution)/shard_map/up_gradient/pallas_call | solution.py:403
  145.4 4.3 %up_gradient.9 = (bf16[1536,6144]{1,0:T(8,128)(2,1)}, f32[8,128]{1,0:T(8,128)S(1)}) custom-call(s32[1]{0:T(128)} %bitcast.refs_0_.half, s32[12,48]{1,0:T(8,128)S(1)} %copy-done.16, bf16[1536,512]{1,0:T(8,128)(2,1)S(1)} %copy-done.18, bf16[512,768]{1,0:T(8,128)(2,1)S(1)} %get-tuple-element.205.refs_1_, ...), custom_call_target="tpu_custom_call", output_to_operand_aliasing={{0}: (5, {})} | custom-call | flops 10000000000 | tf_op jit(solution)/shard_map/up_gradient/pallas_call | solution.py:403
  149.7 2.6 %collective-permute-done.30.refs_3_ = bf16[384,768]{1,0:T(8,128)(2,1)S(1)} collective-permute-done((bf16[384,768]{1,0:T(8,128)(2,1)S(1)}, bf16[384,768]{1,0:T(8,128)(2,1)S(1)}, u32[]{:S(2)}, u32[]{:S(2)}) %collective-permute-start.30) | collective-permute-done | bytes 589856 | tf_op jit(solution)/shard_map/ppermute | solution.py:440
  152.3 0.6 hidden_gradient.7
  153.1 2.8 %up_gradient.10 = (bf16[1536,6144]{1,0:T(8,128)(2,1)}, f32[8,128]{1,0:T(8,128)S(1)}) custom-call(s32[1]{0:T(128)} %bitcast.refs_0_.half, s32[12,48]{1,0:T(8,128)S(1)} %copy-done.16, bf16[1536,512]{1,0:T(8,128)(2,1)S(1)} %copy-done.18, bf16[512,768]{1,0:T(8,128)(2,1)S(1)} %get-tuple-element.211.refs_1_, ...), custom_call_target="tpu_custom_call", output_to_operand_aliasing={{0}: (4, {})} | custom-call | flops 10000000000 | tf_op jit(solution)/shard_map/up_gradient/pallas_call | solution.py:403
  155.9 2.8 %up_gradient.11 = (bf16[1536,6144]{1,0:T(8,128)(2,1)}, f32[8,128]{1,0:T(8,128)S(1)}) custom-call(s32[1]{0:T(128)S(6)} %sub.3.refs_1_.half, s32[12,48]{1,0:T(8,128)S(1)} %copy-done.16, bf16[1536,512]{1,0:T(8,128)(2,1)S(1)} %copy-done.18, bf16[512,768]{1,0:T(8,128)(2,1)S(1)} %collective-permute-done.36.refs_1_, ...), custom_call_target="tpu_custom_call", output_to_operand_aliasing={{0}: (4, {})} | custom-call | flops 10000000000 | tf_op jit(solution)/shard_map/up_gradient/pallas_call | solution.py:403
  159.5 2.0 %up_gradient.12 = (bf16[1536,6144]{1,0:T(8,128)(2,1)}, f32[8,128]{1,0:T(8,128)S(1)}) custom-call(s32[1]{0:T(128)} %bitcast.refs_0_.half, s32[12,48]{1,0:T(8,128)S(1)} %copy-done.16, bf16[1536,512]{1,0:T(8,128)(2,1)S(1)} %copy-done.18, bf16[512,384]{1,0:T(8,128)(2,1)S(1)} %get-tuple-element.217.refs_1_, ...), custom_call_target="tpu_custom_call", output_to_operand_aliasing={{0}: (4, {})} | custom-call | flops 10000000000 | tf_op jit(solution)/shard_map/up_gradient/pallas_call | solution.py:403
  161.5 2.0 %up_gradient.13 = (bf16[1536,6144]{1,0:T(8,128)(2,1)}, f32[8,128]{1,0:T(8,128)S(1)}) custom-call(s32[1]{0:T(128)S(6)} %sub.3.refs_1_.half, s32[12,48]{1,0:T(8,128)S(1)} %copy-done.16, bf16[1536,512]{1,0:T(8,128)(2,1)S(1)} %copy-done.18, bf16[512,384]{1,0:T(8,128)(2,1)S(1)} %collective-permute-done.37.refs_1_, ...), custom_call_target="tpu_custom_call", output_to_operand_aliasing={{0}: (4, {})} | custom-call | flops 10000000000 | tf_op jit(solution)/shard_map/up_gradient/pallas_call | solution.py:403
  164.4 2.0 %up_gradient.14 = (bf16[1536,6144]{1,0:T(8,128)(2,1)}, f32[8,128]{1,0:T(8,128)S(1)}) custom-call(s32[1]{0:T(128)} %bitcast.refs_0_.half, s32[12,48]{1,0:T(8,128)S(1)} %copy-done.16, bf16[1536,512]{1,0:T(8,128)(2,1)S(1)} %copy-done.18, bf16[512,384]{1,0:T(8,128)(2,1)S(1)} %get-tuple-element.223.refs_1_, ...), custom_call_target="tpu_custom_call", output_to_operand_aliasing={{0}: (4, {})} | custom-call | flops 10000000000 | tf_op jit(solution)/shard_map/up_gradient/pallas_call | solution.py:403
  166.4 2.0 %up_gradient.15 = (bf16[1536,6144]{1,0:T(8,128)(2,1)}, f32[8,128]{1,0:T(8,128)}) custom-call(s32[1]{0:T(128)S(6)} %sub.3.refs_1_.half, s32[12,48]{1,0:T(8,128)S(1)} %copy-done.16, bf16[1536,512]{1,0:T(8,128)(2,1)S(1)} %copy-done.18, bf16[512,384]{1,0:T(8,128)(2,1)S(1)} %collective-permute-done.38.refs_1_, ...), custom_call_target="tpu_custom_call", output_to_operand_aliasing={{0}: (4, {})} | custom-call | flops 10000000000 | tf_op jit(solution)/shard_map/up_gradient/pallas_call | solution.py:403
  (107 shorter events, 10.4 us)
Async XLA Ops:
  0.7 7.6 %copy-start = (bf16[128,1536]{1,0:T(8,128)(2,1)S(1)}, bf16[128,1536]{1,0:T(8,128)(2,1)}, u32[]{:S(2)}) copy-start(bf16[128,1536]{1,0:T(8,128)(2,1)} %refs_0_.22) | copy-start | bytes 1179652
  0.7 7.6 %copy-start.15 = (s32[12,48]{1,0:T(8,128)S(1)}, s32[12,48]{1,0:T(8,128)}, u32[]{:S(2)}) copy-start(s32[12,48]{1,0:T(8,128)} %mask.15) | copy-start | bytes 6916
  3.1 17.8 %collective-permute-start.1 = (bf16[128,1536]{1,0:T(8,128)(2,1)S(1)}, bf16[128,1536]{1,0:T(8,128)(2,1)S(1)}, u32[]{:S(2)}, u32[]{:S(2)}) collective-permute-start(bf16[128,1536]{1,0:T(8,128)(2,1)S(1)} %get-tuple-element.116), channel_id=1, source_target_pairs={{0,12},{4,0},{8,4},{12,8},{1,13},{5,1},{9,5},{13,9},{2,14},{6,2},{... | collective-permute-start | bytes 1179656 | tf_op jit(solution)/shard_map/ppermute | solution.py:428
  8.2 31.0 %collective-permute-start = (bf16[128,1536]{1,0:T(8,128)(2,1)S(1)}, bf16[128,1536]{1,0:T(8,128)(2,1)S(1)}, u32[]{:S(2)}, u32[]{:S(2)}) collective-permute-start(bf16[128,1536]{1,0:T(8,128)(2,1)S(1)} %get-tuple-element.116), channel_id=1, source_target_pairs={{0,4},{4,8},{8,12},{12,0},{1,5},{5,9},{9,13},{13,1},{2,6},{6,10},{... | collective-permute-start | bytes 1179656 | tf_op jit(solution)/shard_map/ppermute | solution.py:428
  8.2 2.8 %collective-permute-start.3 = (bf16[128,768]{1,0:T(8,128)(2,1)S(1)}, bf16[128,768]{1,0:T(8,128)(2,1)S(1)}, u32[]{:S(2)}, u32[]{:S(2)}) collective-permute-start(bf16[128,768]{1,0:T(8,128)(2,1)S(1)} %get-tuple-element.119), channel_id=1, source_target_pairs={{0,1},{1,0},{2,3},{3,2},{4,5},{5,4},{6,7},{7,6},{8,9},{9,8},{10,11... | collective-permute-start | bytes 589832 | tf_op jit(solution)/shard_map/ppermute | solution.py:431
  10.5 7.5 %collective-permute-start.2 = (bf16[128,768]{1,0:T(8,128)(2,1)S(1)}, bf16[128,768]{1,0:T(8,128)(2,1)S(1)}, u32[]{:S(2)}, u32[]{:S(2)}) collective-permute-start(bf16[128,768]{1,0:T(8,128)(2,1)S(1)} %get-tuple-element.118), channel_id=1, source_target_pairs={{0,1},{1,0},{2,3},{3,2},{4,5},{5,4},{6,7},{7,6},{8,9},{9,8},{10,11... | collective-permute-start | bytes 589832 | tf_op jit(solution)/shard_map/ppermute | solution.py:431
  16.4 8.7 %collective-permute-start.5 = (bf16[128,1536]{1,0:T(8,128)(2,1)S(1)}, bf16[128,1536]{1,0:T(8,128)(2,1)S(1)}, u32[]{:S(2)}, u32[]{:S(2)}) collective-permute-start(bf16[128,1536]{1,0:T(8,128)(2,1)S(1)} %get-tuple-element.126), channel_id=1, source_target_pairs={{0,1},{1,0},{2,3},{3,2},{4,5},{5,4},{6,7},{7,6},{8,9},{9,8},{10,11... | collective-permute-start | bytes 1179656 | tf_op jit(solution)/shard_map/ppermute | solution.py:431
  16.5 12.7 %collective-permute-start.6 = (bf16[128,768]{1,0:T(8,128)(2,1)S(1)}, bf16[128,768]{1,0:T(8,128)(2,1)S(1)}, u32[]{:S(2)}, u32[]{:S(2)}) collective-permute-start(bf16[128,768]{1,0:T(8,128)(2,1)S(1)} %get-tuple-element.129.refs_0_), channel_id=1, source_target_pairs={{0,2},{1,3},{2,0},{3,1},{4,6},{5,7},{6,4},{7,5},{8,10},{9,11},{10,... | collective-permute-start | bytes 589832 | tf_op jit(solution)/shard_map/ppermute | solution.py:440
  18.0 2.9 %copy-start.1 = (bf16[128,1536]{1,0:T(8,128)(2,1)S(1)}, bf16[128,1536]{1,0:T(8,128)(2,1)}, u32[]{:S(2)}) copy-start(bf16[128,1536]{1,0:T(8,128)(2,1)} %refs_0_.23) | copy-start | bytes 1179652
  18.0 2.9 %copy-start.14 = (s32[48,12]{0,1:T(8,128)S(1)}, s32[48,12]{0,1:T(8,128)}, u32[]{:S(2)}) copy-start(s32[48,12]{0,1:T(8,128)} %param.11) | copy-start | bytes 6916
  20.4 33.1 %collective-permute-start.14 = (bf16[128,768]{1,0:T(8,128)(2,1)S(1)}, bf16[128,768]{1,0:T(8,128)(2,1)S(1)}, u32[]{:S(2)}, u32[]{:S(2)}) collective-permute-start(bf16[128,768]{1,0:T(8,128)(2,1)S(1)} %get-tuple-element.150.refs_0_), channel_id=1, source_target_pairs={{0,2},{1,3},{2,0},{3,1},{4,6},{5,7},{6,4},{7,5},{8,10},{9,11},{10,... | collective-permute-start | bytes 589832 | tf_op jit(solution)/shard_map/ppermute | solution.py:440
  25.0 8.6 %collective-permute-start.8 = (bf16[128,1536]{1,0:T(8,128)(2,1)S(1)}, bf16[128,1536]{1,0:T(8,128)(2,1)S(1)}, u32[]{:S(2)}, u32[]{:S(2)}) collective-permute-start(bf16[128,1536]{1,0:T(8,128)(2,1)S(1)} %get-tuple-element.131), channel_id=1, source_target_pairs={{0,1},{1,0},{2,3},{3,2},{4,5},{5,4},{6,7},{7,6},{8,9},{9,8},{10,11... | collective-permute-start | bytes 1179656 | tf_op jit(solution)/shard_map/ppermute | solution.py:431
  25.1 20.8 %collective-permute-start.4 = (bf16[128,1536]{1,0:T(8,128)(2,1)S(1)}, bf16[128,1536]{1,0:T(8,128)(2,1)S(1)}, u32[]{:S(2)}, u32[]{:S(2)}) collective-permute-start(bf16[128,1536]{1,0:T(8,128)(2,1)S(1)} %get-tuple-element.125), channel_id=1, source_target_pairs={{0,8},{4,12},{8,0},{12,4},{1,9},{5,13},{9,1},{13,5},{2,10},{6,14},... | collective-permute-start | bytes 1179656 | tf_op jit(solution)/shard_map/ppermute | solution.py:428
  29.2 4.4 %copy-start.10 = (bf16[128,1536]{1,0:T(8,128)(2,1)}, bf16[128,1536]{1,0:T(8,128)(2,1)S(1)}, u32[]{:S(2)}) copy-start(bf16[128,1536]{1,0:T(8,128)(2,1)S(1)} %get-tuple-element.135.refs_0_) | copy-start | bytes 1179652
  33.4 6.4 %collective-permute-start.7 = (bf16[128,1536]{1,0:T(8,128)(2,1)S(1)}, bf16[128,1536]{1,0:T(8,128)(2,1)S(1)}, u32[]{:S(2)}, u32[]{:S(2)}) collective-permute-start(bf16[128,1536]{1,0:T(8,128)(2,1)S(1)} %get-tuple-element.130), channel_id=1, source_target_pairs={{0,1},{1,0},{2,3},{3,2},{4,5},{5,4},{6,7},{7,6},{8,9},{9,8},{10,11... | collective-permute-start | bytes 1179656 | tf_op jit(solution)/shard_map/ppermute | solution.py:431
  33.6 12.3 %collective-permute-start.9 = (bf16[128,1536]{1,0:T(8,128)(2,1)S(1)}, bf16[128,1536]{1,0:T(8,128)(2,1)S(1)}, u32[]{:S(2)}, u32[]{:S(2)}) collective-permute-start(bf16[128,1536]{1,0:T(8,128)(2,1)S(1)} %get-tuple-element.135.refs_0_), channel_id=1, source_target_pairs={{0,2},{1,3},{2,0},{3,1},{4,6},{5,7},{6,4},{7,5},{8,10},{9,11},{10,... | collective-permute-start | bytes 1179656 | tf_op jit(solution)/shard_map/ppermute | solution.py:440
  39.2 4.6 %copy-start.6 = (bf16[128,1536]{1,0:T(8,128)(2,1)}, bf16[128,1536]{1,0:T(8,128)(2,1)S(1)}, u32[]{:S(2)}) copy-start(bf16[128,1536]{1,0:T(8,128)(2,1)S(1)} %get-tuple-element.149.refs_0_) | copy-start | bytes 1179652
  39.2 17.2 %collective-permute-start.13 = (bf16[128,1536]{1,0:T(8,128)(2,1)S(1)}, bf16[128,1536]{1,0:T(8,128)(2,1)S(1)}, u32[]{:S(2)}, u32[]{:S(2)}) collective-permute-start(bf16[128,1536]{1,0:T(8,128)(2,1)S(1)} %get-tuple-element.149.refs_0_), channel_id=1, source_target_pairs={{0,2},{1,3},{2,0},{3,1},{4,6},{5,7},{6,4},{7,5},{8,10},{9,11},{10,... | collective-permute-start | bytes 1179656 | tf_op jit(solution)/shard_map/ppermute | solution.py:440
  43.8 8.0 %copy-start.2 = (bf16[128,1536]{1,0:T(8,128)(2,1)}, bf16[128,1536]{1,0:T(8,128)(2,1)S(1)}, u32[]{:S(2)}) copy-start(bf16[128,1536]{1,0:T(8,128)(2,1)S(1)} %get-tuple-element.137.refs_0_) | copy-start | bytes 1179652
  46.0 0.8 copy-start.12
  46.7 1.1 copy-start.17
  46.7 10.8 %copy-start.19 = (bf16[512,1536]{1,0:T(8,128)(2,1)}, bf16[512,1536]{1,0:T(8,128)(2,1)S(1)}, u32[]{:S(2)}) copy-start(bf16[512,1536]{1,0:T(8,128)(2,1)S(1)} %get-tuple-element.140.refs_0_) | copy-start | bytes 4718596
  48.9 8.6 %collective-permute-start.12 = (bf16[384,768]{1,0:T(8,128)(2,1)S(1)}, bf16[384,768]{1,0:T(8,128)(2,1)S(1)}, u32[]{:S(2)}, u32[]{:S(2)}) collective-permute-start(bf16[384,768]{1,0:T(8,128)(2,1)S(1)} %get-tuple-element.144), channel_id=1, source_target_pairs={{0,1},{1,0},{2,3},{3,2},{4,5},{5,4},{6,7},{7,6},{8,9},{9,8},{10,11... | collective-permute-start | bytes 1769480 | tf_op jit(solution)/shard_map/ppermute | solution.py:431
  51.3 14.1 %collective-permute-start.20 = (bf16[384,1536]{1,0:T(8,128)(2,1)S(1)}, bf16[384,1536]{1,0:T(8,128)(2,1)S(1)}, u32[]{:S(2)}, u32[]{:S(2)}) collective-permute-start(bf16[384,1536]{1,0:T(8,128)(2,1)S(1)} %get-tuple-element.162), channel_id=1, source_target_pairs={{0,1},{1,0},{2,3},{3,2},{4,5},{5,4},{6,7},{7,6},{8,9},{9,8},{10,11... | collective-permute-start | bytes 3538952 | tf_op jit(solution)/shard_map/ppermute | solution.py:431
  51.9 12.0 %collective-permute-start.10 = (bf16[128,1536]{1,0:T(8,128)(2,1)S(1)}, bf16[128,1536]{1,0:T(8,128)(2,1)S(1)}, u32[]{:S(2)}, u32[]{:S(2)}) collective-permute-start(bf16[128,1536]{1,0:T(8,128)(2,1)S(1)} %get-tuple-element.137.refs_0_), channel_id=1, source_target_pairs={{0,2},{1,3},{2,0},{3,1},{4,6},{5,7},{6,4},{7,5},{8,10},{9,11},{10,... | collective-permute-start | bytes 1179656 | tf_op jit(solution)/shard_map/ppermute | solution.py:440
  53.4 24.4 %collective-permute-start.11 = (bf16[128,1536]{1,0:T(8,128)(2,1)S(1)}, bf16[128,1536]{1,0:T(8,128)(2,1)S(1)}, u32[]{:S(2)}, u32[]{:S(2)}) collective-permute-start(bf16[128,1536]{1,0:T(8,128)(2,1)S(1)} %get-tuple-element.139), channel_id=1, source_target_pairs={{0,4},{4,8},{8,12},{12,0},{1,5},{5,9},{9,13},{13,1},{2,6},{6,10},{... | collective-permute-start | bytes 1179656 | tf_op jit(solution)/shard_map/ppermute | solution.py:428
  56.4 1.1 copy-start.8
  57.5 2.1 %collective-permute-start.17 = (bf16[384,768]{1,0:T(8,128)(2,1)S(1)}, bf16[384,768]{1,0:T(8,128)(2,1)S(1)}, u32[]{:S(2)}, u32[]{:S(2)}) collective-permute-start(bf16[384,768]{1,0:T(8,128)(2,1)S(1)} %get-tuple-element.157), channel_id=1, source_target_pairs={{0,1},{1,0},{2,3},{3,2},{4,5},{5,4},{6,7},{7,6},{8,9},{9,8},{10,11... | collective-permute-start | bytes 1769480 | tf_op jit(solution)/shard_map/ppermute | solution.py:431
  58.7 1.7 %copy-start.20 = (bf16[512,1536]{1,0:T(8,128)(2,1)S(1)}, bf16[512,1536]{1,0:T(8,128)(2,1)}, u32[]{:S(2)}) copy-start(bf16[512,1536]{1,0:T(8,128)(2,1)} %copy-done.19) | copy-start | bytes 4718596
  58.7 17.7 %collective-permute-start.19 = (bf16[384,768]{1,0:T(8,128)(2,1)S(1)}, bf16[384,768]{1,0:T(8,128)(2,1)S(1)}, u32[]{:S(2)}, u32[]{:S(2)}) collective-permute-start(bf16[384,768]{1,0:T(8,128)(2,1)S(1)} %get-tuple-element.160.refs_2_), channel_id=1, source_target_pairs={{0,2},{1,3},{2,0},{3,1},{4,6},{5,7},{6,4},{7,5},{8,10},{9,11},{10,... | collective-permute-start | bytes 1769480 | tf_op jit(solution)/shard_map/ppermute | solution.py:440
  59.5 30.8 %collective-permute-start.15 = (bf16[128,1536]{1,0:T(8,128)(2,1)S(1)}, bf16[128,1536]{1,0:T(8,128)(2,1)S(1)}, u32[]{:S(2)}, u32[]{:S(2)}) collective-permute-start(bf16[128,1536]{1,0:T(8,128)(2,1)S(1)} %get-tuple-element.154), channel_id=1, source_target_pairs={{0,12},{4,0},{8,4},{12,8},{1,13},{5,1},{9,5},{13,9},{2,14},{6,2},{... | collective-permute-start | bytes 1179656 | tf_op jit(solution)/shard_map/ppermute | solution.py:428
  63.8 5.3 %copy-start.4 = (bf16[128,1536]{1,0:T(8,128)(2,1)}, bf16[128,1536]{1,0:T(8,128)(2,1)S(1)}, u32[]{:S(2)}) copy-start(bf16[128,1536]{1,0:T(8,128)(2,1)S(1)} %collective-permute-done.10.refs_4_.refs_1_) | copy-start | bytes 1179652
  63.8 27.5 %collective-permute-start.16 = (bf16[128,1536]{1,0:T(8,128)(2,1)S(1)}, bf16[128,1536]{1,0:T(8,128)(2,1)S(1)}, u32[]{:S(2)}, u32[]{:S(2)}) collective-permute-start(bf16[128,1536]{1,0:T(8,128)(2,1)S(1)} %get-tuple-element.155), channel_id=1, source_target_pairs={{0,8},{4,12},{8,0},{12,4},{1,9},{5,13},{9,1},{13,5},{2,10},{6,14},... | collective-permute-start | bytes 1179656 | tf_op jit(solution)/shard_map/ppermute | solution.py:428
  65.4 23.8 %collective-permute-start.18 = (bf16[384,768]{1,0:T(8,128)(2,1)S(1)}, bf16[384,768]{1,0:T(8,128)(2,1)S(1)}, u32[]{:S(2)}, u32[]{:S(2)}) collective-permute-start(bf16[384,768]{1,0:T(8,128)(2,1)S(1)} %get-tuple-element.159.refs_2_), channel_id=1, source_target_pairs={{0,2},{1,3},{2,0},{3,1},{4,6},{5,7},{6,4},{7,5},{8,10},{9,11},{10,... | collective-permute-start | bytes 1769480 | tf_op jit(solution)/shard_map/ppermute | solution.py:440
  77.7 15.4 %collective-permute-start.22 = (bf16[512,768]{1,0:T(8,128)(2,1)S(1)}, bf16[512,768]{1,0:T(8,128)(2,1)S(1)}, u32[]{:S(2)}, u32[]{:S(2)}) collective-permute-start(bf16[512,768]{1,0:T(8,128)(2,1)S(1)} %get-tuple-element.174.refs_1_), channel_id=1, source_target_pairs={{0,1},{1,0},{2,3},{3,2},{4,5},{5,4},{6,7},{7,6},{8,9},{9,8},{10,11... | collective-permute-start | bytes 2359304 | tf_op jit(solution)/shard_map/ppermute | solution.py:431
  77.8 36.6 %collective-permute-start.27 = (bf16[384,1536]{1,0:T(8,128)(2,1)S(1)}, bf16[384,1536]{1,0:T(8,128)(2,1)S(1)}, u32[]{:S(2)}, u32[]{:S(2)}) collective-permute-start(bf16[384,1536]{1,0:T(8,128)(2,1)S(1)} %get-tuple-element.187.refs_2_), channel_id=1, source_target_pairs={{0,2},{1,3},{2,0},{3,1},{4,6},{5,7},{6,4},{7,5},{8,10},{9,11},{10,... | collective-permute-start | bytes 3538952 | tf_op jit(solution)/shard_map/ppermute | solution.py:440
  92.5 5.1 %collective-permute-start.21 = (bf16[384,768]{1,0:T(8,128)(2,1)S(1)}, bf16[384,768]{1,0:T(8,128)(2,1)S(1)}, u32[]{:S(2)}, u32[]{:S(2)}) collective-permute-start(bf16[384,768]{1,0:T(8,128)(2,1)S(1)} %get-tuple-element.173), channel_id=1, source_target_pairs={{0,1},{1,0},{2,3},{3,2},{4,5},{5,4},{6,7},{7,6},{8,9},{9,8},{10,11... | collective-permute-start | bytes 1769480 | tf_op jit(solution)/shard_map/ppermute | solution.py:431
  92.6 8.0 %collective-permute-start.24 = (bf16[512,768]{1,0:T(8,128)(2,1)S(1)}, bf16[512,768]{1,0:T(8,128)(2,1)S(1)}, u32[]{:S(2)}, u32[]{:S(2)}) collective-permute-start(bf16[512,768]{1,0:T(8,128)(2,1)S(1)} %get-tuple-element.179.refs_1_), channel_id=1, source_target_pairs={{0,1},{1,0},{2,3},{3,2},{4,5},{5,4},{6,7},{7,6},{8,9},{9,8},{10,11... | collective-permute-start | bytes 2359304 | tf_op jit(solution)/shard_map/ppermute | solution.py:431
  99.9 5.3 %collective-permute-start.23 = (bf16[384,768]{1,0:T(8,128)(2,1)S(1)}, bf16[384,768]{1,0:T(8,128)(2,1)S(1)}, u32[]{:S(2)}, u32[]{:S(2)}) collective-permute-start(bf16[384,768]{1,0:T(8,128)(2,1)S(1)} %get-tuple-element.178), channel_id=1, source_target_pairs={{0,1},{1,0},{2,3},{3,2},{4,5},{5,4},{6,7},{7,6},{8,9},{9,8},{10,11... | collective-permute-start | bytes 1769480 | tf_op jit(solution)/shard_map/ppermute | solution.py:431
  100.0 32.8 %collective-permute-start.32 = (bf16[384,768]{1,0:T(8,128)(2,1)S(1)}, bf16[384,768]{1,0:T(8,128)(2,1)S(1)}, u32[]{:S(2)}, u32[]{:S(2)}) collective-permute-start(bf16[384,768]{1,0:T(8,128)(2,1)S(1)} %get-tuple-element.198.refs_2_), channel_id=1, source_target_pairs={{0,2},{1,3},{2,0},{3,1},{4,6},{5,7},{6,4},{7,5},{8,10},{9,11},{10,... | collective-permute-start | bytes 1769480 | tf_op jit(solution)/shard_map/ppermute | solution.py:440
  107.4 11.6 %collective-permute-start.26 = (bf16[384,768]{1,0:T(8,128)(2,1)S(1)}, bf16[384,768]{1,0:T(8,128)(2,1)S(1)}, u32[]{:S(2)}, u32[]{:S(2)}) collective-permute-start(bf16[384,768]{1,0:T(8,128)(2,1)S(1)} %get-tuple-element.186), channel_id=1, source_target_pairs={{0,1},{1,0},{2,3},{3,2},{4,5},{5,4},{6,7},{7,6},{8,9},{9,8},{10,11... | collective-permute-start | bytes 1769480 | tf_op jit(solution)/shard_map/ppermute | solution.py:431
  107.6 6.8 %copy-start.11 = (bf16[128,1536]{1,0:T(8,128)(2,1)S(1)}, bf16[128,1536]{1,0:T(8,128)(2,1)}, u32[]{:S(2)}) copy-start(bf16[128,1536]{1,0:T(8,128)(2,1)} %copy-done.10) | copy-start | bytes 1179652
  107.6 6.8 %copy-start.13 = (bf16[128,1536]{1,0:T(8,128)(2,1)S(1)}, bf16[128,1536]{1,0:T(8,128)(2,1)}, u32[]{:S(2)}) copy-start(bf16[128,1536]{1,0:T(8,128)(2,1)} %copy-done.12) | copy-start | bytes 1179652
  116.8 7.5 %collective-permute-start.33 = (bf16[512,1536]{1,0:T(8,128)(2,1)S(1)}, bf16[512,1536]{1,0:T(8,128)(2,1)S(1)}, u32[]{:S(2)}, u32[]{:S(2)}) collective-permute-start(bf16[512,1536]{1,0:T(8,128)(2,1)S(1)} %get-tuple-element.200.refs_1_), channel_id=1, source_target_pairs={{0,1},{1,0},{2,3},{3,2},{4,5},{5,4},{6,7},{7,6},{8,9},{9,8},{10,11... | collective-permute-start | bytes 4718600 | tf_op jit(solution)/shard_map/ppermute | solution.py:431
  116.9 4.2 %collective-permute-start.25 = (bf16[384,768]{1,0:T(8,128)(2,1)S(1)}, bf16[384,768]{1,0:T(8,128)(2,1)S(1)}, u32[]{:S(2)}, u32[]{:S(2)}) collective-permute-start(bf16[384,768]{1,0:T(8,128)(2,1)S(1)} %get-tuple-element.185), channel_id=1, source_target_pairs={{0,1},{1,0},{2,3},{3,2},{4,5},{5,4},{6,7},{7,6},{8,9},{9,8},{10,11... | collective-permute-start | bytes 1769480 | tf_op jit(solution)/shard_map/ppermute | solution.py:431
  117.4 22.3 %collective-permute-start.31 = (bf16[384,768]{1,0:T(8,128)(2,1)S(1)}, bf16[384,768]{1,0:T(8,128)(2,1)S(1)}, u32[]{:S(2)}, u32[]{:S(2)}) collective-permute-start(bf16[384,768]{1,0:T(8,128)(2,1)S(1)} %get-tuple-element.196.refs_2_), channel_id=1, source_target_pairs={{0,2},{1,3},{2,0},{3,1},{4,6},{5,7},{6,4},{7,5},{8,10},{9,11},{10,... | collective-permute-start | bytes 1769480 | tf_op jit(solution)/shard_map/ppermute | solution.py:440
  120.0 32.3 %collective-permute-start.30 = (bf16[384,768]{1,0:T(8,128)(2,1)S(1)}, bf16[384,768]{1,0:T(8,128)(2,1)S(1)}, u32[]{:S(2)}, u32[]{:S(2)}) collective-permute-start(bf16[384,768]{1,0:T(8,128)(2,1)S(1)} %get-tuple-element.195.refs_2_), channel_id=1, source_target_pairs={{0,2},{1,3},{2,0},{3,1},{4,6},{5,7},{6,4},{7,5},{8,10},{9,11},{10,... | collective-permute-start | bytes 1769480 | tf_op jit(solution)/shard_map/ppermute | solution.py:440
  121.9 36.8 %collective-permute-start.29 = (bf16[384,384]{1,0:T(8,128)(2,1)S(1)}, bf16[384,384]{1,0:T(8,128)(2,1)S(1)}, u32[]{:S(2)}, u32[]{:S(2)}) collective-permute-start(bf16[384,384]{1,0:T(8,128)(2,1)S(1)} %get-tuple-element.194.refs_2_), channel_id=1, source_target_pairs={{0,2},{1,3},{2,0},{3,1},{4,6},{5,7},{6,4},{7,5},{8,10},{9,11},{10,... | collective-permute-start | bytes 884744 | tf_op jit(solution)/shard_map/ppermute | solution.py:440
  124.3 39.8 %collective-permute-start.28 = (bf16[384,384]{1,0:T(8,128)(2,1)S(1)}, bf16[384,384]{1,0:T(8,128)(2,1)S(1)}, u32[]{:S(2)}, u32[]{:S(2)}) collective-permute-start(bf16[384,384]{1,0:T(8,128)(2,1)S(1)} %get-tuple-element.192.refs_2_), channel_id=1, source_target_pairs={{0,2},{1,3},{2,0},{3,1},{4,6},{5,7},{6,4},{7,5},{8,10},{9,11},{10,... | collective-permute-start | bytes 884744 | tf_op jit(solution)/shard_map/ppermute | solution.py:440
  124.9 7.9 %copy-start.7 = (bf16[128,1536]{1,0:T(8,128)(2,1)S(1)}, bf16[128,1536]{1,0:T(8,128)(2,1)}, u32[]{:S(2)}) copy-start(bf16[128,1536]{1,0:T(8,128)(2,1)} %copy-done.6) | copy-start | bytes 1179652
  124.9 8.0 %copy-start.9 = (bf16[128,1536]{1,0:T(8,128)(2,1)S(1)}, bf16[128,1536]{1,0:T(8,128)(2,1)}, u32[]{:S(2)}) copy-start(bf16[128,1536]{1,0:T(8,128)(2,1)} %copy-done.8) | copy-start | bytes 1179652
  133.5 6.9 %collective-permute-start.35 = (bf16[512,768]{1,0:T(8,128)(2,1)S(1)}, bf16[512,768]{1,0:T(8,128)(2,1)S(1)}, u32[]{:S(2)}, u32[]{:S(2)}) collective-permute-start(bf16[512,768]{1,0:T(8,128)(2,1)S(1)} %get-tuple-element.206.refs_1_), channel_id=1, source_target_pairs={{0,1},{1,0},{2,3},{3,2},{4,5},{5,4},{6,7},{7,6},{8,9},{9,8},{10,11... | collective-permute-start | bytes 2359304 | tf_op jit(solution)/shard_map/ppermute | solution.py:431
  139.7 0.8 copy-start.16
  139.7 1.4 copy-start.18
  140.4 5.1 %collective-permute-start.34 = (bf16[512,768]{1,0:T(8,128)(2,1)S(1)}, bf16[512,768]{1,0:T(8,128)(2,1)S(1)}, u32[]{:S(2)}, u32[]{:S(2)}) collective-permute-start(bf16[512,768]{1,0:T(8,128)(2,1)S(1)} %get-tuple-element.205.refs_1_), channel_id=1, source_target_pairs={{0,1},{1,0},{2,3},{3,2},{4,5},{5,4},{6,7},{7,6},{8,9},{9,8},{10,11... | collective-permute-start | bytes 2359304 | tf_op jit(solution)/shard_map/ppermute | solution.py:431
  145.4 6.9 %copy-start.3 = (bf16[128,1536]{1,0:T(8,128)(2,1)S(1)}, bf16[128,1536]{1,0:T(8,128)(2,1)}, u32[]{:S(2)}) copy-start(bf16[128,1536]{1,0:T(8,128)(2,1)} %copy-done.2) | copy-start | bytes 1179652
  145.4 6.9 %copy-start.5 = (bf16[128,1536]{1,0:T(8,128)(2,1)S(1)}, bf16[128,1536]{1,0:T(8,128)(2,1)}, u32[]{:S(2)}) copy-start(bf16[128,1536]{1,0:T(8,128)(2,1)} %copy-done.4) | copy-start | bytes 1179652
  153.0 2.9 %collective-permute-start.36 = (bf16[512,768]{1,0:T(8,128)(2,1)S(1)}, bf16[512,768]{1,0:T(8,128)(2,1)S(1)}, u32[]{:S(2)}, u32[]{:S(2)}) collective-permute-start(bf16[512,768]{1,0:T(8,128)(2,1)S(1)} %get-tuple-element.211.refs_1_), channel_id=1, source_target_pairs={{0,1},{1,0},{2,3},{3,2},{4,5},{5,4},{6,7},{7,6},{8,9},{9,8},{10,11... | collective-permute-start | bytes 2359304 | tf_op jit(solution)/shard_map/ppermute | solution.py:431
  159.0 2.6 %collective-permute-start.37 = (bf16[512,384]{1,0:T(8,128)(2,1)S(1)}, bf16[512,384]{1,0:T(8,128)(2,1)S(1)}, u32[]{:S(2)}, u32[]{:S(2)}) collective-permute-start(bf16[512,384]{1,0:T(8,128)(2,1)S(1)} %get-tuple-element.217.refs_1_), channel_id=1, source_target_pairs={{0,1},{1,0},{2,3},{3,2},{4,5},{5,4},{6,7},{7,6},{8,9},{9,8},{10,11... | collective-permute-start | bytes 1179656 | tf_op jit(solution)/shard_map/ppermute | solution.py:431
  164.3 2.1 %collective-permute-start.38 = (bf16[512,384]{1,0:T(8,128)(2,1)S(1)}, bf16[512,384]{1,0:T(8,128)(2,1)S(1)}, u32[]{:S(2)}, u32[]{:S(2)}) collective-permute-start(bf16[512,384]{1,0:T(8,128)(2,1)S(1)} %get-tuple-element.223.refs_1_), channel_id=1, source_target_pairs={{0,1},{1,0},{2,3},{3,2},{4,5},{5,4},{6,7},{7,6},{8,9},{9,8},{10,11... | collective-permute-start | bytes 1179656 | tf_op jit(solution)/shard_map/ppermute | solution.py:431

commit v2 on v1

--- a/solution.py
+++ b/solution.py
@@ -24,7 +24,7 @@
 
 CUTS = {
     "h0": (2, 2, 4),
-    "h0s": (2, 2, 4),
+    "h0s": (4, 4),
     "g0": (4, 4),
     "g0s": (4, 4),
     "h1": (2, 2, 4),
@@ -38,27 +38,27 @@
 ORDER = [
     ("send", "h0s", 0),
     ("turn", "x", 0),
-    ("turn", "x", 1),
     ("send", "h0s", 1),
     ("add", "h0", 0),
     ("send", "h0s", 2),
+    ("turn", "x", 1),
     ("add", "h0", 1),
-    ("send", "g0s", 0, ("x", 1)),
+    ("send", "g0s", 0),
     ("turn", "x", 2),
     ("add", "h0", 2),
     ("send", "g0s", 1, ("h0", 0)),
     ("add", "g0", 0),
     ("add", "g0", 1, ("x", 0)),
-    ("stack", "x", 0, ("h0", 2)),
-    ("turn", "c", 0),
+    ("turn", "c", 0, ("h0", 2)),
+    ("stack", "x", 0),
     ("send", "h1s", 0),
     ("send", "h1s", 2),
     ("send", "h1s", 1, ("g0", 0), ("h0", 1)),
     ("add", "h1", 0),
+    ("add", "h1", 1),
+    ("turn", "c", 1),
+    ("add", "h1", 2, ("g0", 1)),
     ("turn", "c", 2),
-    ("turn", "c", 1),
-    ("add", "h1", 1),
-    ("add", "h1", 2, ("g0", 1)),
     ("act", "a", 0),
     ("act", "a", 1, ("c", 0)),
     ("stack", "c", 0),
@@ -489,11 +489,15 @@
 
     def run(action, name, at):
         if action == "turn":
-            if turns[at]:
-                source = shards["echo"] if name == "x" and at < 2 else step(late, shards[name])
+            moves[name, at] = []
+            if turns[at] and at < 2:
+                source = shards["echo"] if name == "x" else step(late, shards[name])
                 moves[name, at] = [turn(source, by) for by in turns[at]]
-            else:
-                moves[name, at] = []
+            elif turns[at]:
+                source = step(late, moves[name, 0][0])
+                for _ in turns[at]:
+                    source = turn(source, 1)
+                    moves[name, at].append(source)
             return
         if action == "stack":
             pieces = [shards[name], *(piece for i in range(3) for piece in moves[name, i])]

time: 169 us -> 167 us (0.988)
  waiting for transfers between devices: 38.2 us -> 31.5 us
  local copies, waits for them, and re-layouts: 2.08 us -> 5.22 us
  starting transfers between devices: 29.9 us -> 32.2 us
  Pallas kernels: 97 us -> 95.3 us
    ppermute x13, waiting for transfers between devices: 34.4 us -> 30.9 us  [chip_swap(): lax.ppermute(value, 'col', [(i, i ^ CORES * hop) for i in range(n_col)])]
    unnamed x42 -> x46, local copies, waits for them, and re-layouts: 2.08 us -> 5.22 us
    ppermute x6, waiting for transfers between devices: 3.07 us -> 0.02 us  [turn(): lax.ppermute(value, 'row', [(i, (i + by) % n_row) for i in range(n_row)])]
    pallas_call x25 -> x24, Pallas kernels: 49.7 us -> 48.1 us  [project(): pl.pallas_call(functools.partial(project_kernel, opening, fresh, down, bo...]
    ppermute x20 -> x19, starting transfers between devices: 4.09 us -> 3.75 us  [core_swap(): return lax.ppermute(value, 'col', [(i, i ^ 1) for i in range(n_col)])]
  transfers between devices with their start and end apart: 39 -> 38, of which waited for: 11 -> 7; matrix products, arithmetic and copies ran while one was open for 0% -> 0% of each run, Pallas kernels for 55% -> 54%
where the time goes in v2:
time: 167 us; the launch traced here: 166 us
  Pallas kernels  95.3 us (57%)
  starting transfers between devices  32.2 us (19%)
  waiting for transfers between devices  31.5 us (19%)
  local copies, waits for them, and re-layouts  5.22 us (3%)
    pallas_call x24, Pallas kernels, project(): pl.pallas_call(functools.partial(project_kernel, opening, fresh, down, bo...  48.1 us
    pallas_call x11, Pallas kernels, gradient(): pl.pallas_call(functools.partial(gradient_kernel, down, parts, span, star...  39.4 us
    ppermute x13, waiting for transfers between devices, chip_swap(): lax.ppermute(value, 'col', [(i, i ^ CORES * hop) for i in range(n_col)])  30.9 us
    ppermute x13, starting transfers between devices, chip_swap(): lax.ppermute(value, 'col', [(i, i ^ CORES * hop) for i in range(n_col)])  15.4 us
    ppermute x6, starting transfers between devices, turn(): lax.ppermute(value, 'row', [(i, (i + by) % n_row) for i in range(n_row)])  13.1 us
    pallas_call x8, Pallas kernels, pointwise(): pl.pallas_call(functools.partial(kernel, len(pairs)), out_shape=shapes, g...  7.19 us
    unnamed x46, local copies, waits for them, and re-layouts  5.22 us
    ppermute x19, starting transfers between devices, core_swap(): return lax.ppermute(value, 'col', [(i, i ^ 1) for i in range(n_col)])  3.75 us
  transfers between devices with their start and end apart: 38, of which 7 were waited for; matrix products, arithmetic and copies ran while one was open for 0% of the time, Pallas kernels for 54%

profile of v2, /device:TPU:0, one launch (start us, length us, event | category | flops | bytes accessed | tf_op | source)
XLA Modules:
  0.0 165.6 jit_solution(14512403618743772108)
XLA Ops:
  0.7 3.2 %project_up.11 = (bf16[128,1536]{1,0:T(8,128)(2,1)S(1)}, bf16[1536,1536]{1,0:T(8,128)(2,1)S(1)}, bf16[128,1536]{1,0:T(8,128)(2,1)S(1)}, f32[8,128]{1,0:T(8,128)S(1)}) custom-call(s32[1]{0:T(128)S(6)} %sub.3.refs_1_.half, bf16[128,1536]{1,0:T(8,128)(2,1)} %refs_0_.20, bf16[1536,6144]{1,0:T(8,128)(2,1)} %refs_1_.14, s32[12,48]{1,0:T(8,128)} %mask.15, ...), custom_call_target="tpu_custom_call" | custom-call | flops 10000000000 | tf_op jit(solution)/shard_map/project_up/pallas_call | solution.py:210
  3.9 3.1 %collective-permute-start = (bf16[128,1536]{1,0:T(8,128)(2,1)S(1)}, bf16[128,1536]{1,0:T(8,128)(2,1)S(1)}, u32[]{:S(2)}, u32[]{:S(2)}) collective-permute-start(bf16[128,1536]{1,0:T(8,128)(2,1)S(1)} %get-tuple-element.113), channel_id=1, source_target_pairs={{0,4},{4,8},{8,12},{12,0},{1,5},{5,9},{9,13},{13,1},{2,6},{6,10},{... | collective-permute-start | bytes 1179656 | tf_op jit(solution)/shard_map/ppermute | solution.py:428
  7.0 2.1 %collective-permute-start.1 = (bf16[128,1536]{1,0:T(8,128)(2,1)S(1)}, bf16[128,1536]{1,0:T(8,128)(2,1)S(1)}, u32[]{:S(2)}, u32[]{:S(2)}) collective-permute-start(bf16[128,1536]{1,0:T(8,128)(2,1)S(1)} %get-tuple-element.113), channel_id=1, source_target_pairs={{0,12},{4,0},{8,4},{12,8},{1,13},{5,1},{9,5},{13,9},{2,14},{6,2},{... | collective-permute-start | bytes 1179656 | tf_op jit(solution)/shard_map/ppermute | solution.py:428
  9.1 3.0 %project_up.12 = (bf16[128,1536]{1,0:T(8,128)(2,1)S(1)}, bf16[1536,1536]{1,0:T(8,128)(2,1)S(1)}, f32[8,128]{1,0:T(8,128)S(1)}) custom-call(s32[1]{0:T(128)S(6)} %sub.3.refs_1_.half, bf16[128,1536]{1,0:T(8,128)(2,1)S(1)} %copy-done, bf16[1536,6144]{1,0:T(8,128)(2,1)} %refs_1_.14, s32[12,48]{1,0:T(8,128)S(1)} %copy-done.15, ...), custom_call_target="tpu_custom_call" | custom-call | flops 10000000000 | tf_op jit(solution)/shard_map/project_up/pallas_call | solution.py:210
  12.6 2.2 %project_up.13 = (bf16[128,768]{1,0:T(8,128)(2,1)S(1)}, bf16[1536,768]{1,0:T(8,128)(2,1)S(1)}, f32[8,128]{1,0:T(8,128)S(1)}) custom-call(s32[1]{0:T(128)} %bitcast.refs_0_.half, bf16[128,1536]{1,0:T(8,128)(2,1)S(1)} %copy-done, bf16[1536,6144]{1,0:T(8,128)(2,1)} %refs_1_.14, s32[12,48]{1,0:T(8,128)S(1)} %copy-done.15, ...), custom_call_target="tpu_custom_call" | custom-call | flops 10000000000 | tf_op jit(solution)/shard_map/project_up/pallas_call | solution.py:210
  14.9 1.4 copy-done.17
  16.3 1.7 %collective-permute-start.5 = (bf16[128,768]{1,0:T(8,128)(2,1)S(1)}, bf16[128,768]{1,0:T(8,128)(2,1)S(1)}, u32[]{:S(2)}, u32[]{:S(2)}) collective-permute-start(bf16[128,768]{1,0:T(8,128)(2,1)S(1)} %get-tuple-element.124.refs_0_), channel_id=1, source_target_pairs={{0,2},{1,3},{2,0},{3,1},{4,6},{5,7},{6,4},{7,5},{8,10},{9,11},{10,... | collective-permute-start | bytes 589832 | tf_op jit(solution)/shard_map/ppermute | solution.py:440
  18.0 2.3 %project_up.14 = (bf16[128,768]{1,0:T(8,128)(2,1)S(1)}, bf16[1536,768]{1,0:T(8,128)(2,1)S(1)}, f32[8,128]{1,0:T(8,128)S(1)}) custom-call(s32[1]{0:T(128)} %bitcast.refs_0_.half, bf16[128,1536]{1,0:T(8,128)(2,1)S(1)} %copy-done, bf16[1536,6144]{1,0:T(8,128)(2,1)} %refs_1_.14, s32[12,48]{1,0:T(8,128)S(1)} %copy-done.15, ...), custom_call_target="tpu_custom_call" | custom-call | flops 10000000000 | tf_op jit(solution)/shard_map/project_up/pallas_call | solution.py:210
  20.3 4.0 %project_down.13 = (bf16[128,1536]{1,0:T(8,128)(2,1)S(1)}, bf16[1536,1536]{1,0:T(8,128)(2,1)S(1)}, f32[8,128]{1,0:T(8,128)S(1)}) custom-call(s32[1]{0:T(128)S(6)} %sub.3.refs_1_.half, bf16[128,1536]{1,0:T(8,128)(2,1)S(1)} %copy-done.1, bf16[6144,1536]{1,0:T(8,128)(2,1)} %refs_1_.17, s32[12,48]{1,0:T(8,128)S(1)} %bitcast.2, ...), custom_call_target="tpu_custom_call" | custom-call | flops 10000000000 | tf_op jit(solution)/shard_map/project_down/pallas_call | solution.py:210
  24.5 3.0 %project_up.15 = (bf16[128,1536]{1,0:T(8,128)(2,1)S(1)}, bf16[1536,1536]{1,0:T(8,128)(2,1)S(1)}, f32[8,128]{1,0:T(8,128)S(1)}) custom-call(s32[1]{0:T(128)} %bitcast.refs_0_.half, bf16[128,1536]{1,0:T(8,128)(2,1)S(1)} %copy-done, bf16[1536,6144]{1,0:T(8,128)(2,1)} %refs_1_.14, s32[12,48]{1,0:T(8,128)S(1)} %copy-done.15, ...), custom_call_target="tpu_custom_call" | custom-call | flops 10000000000 | tf_op jit(solution)/shard_map/project_up/pallas_call | solution.py:210
  27.9 1.7 %collective-permute-start.12 = (bf16[128,768]{1,0:T(8,128)(2,1)S(1)}, bf16[128,768]{1,0:T(8,128)(2,1)S(1)}, u32[]{:S(2)}, u32[]{:S(2)}) collective-permute-start(bf16[128,768]{1,0:T(8,128)(2,1)S(1)} %get-tuple-element.143.refs_0_), channel_id=1, source_target_pairs={{0,2},{1,3},{2,0},{3,1},{4,6},{5,7},{6,4},{7,5},{8,10},{9,11},{10,... | collective-permute-start | bytes 589832 | tf_op jit(solution)/shard_map/ppermute | solution.py:440
  29.6 4.0 %project_down.14 = (bf16[128,1536]{1,0:T(8,128)(2,1)S(1)}, bf16[1536,1536]{1,0:T(8,128)(2,1)S(1)}, f32[8,128]{1,0:T(8,128)S(1)}) custom-call(s32[1]{0:T(128)S(6)} %sub.3.refs_1_.half, bf16[128,1536]{1,0:T(8,128)(2,1)S(1)} %copy-done.1, bf16[6144,1536]{1,0:T(8,128)(2,1)} %refs_1_.17, s32[12,48]{1,0:T(8,128)S(1)} %bitcast.3, ...), custom_call_target="tpu_custom_call" | custom-call | flops 10000000000 | tf_op jit(solution)/shard_map/project_down/pallas_call | solution.py:210
  33.7 4.0 %project_down.15 = (bf16[128,1536]{1,0:T(8,128)(2,1)S(1)}, bf16[1536,1536]{1,0:T(8,128)(2,1)S(1)}, f32[8,128]{1,0:T(8,128)S(1)}) custom-call(s32[1]{0:T(128)} %bitcast.refs_0_.half, bf16[128,1536]{1,0:T(8,128)(2,1)S(1)} %copy-done.1, bf16[6144,1536]{1,0:T(8,128)(2,1)} %refs_1_.17, s32[12,48]{1,0:T(8,128)S(1)} %bitcast.4, ...), custom_call_target="tpu_custom_call" | custom-call | flops 10000000000 | tf_op jit(solution)/shard_map/project_down/pallas_call | solution.py:210
  38.2 4.0 %project_down.16 = (bf16[128,1536]{1,0:T(8,128)(2,1)S(1)}, bf16[1536,1536]{1,0:T(8,128)(2,1)S(1)}, f32[8,128]{1,0:T(8,128)S(1)}) custom-call(s32[1]{0:T(128)} %bitcast.refs_0_.half, bf16[128,1536]{1,0:T(8,128)(2,1)S(1)} %copy-done.1, bf16[6144,1536]{1,0:T(8,128)(2,1)} %refs_1_.17, s32[12,48]{1,0:T(8,128)S(1)} %bitcast.5, ...), custom_call_target="tpu_custom_call" | custom-call | flops 10000000000 | tf_op jit(solution)/shard_map/project_down/pallas_call | solution.py:210
  42.3 0.8 copy-done.12
  43.7 1.1 project_up.16
  45.3 2.3 %project_up.17 = (bf16[384,1536]{1,0:T(8,128)(2,1)S(1)}, f32[8,128]{1,0:T(8,128)S(1)}) custom-call(s32[1]{0:T(128)S(6)} %sub.3.refs_1_.half, bf16[512,1536]{1,0:T(8,128)(2,1)S(1)} %get-tuple-element.135.refs_0_, bf16[1536,1536]{1,0:T(8,128)(2,1)S(1)} %get-tuple-element.138.refs_1_, f32[8,128]{1,0:T(8,128)S(1)} %get-tuple-element.140.refs_2_), custom_call_target="tpu_custom_call" | custom-call | flops 10000000000 | tf_op jit(solution)/shard_map/project_up/pallas_call | solution.py:210
  47.9 1.7 %collective-permute-start.9 = (bf16[128,1536]{1,0:T(8,128)(2,1)S(1)}, bf16[128,1536]{1,0:T(8,128)(2,1)S(1)}, u32[]{:S(2)}, u32[]{:S(2)}) collective-permute-start(bf16[128,1536]{1,0:T(8,128)(2,1)S(1)} %get-tuple-element.133.refs_0_), channel_id=1, source_target_pairs={{0,2},{1,3},{2,0},{3,1},{4,6},{5,7},{6,4},{7,5},{8,10},{9,11},{10,... | collective-permute-start | bytes 1179656 | tf_op jit(solution)/shard_map/ppermute | solution.py:440
  49.5 3.4 %collective-permute-start.10 = (bf16[128,1536]{1,0:T(8,128)(2,1)S(1)}, bf16[128,1536]{1,0:T(8,128)(2,1)S(1)}, u32[]{:S(2)}, u32[]{:S(2)}) collective-permute-start(bf16[128,1536]{1,0:T(8,128)(2,1)S(1)} %get-tuple-element.134), channel_id=1, source_target_pairs={{0,4},{4,8},{8,12},{12,0},{1,5},{5,9},{9,13},{13,1},{2,6},{6,10},{... | collective-permute-start | bytes 1179656 | tf_op jit(solution)/shard_map/ppermute | solution.py:428
  52.9 1.5 copy-done.22
  54.5 1.1 project_up.18
  56.2 1.1 project_up.19
  57.2 1.6 collective-permute-start.19
  58.8 1.1 project_up.20
  60.5 4.3 %collective-permute-start.15 = (bf16[128,1536]{1,0:T(8,128)(2,1)S(1)}, bf16[128,1536]{1,0:T(8,128)(2,1)S(1)}, u32[]{:S(2)}, u32[]{:S(2)}) collective-permute-start(bf16[128,1536]{1,0:T(8,128)(2,1)S(1)} %get-tuple-element.150), channel_id=1, source_target_pairs={{0,12},{4,0},{8,4},{12,8},{1,13},{5,1},{9,5},{13,9},{2,14},{6,2},{... | collective-permute-start | bytes 1179656 | tf_op jit(solution)/shard_map/ppermute | solution.py:428
  64.8 2.3 %project_up.21 = (bf16[384,1536]{1,0:T(8,128)(2,1)S(1)}, f32[8,128]{1,0:T(8,128)S(1)}) custom-call(s32[1]{0:T(128)} %bitcast.refs_0_.half, bf16[512,1536]{1,0:T(8,128)(2,1)S(1)} %copy-done.22, bf16[1536,1536]{1,0:T(8,128)(2,1)S(1)} %get-tuple-element.151.refs_1_, bf16[384,1536]{1,0:T(8,128)(2,1)S(1)} %collective-permute-done.16.refs_2_, ...), custom_call_target="tpu_custom_call" | custom-call | flops 10000000000 | tf_op jit(solution)/shard_map/project_up/pallas_call | solution.py:210
  67.4 6.1 %collective-permute-done.19.refs_3_ = bf16[384,768]{1,0:T(8,128)(2,1)S(1)} collective-permute-done((bf16[384,768]{1,0:T(8,128)(2,1)S(1)}, bf16[384,768]{1,0:T(8,128)(2,1)S(1)}, u32[]{:S(2)}, u32[]{:S(2)}) %collective-permute-start.19) | collective-permute-done | bytes 589856 | tf_op jit(solution)/shard_map/ppermute | solution.py:440
  73.5 1.2 activation.3
  74.8 1.6 collective-permute-start.26
  76.4 9.8 %collective-permute-done.18.refs_3_ = bf16[384,768]{1,0:T(8,128)(2,1)S(1)} collective-permute-done((bf16[384,768]{1,0:T(8,128)(2,1)S(1)}, bf16[384,768]{1,0:T(8,128)(2,1)S(1)}, u32[]{:S(2)}, u32[]{:S(2)}) %collective-permute-start.18) | collective-permute-done | bytes 589856 | tf_op jit(solution)/shard_map/ppermute | solution.py:440
  86.1 1.2 activation.4
  87.6 1.1 project_down.17
  89.2 4.5 %down_gradient.3 = (bf16[6144,1536]{1,0:T(8,128)(2,1)}, f32[8,128]{1,0:T(8,128)S(1)}) custom-call(s32[1]{0:T(128)} %bitcast.refs_0_.half, s32[12,48]{1,0:T(8,128)S(1)} %bitcast.6, bf16[512,1536]{1,0:T(8,128)(2,1)S(1)} %get-tuple-element.161.refs_0_, bf16[512,768]{1,0:T(8,128)(2,1)S(1)} %get-tuple-element.168.refs_1_, ...), custom_call_target="tpu_custom_call" | custom-call | flops 10000000000 | tf_op jit(solution)/shard_map/down_gradient/pallas_call | solution.py:403
  93.8 1.1 project_down.18
  94.9 1.1 project_down.19
  96.1 1.6 collective-permute-start.31
  97.7 4.5 %down_gradient.4 = (bf16[6144,1536]{1,0:T(8,128)(2,1)}, f32[8,128]{1,0:T(8,128)S(1)}) custom-call(s32[1]{0:T(128)} %bitcast.refs_0_.half, s32[12,48]{1,0:T(8,128)S(1)} %bitcast.7, bf16[512,1536]{1,0:T(8,128)(2,1)S(1)} %get-tuple-element.161.refs_0_, bf16[512,768]{1,0:T(8,128)(2,1)S(1)} %get-tuple-element.173.refs_1_, ...), custom_call_target="tpu_custom_call", output_to_operand_aliasing={{0}: (5, {})} | custom-call | flops 10000000000 | tf_op jit(solution)/shard_map/down_gradient/pallas_call | solution.py:403
  102.2 1.1 project_down.20
  103.3 1.1 project_down.21
  104.6 1.1 project_down.22
  105.7 5.7 %collective-permute-done.26.refs_3_ = bf16[384,1536]{1,0:T(8,128)(2,1)S(1)} collective-permute-done((bf16[384,1536]{1,0:T(8,128)(2,1)S(1)}, bf16[384,1536]{1,0:T(8,128)(2,1)S(1)}, u32[]{:S(2)}, u32[]{:S(2)}) %collective-permute-start.26) | collective-permute-done | bytes 1179680 | tf_op jit(solution)/shard_map/ppermute | solution.py:440
  111.4 2.4 %activation.5 = (bf16[512,1536]{1,0:T(8,128)(2,1)S(1)}, f32[512,1536]{1,0:T(8,128)S(1)}, f32[8,128]{1,0:T(8,128)S(1)}) custom-call(bf16[128,1536]{1,0:T(8,128)(2,1)S(1)} %copy-done.11, bf16[128,1536]{1,0:T(8,128)(2,1)S(1)} %copy-done.13, bf16[384,1536]{1,0:T(8,128)(2,1)S(1)} %get-tuple-element.181.refs_2_, ...), custom_call_target="tpu_custom_call" | custom-call | flops 10000000000 | tf_op jit(solution)/shard_map/activation/pallas_call | solution.py:270
  114.4 1.5 collective-permute-start.30
  115.9 1.1 project_down.23
  117.0 0.6 collective-permute-start.29
  118.1 0.8 project_down.24
  118.9 1.6 collective-permute-start.28
  120.5 0.8 project_down.25
  121.9 7.9 %down_gradient.5 = (bf16[6144,1536]{1,0:T(8,128)(2,1)}, f32[8,128]{1,0:T(8,128)S(1)}) custom-call(s32[1]{0:T(128)} %bitcast.refs_0_.half, s32[12,48]{1,0:T(8,128)S(1)} %bitcast.8, bf16[512,1536]{1,0:T(8,128)(2,1)S(1)} %get-tuple-element.161.refs_0_, bf16[512,1536]{1,0:T(8,128)(2,1)S(1)} %get-tuple-element.194.refs_1_, ...), custom_call_target="tpu_custom_call", output_to_operand_aliasing={{0}: (5, {})} | custom-call | flops 10000000000 | tf_op jit(solution)/shard_map/down_gradient/pallas_call | solution.py:403
  129.8 0.7 hidden_gradient.5
  130.6 6.1 %collective-permute-done.30.refs_3_ = bf16[384,768]{1,0:T(8,128)(2,1)S(1)} collective-permute-done((bf16[384,768]{1,0:T(8,128)(2,1)S(1)}, bf16[384,768]{1,0:T(8,128)(2,1)S(1)}, u32[]{:S(2)}, u32[]{:S(2)}) %collective-permute-start.30) | collective-permute-done | bytes 589856 | tf_op jit(solution)/shard_map/ppermute | solution.py:440
  136.7 0.7 hidden_gradient.6
  137.5 0.7 copy-done.20
  138.1 4.3 %up_gradient.8 = (bf16[1536,6144]{1,0:T(8,128)(2,1)}, f32[8,128]{1,0:T(8,128)S(1)}) custom-call(s32[1]{0:T(128)} %bitcast.refs_0_.half, s32[12,48]{1,0:T(8,128)S(1)} %copy-done.16, bf16[1536,512]{1,0:T(8,128)(2,1)S(1)} %copy-done.20, bf16[512,768]{1,0:T(8,128)(2,1)S(1)} %get-tuple-element.200.refs_1_, bf16[512,768]{1,0:T(8,128)(2,1)S(1)} %collective-permute-done.34.refs_2_, ...), custom_call_target="tpu_custom_call" | custom-call | flops 10000000000 | tf_op jit(solution)/shard_map/up_gradient/pallas_call | solution.py:403
  142.4 4.3 %up_gradient.9 = (bf16[1536,6144]{1,0:T(8,128)(2,1)}, f32[8,128]{1,0:T(8,128)S(1)}) custom-call(s32[1]{0:T(128)} %bitcast.refs_0_.half, s32[12,48]{1,0:T(8,128)S(1)} %copy-done.16, bf16[1536,512]{1,0:T(8,128)(2,1)S(1)} %copy-done.20, bf16[512,768]{1,0:T(8,128)(2,1)S(1)} %get-tuple-element.199.refs_1_, ...), custom_call_target="tpu_custom_call", output_to_operand_aliasing={{0}: (5, {})} | custom-call | flops 10000000000 | tf_op jit(solution)/shard_map/up_gradient/pallas_call | solution.py:403
  146.7 2.6 %collective-permute-done.29.refs_3_ = bf16[384,768]{1,0:T(8,128)(2,1)S(1)} collective-permute-done((bf16[384,768]{1,0:T(8,128)(2,1)S(1)}, bf16[384,768]{1,0:T(8,128)(2,1)S(1)}, u32[]{:S(2)}, u32[]{:S(2)}) %collective-permute-start.29) | collective-permute-done | bytes 589856 | tf_op jit(solution)/shard_map/ppermute | solution.py:440
  149.3 0.6 hidden_gradient.7
  150.1 2.8 %up_gradient.10 = (bf16[1536,6144]{1,0:T(8,128)(2,1)}, f32[8,128]{1,0:T(8,128)S(1)}) custom-call(s32[1]{0:T(128)} %bitcast.refs_0_.half, s32[12,48]{1,0:T(8,128)S(1)} %copy-done.16, bf16[1536,512]{1,0:T(8,128)(2,1)S(1)} %copy-done.20, bf16[512,768]{1,0:T(8,128)(2,1)S(1)} %get-tuple-element.205.refs_1_, ...), custom_call_target="tpu_custom_call", output_to_operand_aliasing={{0}: (4, {})} | custom-call | flops 10000000000 | tf_op jit(solution)/shard_map/up_gradient/pallas_call | solution.py:403
  152.9 2.8 %up_gradient.11 = (bf16[1536,6144]{1,0:T(8,128)(2,1)}, f32[8,128]{1,0:T(8,128)S(1)}) custom-call(s32[1]{0:T(128)S(6)} %sub.3.refs_1_.half, s32[12,48]{1,0:T(8,128)S(1)} %copy-done.16, bf16[1536,512]{1,0:T(8,128)(2,1)S(1)} %copy-done.20, bf16[512,768]{1,0:T(8,128)(2,1)S(1)} %collective-permute-done.35.refs_1_, ...), custom_call_target="tpu_custom_call", output_to_operand_aliasing={{0}: (4, {})} | custom-call | flops 10000000000 | tf_op jit(solution)/shard_map/up_gradient/pallas_call | solution.py:403
  156.5 2.0 %up_gradient.12 = (bf16[1536,6144]{1,0:T(8,128)(2,1)}, f32[8,128]{1,0:T(8,128)S(1)}) custom-call(s32[1]{0:T(128)} %bitcast.refs_0_.half, s32[12,48]{1,0:T(8,128)S(1)} %copy-done.16, bf16[1536,512]{1,0:T(8,128)(2,1)S(1)} %copy-done.20, bf16[512,384]{1,0:T(8,128)(2,1)S(1)} %get-tuple-element.211.refs_1_, ...), custom_call_target="tpu_custom_call", output_to_operand_aliasing={{0}: (4, {})} | custom-call | flops 10000000000 | tf_op jit(solution)/shard_map/up_gradient/pallas_call | solution.py:403
  158.5 2.0 %up_gradient.13 = (bf16[1536,6144]{1,0:T(8,128)(2,1)}, f32[8,128]{1,0:T(8,128)S(1)}) custom-call(s32[1]{0:T(128)S(6)} %sub.3.refs_1_.half, s32[12,48]{1,0:T(8,128)S(1)} %copy-done.16, bf16[1536,512]{1,0:T(8,128)(2,1)S(1)} %copy-done.20, bf16[512,384]{1,0:T(8,128)(2,1)S(1)} %collective-permute-done.36.refs_1_, ...), custom_call_target="tpu_custom_call", output_to_operand_aliasing={{0}: (4, {})} | custom-call | flops 10000000000 | tf_op jit(solution)/shard_map/up_gradient/pallas_call | solution.py:403
  160.6 0.7 collective-permute-done.27.refs_3_
  161.5 2.0 %up_gradient.14 = (bf16[1536,6144]{1,0:T(8,128)(2,1)}, f32[8,128]{1,0:T(8,128)S(1)}) custom-call(s32[1]{0:T(128)} %bitcast.refs_0_.half, s32[12,48]{1,0:T(8,128)S(1)} %copy-done.16, bf16[1536,512]{1,0:T(8,128)(2,1)S(1)} %copy-done.20, bf16[512,384]{1,0:T(8,128)(2,1)S(1)} %get-tuple-element.217.refs_1_, ...), custom_call_target="tpu_custom_call", output_to_operand_aliasing={{0}: (4, {})} | custom-call | flops 10000000000 | tf_op jit(solution)/shard_map/up_gradient/pallas_call | solution.py:403
  163.6 2.0 %up_gradient.15 = (bf16[1536,6144]{1,0:T(8,128)(2,1)}, f32[8,128]{1,0:T(8,128)}) custom-call(s32[1]{0:T(128)S(6)} %sub.3.refs_1_.half, s32[12,48]{1,0:T(8,128)S(1)} %copy-done.16, bf16[1536,512]{1,0:T(8,128)(2,1)S(1)} %copy-done.20, bf16[512,384]{1,0:T(8,128)(2,1)S(1)} %collective-permute-done.37.refs_1_, ...), custom_call_target="tpu_custom_call", output_to_operand_aliasing={{0}: (4, {})} | custom-call | flops 10000000000 | tf_op jit(solution)/shard_map/up_gradient/pallas_call | solution.py:403
  (108 shorter events, 8.6 us)
Async XLA Ops:
  0.7 8.4 %copy-start = (bf16[128,1536]{1,0:T(8,128)(2,1)S(1)}, bf16[128,1536]{1,0:T(8,128)(2,1)}, u32[]{:S(2)}) copy-start(bf16[128,1536]{1,0:T(8,128)(2,1)} %refs_0_.20) | copy-start | bytes 1179652
  0.7 8.4 %copy-start.15 = (s32[12,48]{1,0:T(8,128)S(1)}, s32[12,48]{1,0:T(8,128)}, u32[]{:S(2)}) copy-start(s32[12,48]{1,0:T(8,128)} %mask.15) | copy-start | bytes 6916
  3.9 20.5 %collective-permute-start = (bf16[128,1536]{1,0:T(8,128)(2,1)S(1)}, bf16[128,1536]{1,0:T(8,128)(2,1)S(1)}, u32[]{:S(2)}, u32[]{:S(2)}) collective-permute-start(bf16[128,1536]{1,0:T(8,128)(2,1)S(1)} %get-tuple-element.113), channel_id=1, source_target_pairs={{0,4},{4,8},{8,12},{12,0},{1,5},{5,9},{9,13},{13,1},{2,6},{6,10},{... | collective-permute-start | bytes 1179656 | tf_op jit(solution)/shard_map/ppermute | solution.py:428
  7.0 36.1 %collective-permute-start.1 = (bf16[128,1536]{1,0:T(8,128)(2,1)S(1)}, bf16[128,1536]{1,0:T(8,128)(2,1)S(1)}, u32[]{:S(2)}, u32[]{:S(2)}) collective-permute-start(bf16[128,1536]{1,0:T(8,128)(2,1)S(1)} %get-tuple-element.113), channel_id=1, source_target_pairs={{0,12},{4,0},{8,4},{12,8},{1,13},{5,1},{9,5},{13,9},{2,14},{6,2},{... | collective-permute-start | bytes 1179656 | tf_op jit(solution)/shard_map/ppermute | solution.py:428
  9.1 3.6 %collective-permute-start.2 = (bf16[128,1536]{1,0:T(8,128)(2,1)S(1)}, bf16[128,1536]{1,0:T(8,128)(2,1)S(1)}, u32[]{:S(2)}, u32[]{:S(2)}) collective-permute-start(bf16[128,1536]{1,0:T(8,128)(2,1)S(1)} %get-tuple-element.114), channel_id=1, source_target_pairs={{0,1},{1,0},{2,3},{3,2},{4,5},{5,4},{6,7},{7,6},{8,9},{9,8},{10,11... | collective-permute-start | bytes 1179656 | tf_op jit(solution)/shard_map/ppermute | solution.py:431
  12.1 12.4 %collective-permute-start.4 = (bf16[128,1536]{1,0:T(8,128)(2,1)S(1)}, bf16[128,1536]{1,0:T(8,128)(2,1)S(1)}, u32[]{:S(2)}, u32[]{:S(2)}) collective-permute-start(bf16[128,1536]{1,0:T(8,128)(2,1)S(1)} %get-tuple-element.121), channel_id=1, source_target_pairs={{0,1},{1,0},{2,3},{3,2},{4,5},{5,4},{6,7},{7,6},{8,9},{9,8},{10,11... | collective-permute-start | bytes 1179656 | tf_op jit(solution)/shard_map/ppermute | solution.py:431
  14.9 1.4 copy-start.17
  16.3 11.6 %collective-permute-start.5 = (bf16[128,768]{1,0:T(8,128)(2,1)S(1)}, bf16[128,768]{1,0:T(8,128)(2,1)S(1)}, u32[]{:S(2)}, u32[]{:S(2)}) collective-permute-start(bf16[128,768]{1,0:T(8,128)(2,1)S(1)} %get-tuple-element.124.refs_0_), channel_id=1, source_target_pairs={{0,2},{1,3},{2,0},{3,1},{4,6},{5,7},{6,4},{7,5},{8,10},{9,11},{10,... | collective-permute-start | bytes 589832 | tf_op jit(solution)/shard_map/ppermute | solution.py:440
  17.9 2.3 %copy-start.1 = (bf16[128,1536]{1,0:T(8,128)(2,1)S(1)}, bf16[128,1536]{1,0:T(8,128)(2,1)}, u32[]{:S(2)}) copy-start(bf16[128,1536]{1,0:T(8,128)(2,1)} %refs_0_.21) | copy-start | bytes 1179652
  17.9 2.3 %copy-start.14 = (s32[48,12]{0,1:T(8,128)S(1)}, s32[48,12]{0,1:T(8,128)}, u32[]{:S(2)}) copy-start(s32[48,12]{0,1:T(8,128)} %param.11) | copy-start | bytes 6916
  24.3 9.3 %collective-permute-start.7 = (bf16[128,1536]{1,0:T(8,128)(2,1)S(1)}, bf16[128,1536]{1,0:T(8,128)(2,1)S(1)}, u32[]{:S(2)}, u32[]{:S(2)}) collective-permute-start(bf16[128,1536]{1,0:T(8,128)(2,1)S(1)} %get-tuple-element.126), channel_id=1, source_target_pairs={{0,1},{1,0},{2,3},{3,2},{4,5},{5,4},{6,7},{7,6},{8,9},{9,8},{10,11... | collective-permute-start | bytes 1179656 | tf_op jit(solution)/shard_map/ppermute | solution.py:431
  27.5 6.2 %copy-start.10 = (bf16[128,1536]{1,0:T(8,128)(2,1)}, bf16[128,1536]{1,0:T(8,128)(2,1)S(1)}, u32[]{:S(2)}) copy-start(bf16[128,1536]{1,0:T(8,128)(2,1)S(1)} %get-tuple-element.130.refs_0_) | copy-start | bytes 1179652
  27.5 14.8 %collective-permute-start.8 = (bf16[128,1536]{1,0:T(8,128)(2,1)S(1)}, bf16[128,1536]{1,0:T(8,128)(2,1)S(1)}, u32[]{:S(2)}, u32[]{:S(2)}) collective-permute-start(bf16[128,1536]{1,0:T(8,128)(2,1)S(1)} %get-tuple-element.130.refs_0_), channel_id=1, source_target_pairs={{0,2},{1,3},{2,0},{3,1},{4,6},{5,7},{6,4},{7,5},{8,10},{9,11},{10,... | collective-permute-start | bytes 1179656 | tf_op jit(solution)/shard_map/ppermute | solution.py:440
  27.9 15.2 %collective-permute-start.3 = (bf16[128,1536]{1,0:T(8,128)(2,1)S(1)}, bf16[128,1536]{1,0:T(8,128)(2,1)S(1)}, u32[]{:S(2)}, u32[]{:S(2)}) collective-permute-start(bf16[128,1536]{1,0:T(8,128)(2,1)S(1)} %get-tuple-element.120), channel_id=1, source_target_pairs={{0,4},{4,8},{8,12},{12,0},{1,5},{5,9},{9,13},{13,1},{2,6},{6,10},{... | collective-permute-start | bytes 1179656 | tf_op jit(solution)/shard_map/ppermute | solution.py:428
  27.9 21.6 %collective-permute-start.12 = (bf16[128,768]{1,0:T(8,128)(2,1)S(1)}, bf16[128,768]{1,0:T(8,128)(2,1)S(1)}, u32[]{:S(2)}, u32[]{:S(2)}) collective-permute-start(bf16[128,768]{1,0:T(8,128)(2,1)S(1)} %get-tuple-element.143.refs_0_), channel_id=1, source_target_pairs={{0,2},{1,3},{2,0},{3,1},{4,6},{5,7},{6,4},{7,5},{8,10},{9,11},{10,... | collective-permute-start | bytes 589832 | tf_op jit(solution)/shard_map/ppermute | solution.py:440
  33.7 4.1 %collective-permute-start.6 = (bf16[128,1536]{1,0:T(8,128)(2,1)S(1)}, bf16[128,1536]{1,0:T(8,128)(2,1)S(1)}, u32[]{:S(2)}, u32[]{:S(2)}) collective-permute-start(bf16[128,1536]{1,0:T(8,128)(2,1)S(1)} %get-tuple-element.125), channel_id=1, source_target_pairs={{0,1},{1,0},{2,3},{3,2},{4,5},{5,4},{6,7},{7,6},{8,9},{9,8},{10,11... | collective-permute-start | bytes 1179656 | tf_op jit(solution)/shard_map/ppermute | solution.py:431
  37.8 4.5 %copy-start.6 = (bf16[128,1536]{1,0:T(8,128)(2,1)}, bf16[128,1536]{1,0:T(8,128)(2,1)S(1)}, u32[]{:S(2)}) copy-start(bf16[128,1536]{1,0:T(8,128)(2,1)S(1)} %get-tuple-element.142.refs_0_) | copy-start | bytes 1179652
  37.8 15.1 %collective-permute-start.11 = (bf16[128,1536]{1,0:T(8,128)(2,1)S(1)}, bf16[128,1536]{1,0:T(8,128)(2,1)S(1)}, u32[]{:S(2)}, u32[]{:S(2)}) collective-permute-start(bf16[128,1536]{1,0:T(8,128)(2,1)S(1)} %get-tuple-element.142.refs_0_), channel_id=1, source_target_pairs={{0,2},{1,3},{2,0},{3,1},{4,6},{5,7},{6,4},{7,5},{8,10},{9,11},{10,... | collective-permute-start | bytes 1179656 | tf_op jit(solution)/shard_map/ppermute | solution.py:440
  42.3 5.6 %copy-start.2 = (bf16[128,1536]{1,0:T(8,128)(2,1)}, bf16[128,1536]{1,0:T(8,128)(2,1)S(1)}, u32[]{:S(2)}) copy-start(bf16[128,1536]{1,0:T(8,128)(2,1)S(1)} %get-tuple-element.133.refs_0_) | copy-start | bytes 1179652
  42.3 0.8 copy-start.12
  43.6 1.1 copy-start.19
  43.6 1.7 copy-start.21
  44.8 10.9 %collective-permute-start.14 = (bf16[384,768]{1,0:T(8,128)(2,1)S(1)}, bf16[384,768]{1,0:T(8,128)(2,1)S(1)}, u32[]{:S(2)}, u32[]{:S(2)}) collective-permute-start(bf16[384,768]{1,0:T(8,128)(2,1)S(1)} %get-tuple-element.146), channel_id=1, source_target_pairs={{0,1},{1,0},{2,3},{3,2},{4,5},{5,4},{6,7},{7,6},{8,9},{9,8},{10,11... | collective-permute-start | bytes 1769480 | tf_op jit(solution)/shard_map/ppermute | solution.py:431
  47.6 17.2 %collective-permute-start.16 = (bf16[384,1536]{1,0:T(8,128)(2,1)S(1)}, bf16[384,1536]{1,0:T(8,128)(2,1)S(1)}, u32[]{:S(2)}, u32[]{:S(2)}) collective-permute-start(bf16[384,1536]{1,0:T(8,128)(2,1)S(1)} %get-tuple-element.152), channel_id=1, source_target_pairs={{0,1},{1,0},{2,3},{3,2},{4,5},{5,4},{6,7},{7,6},{8,9},{9,8},{10,11... | collective-permute-start | bytes 3538952 | tf_op jit(solution)/shard_map/ppermute | solution.py:431
  47.9 12.7 %collective-permute-start.9 = (bf16[128,1536]{1,0:T(8,128)(2,1)S(1)}, bf16[128,1536]{1,0:T(8,128)(2,1)S(1)}, u32[]{:S(2)}, u32[]{:S(2)}) collective-permute-start(bf16[128,1536]{1,0:T(8,128)(2,1)S(1)} %get-tuple-element.133.refs_0_), channel_id=1, source_target_pairs={{0,2},{1,3},{2,0},{3,1},{4,6},{5,7},{6,4},{7,5},{8,10},{9,11},{10,... | collective-permute-start | bytes 1179656 | tf_op jit(solution)/shard_map/ppermute | solution.py:440
  49.5 17.6 %collective-permute-start.10 = (bf16[128,1536]{1,0:T(8,128)(2,1)S(1)}, bf16[128,1536]{1,0:T(8,128)(2,1)S(1)}, u32[]{:S(2)}, u32[]{:S(2)}) collective-permute-start(bf16[128,1536]{1,0:T(8,128)(2,1)S(1)} %get-tuple-element.134), channel_id=1, source_target_pairs={{0,4},{4,8},{8,12},{12,0},{1,5},{5,9},{9,13},{13,1},{2,6},{6,10},{... | collective-permute-start | bytes 1179656 | tf_op jit(solution)/shard_map/ppermute | solution.py:428
  52.9 2.6 %copy-start.8 = (bf16[128,1536]{1,0:T(8,128)(2,1)}, bf16[128,1536]{1,0:T(8,128)(2,1)S(1)}, u32[]{:S(2)}) copy-start(bf16[128,1536]{1,0:T(8,128)(2,1)S(1)} %collective-permute-done.11.refs_3_.refs_1_) | copy-start | bytes 1179652
  52.9 1.6 copy-start.22
  54.5 1.7 %copy-start.18 = (bf16[1536,768]{1,0:T(8,128)(2,1)S(1)}, bf16[1536,768]{1,0:T(8,128)(2,1)}, u32[]{:S(2)}) copy-start(bf16[1536,768]{1,0:T(8,128)(2,1)} %copy-done.17) | copy-start | bytes 7077892
  55.6 3.2 %collective-permute-start.13 = (bf16[384,768]{1,0:T(8,128)(2,1)S(1)}, bf16[384,768]{1,0:T(8,128)(2,1)S(1)}, u32[]{:S(2)}, u32[]{:S(2)}) collective-permute-start(bf16[384,768]{1,0:T(8,128)(2,1)S(1)} %get-tuple-element.144), channel_id=1, source_target_pairs={{0,1},{1,0},{2,3},{3,2},{4,5},{5,4},{6,7},{7,6},{8,9},{9,8},{10,11... | collective-permute-start | bytes 1769480 | tf_op jit(solution)/shard_map/ppermute | solution.py:431
  57.2 16.3 %collective-permute-start.19 = (bf16[384,768]{1,0:T(8,128)(2,1)S(1)}, bf16[384,768]{1,0:T(8,128)(2,1)S(1)}, u32[]{:S(2)}, u32[]{:S(2)}) collective-permute-start(bf16[384,768]{1,0:T(8,128)(2,1)S(1)} %get-tuple-element.157.refs_2_), channel_id=1, source_target_pairs={{0,2},{1,3},{2,0},{3,1},{4,6},{5,7},{6,4},{7,5},{8,10},{9,11},{10,... | collective-permute-start | bytes 1769480 | tf_op jit(solution)/shard_map/ppermute | solution.py:440
  60.0 26.2 %collective-permute-start.18 = (bf16[384,768]{1,0:T(8,128)(2,1)S(1)}, bf16[384,768]{1,0:T(8,128)(2,1)S(1)}, u32[]{:S(2)}, u32[]{:S(2)}) collective-permute-start(bf16[384,768]{1,0:T(8,128)(2,1)S(1)} %get-tuple-element.156.refs_2_), channel_id=1, source_target_pairs={{0,2},{1,3},{2,0},{3,1},{4,6},{5,7},{6,4},{7,5},{8,10},{9,11},{10,... | collective-permute-start | bytes 1769480 | tf_op jit(solution)/shard_map/ppermute | solution.py:440
  60.5 6.6 %copy-start.4 = (bf16[128,1536]{1,0:T(8,128)(2,1)}, bf16[128,1536]{1,0:T(8,128)(2,1)S(1)}, u32[]{:S(2)}) copy-start(bf16[128,1536]{1,0:T(8,128)(2,1)S(1)} %collective-permute-done.9.refs_4_.refs_1_) | copy-start | bytes 1179652
  60.5 26.9 %collective-permute-start.15 = (bf16[128,1536]{1,0:T(8,128)(2,1)S(1)}, bf16[128,1536]{1,0:T(8,128)(2,1)S(1)}, u32[]{:S(2)}, u32[]{:S(2)}) collective-permute-start(bf16[128,1536]{1,0:T(8,128)(2,1)S(1)} %get-tuple-element.150), channel_id=1, source_target_pairs={{0,12},{4,0},{8,4},{12,8},{1,13},{5,1},{9,5},{13,9},{2,14},{6,2},{... | collective-permute-start | bytes 1179656 | tf_op jit(solution)/shard_map/ppermute | solution.py:428
  67.2 20.3 %collective-permute-start.17 = (bf16[128,1536]{1,0:T(8,128)(2,1)S(1)}, bf16[128,1536]{1,0:T(8,128)(2,1)S(1)}, u32[]{:S(2)}, u32[]{:S(2)}) collective-permute-start(bf16[128,1536]{1,0:T(8,128)(2,1)S(1)} %get-tuple-element.155), channel_id=1, source_target_pairs={{0,4},{4,8},{8,12},{12,0},{1,5},{5,9},{9,13},{13,1},{2,6},{6,10},{... | collective-permute-start | bytes 1179656 | tf_op jit(solution)/shard_map/ppermute | solution.py:428
  74.7 14.5 %collective-permute-start.21 = (bf16[512,768]{1,0:T(8,128)(2,1)S(1)}, bf16[512,768]{1,0:T(8,128)(2,1)S(1)}, u32[]{:S(2)}, u32[]{:S(2)}) collective-permute-start(bf16[512,768]{1,0:T(8,128)(2,1)S(1)} %get-tuple-element.168.refs_1_), channel_id=1, source_target_pairs={{0,1},{1,0},{2,3},{3,2},{4,5},{5,4},{6,7},{7,6},{8,9},{9,8},{10,11... | collective-permute-start | bytes 2359304 | tf_op jit(solution)/shard_map/ppermute | solution.py:431
  74.8 36.6 %collective-permute-start.26 = (bf16[384,1536]{1,0:T(8,128)(2,1)S(1)}, bf16[384,1536]{1,0:T(8,128)(2,1)S(1)}, u32[]{:S(2)}, u32[]{:S(2)}) collective-permute-start(bf16[384,1536]{1,0:T(8,128)(2,1)S(1)} %get-tuple-element.181.refs_2_), channel_id=1, source_target_pairs={{0,2},{1,3},{2,0},{3,1},{4,6},{5,7},{6,4},{7,5},{8,10},{9,11},{10,... | collective-permute-start | bytes 3538952 | tf_op jit(solution)/shard_map/ppermute | solution.py:440
  87.3 10.3 %collective-permute-start.23 = (bf16[512,768]{1,0:T(8,128)(2,1)S(1)}, bf16[512,768]{1,0:T(8,128)(2,1)S(1)}, u32[]{:S(2)}, u32[]{:S(2)}) collective-permute-start(bf16[512,768]{1,0:T(8,128)(2,1)S(1)} %get-tuple-element.173.refs_1_), channel_id=1, source_target_pairs={{0,1},{1,0},{2,3},{3,2},{4,5},{5,4},{6,7},{7,6},{8,9},{9,8},{10,11... | collective-permute-start | bytes 2359304 | tf_op jit(solution)/shard_map/ppermute | solution.py:431
  88.7 5.1 %collective-permute-start.20 = (bf16[384,768]{1,0:T(8,128)(2,1)S(1)}, bf16[384,768]{1,0:T(8,128)(2,1)S(1)}, u32[]{:S(2)}, u32[]{:S(2)}) collective-permute-start(bf16[384,768]{1,0:T(8,128)(2,1)S(1)} %get-tuple-element.167), channel_id=1, source_target_pairs={{0,1},{1,0},{2,3},{3,2},{4,5},{5,4},{6,7},{7,6},{8,9},{9,8},{10,11... | collective-permute-start | bytes 1769480 | tf_op jit(solution)/shard_map/ppermute | solution.py:431
  96.0 6.2 %collective-permute-start.22 = (bf16[384,768]{1,0:T(8,128)(2,1)S(1)}, bf16[384,768]{1,0:T(8,128)(2,1)S(1)}, u32[]{:S(2)}, u32[]{:S(2)}) collective-permute-start(bf16[384,768]{1,0:T(8,128)(2,1)S(1)} %get-tuple-element.172), channel_id=1, source_target_pairs={{0,1},{1,0},{2,3},{3,2},{4,5},{5,4},{6,7},{7,6},{8,9},{9,8},{10,11... | collective-permute-start | bytes 1769480 | tf_op jit(solution)/shard_map/ppermute | solution.py:431
  96.1 33.7 %collective-permute-start.31 = (bf16[384,768]{1,0:T(8,128)(2,1)S(1)}, bf16[384,768]{1,0:T(8,128)(2,1)S(1)}, u32[]{:S(2)}, u32[]{:S(2)}) collective-permute-start(bf16[384,768]{1,0:T(8,128)(2,1)S(1)} %get-tuple-element.192.refs_2_), channel_id=1, source_target_pairs={{0,2},{1,3},{2,0},{3,1},{4,6},{5,7},{6,4},{7,5},{8,10},{9,11},{10,... | collective-permute-start | bytes 1769480 | tf_op jit(solution)/shard_map/ppermute | solution.py:440
  104.4 11.5 %collective-permute-start.25 = (bf16[384,768]{1,0:T(8,128)(2,1)S(1)}, bf16[384,768]{1,0:T(8,128)(2,1)S(1)}, u32[]{:S(2)}, u32[]{:S(2)}) collective-permute-start(bf16[384,768]{1,0:T(8,128)(2,1)S(1)} %get-tuple-element.180), channel_id=1, source_target_pairs={{0,1},{1,0},{2,3},{3,2},{4,5},{5,4},{6,7},{7,6},{8,9},{9,8},{10,11... | collective-permute-start | bytes 1769480 | tf_op jit(solution)/shard_map/ppermute | solution.py:431
  104.6 6.8 %copy-start.11 = (bf16[128,1536]{1,0:T(8,128)(2,1)S(1)}, bf16[128,1536]{1,0:T(8,128)(2,1)}, u32[]{:S(2)}) copy-start(bf16[128,1536]{1,0:T(8,128)(2,1)} %copy-done.10) | copy-start | bytes 1179652
  104.6 6.8 %copy-start.13 = (bf16[128,1536]{1,0:T(8,128)(2,1)S(1)}, bf16[128,1536]{1,0:T(8,128)(2,1)}, u32[]{:S(2)}) copy-start(bf16[128,1536]{1,0:T(8,128)(2,1)} %copy-done.12) | copy-start | bytes 1179652
  113.8 7.5 %collective-permute-start.32 = (bf16[512,1536]{1,0:T(8,128)(2,1)S(1)}, bf16[512,1536]{1,0:T(8,128)(2,1)S(1)}, u32[]{:S(2)}, u32[]{:S(2)}) collective-permute-start(bf16[512,1536]{1,0:T(8,128)(2,1)S(1)} %get-tuple-element.194.refs_1_), channel_id=1, source_target_pairs={{0,1},{1,0},{2,3},{3,2},{4,5},{5,4},{6,7},{7,6},{8,9},{9,8},{10,11... | collective-permute-start | bytes 4718600 | tf_op jit(solution)/shard_map/ppermute | solution.py:431
  113.9 4.2 %collective-permute-start.24 = (bf16[384,768]{1,0:T(8,128)(2,1)S(1)}, bf16[384,768]{1,0:T(8,128)(2,1)S(1)}, u32[]{:S(2)}, u32[]{:S(2)}) collective-permute-start(bf16[384,768]{1,0:T(8,128)(2,1)S(1)} %get-tuple-element.179), channel_id=1, source_target_pairs={{0,1},{1,0},{2,3},{3,2},{4,5},{5,4},{6,7},{7,6},{8,9},{9,8},{10,11... | collective-permute-start | bytes 1769480 | tf_op jit(solution)/shard_map/ppermute | solution.py:431
  114.4 22.3 %collective-permute-start.30 = (bf16[384,768]{1,0:T(8,128)(2,1)S(1)}, bf16[384,768]{1,0:T(8,128)(2,1)S(1)}, u32[]{:S(2)}, u32[]{:S(2)}) collective-permute-start(bf16[384,768]{1,0:T(8,128)(2,1)S(1)} %get-tuple-element.190.refs_2_), channel_id=1, source_target_pairs={{0,2},{1,3},{2,0},{3,1},{4,6},{5,7},{6,4},{7,5},{8,10},{9,11},{10,... | collective-permute-start | bytes 1769480 | tf_op jit(solution)/shard_map/ppermute | solution.py:440
  117.0 32.3 %collective-permute-start.29 = (bf16[384,768]{1,0:T(8,128)(2,1)S(1)}, bf16[384,768]{1,0:T(8,128)(2,1)S(1)}, u32[]{:S(2)}, u32[]{:S(2)}) collective-permute-start(bf16[384,768]{1,0:T(8,128)(2,1)S(1)} %get-tuple-element.189.refs_2_), channel_id=1, source_target_pairs={{0,2},{1,3},{2,0},{3,1},{4,6},{5,7},{6,4},{7,5},{8,10},{9,11},{10,... | collective-permute-start | bytes 1769480 | tf_op jit(solution)/shard_map/ppermute | solution.py:440
  118.9 36.8 %collective-permute-start.28 = (bf16[384,384]{1,0:T(8,128)(2,1)S(1)}, bf16[384,384]{1,0:T(8,128)(2,1)S(1)}, u32[]{:S(2)}, u32[]{:S(2)}) collective-permute-start(bf16[384,384]{1,0:T(8,128)(2,1)S(1)} %get-tuple-element.188.refs_2_), channel_id=1, source_target_pairs={{0,2},{1,3},{2,0},{3,1},{4,6},{5,7},{6,4},{7,5},{8,10},{9,11},{10,... | collective-permute-start | bytes 884744 | tf_op jit(solution)/shard_map/ppermute | solution.py:440
  121.3 39.9 %collective-permute-start.27 = (bf16[384,384]{1,0:T(8,128)(2,1)S(1)}, bf16[384,384]{1,0:T(8,128)(2,1)S(1)}, u32[]{:S(2)}, u32[]{:S(2)}) collective-permute-start(bf16[384,384]{1,0:T(8,128)(2,1)S(1)} %get-tuple-element.186.refs_2_), channel_id=1, source_target_pairs={{0,2},{1,3},{2,0},{3,1},{4,6},{5,7},{6,4},{7,5},{8,10},{9,11},{10,... | collective-permute-start | bytes 884744 | tf_op jit(solution)/shard_map/ppermute | solution.py:440
  121.9 8.0 %copy-start.7 = (bf16[128,1536]{1,0:T(8,128)(2,1)S(1)}, bf16[128,1536]{1,0:T(8,128)(2,1)}, u32[]{:S(2)}) copy-start(bf16[128,1536]{1,0:T(8,128)(2,1)} %copy-done.6) | copy-start | bytes 1179652
  121.9 8.0 %copy-start.9 = (bf16[128,1536]{1,0:T(8,128)(2,1)S(1)}, bf16[128,1536]{1,0:T(8,128)(2,1)}, u32[]{:S(2)}) copy-start(bf16[128,1536]{1,0:T(8,128)(2,1)} %copy-done.8) | copy-start | bytes 1179652
  130.5 6.9 %collective-permute-start.34 = (bf16[512,768]{1,0:T(8,128)(2,1)S(1)}, bf16[512,768]{1,0:T(8,128)(2,1)S(1)}, u32[]{:S(2)}, u32[]{:S(2)}) collective-permute-start(bf16[512,768]{1,0:T(8,128)(2,1)S(1)} %get-tuple-element.200.refs_1_), channel_id=1, source_target_pairs={{0,1},{1,0},{2,3},{3,2},{4,5},{5,4},{6,7},{7,6},{8,9},{9,8},{10,11... | collective-permute-start | bytes 2359304 | tf_op jit(solution)/shard_map/ppermute | solution.py:431
  136.7 0.8 copy-start.16
  136.7 1.4 copy-start.20
  137.4 5.1 %collective-permute-start.33 = (bf16[512,768]{1,0:T(8,128)(2,1)S(1)}, bf16[512,768]{1,0:T(8,128)(2,1)S(1)}, u32[]{:S(2)}, u32[]{:S(2)}) collective-permute-start(bf16[512,768]{1,0:T(8,128)(2,1)S(1)} %get-tuple-element.199.refs_1_), channel_id=1, source_target_pairs={{0,1},{1,0},{2,3},{3,2},{4,5},{5,4},{6,7},{7,6},{8,9},{9,8},{10,11... | collective-permute-start | bytes 2359304 | tf_op jit(solution)/shard_map/ppermute | solution.py:431
  142.4 6.9 %copy-start.3 = (bf16[128,1536]{1,0:T(8,128)(2,1)S(1)}, bf16[128,1536]{1,0:T(8,128)(2,1)}, u32[]{:S(2)}) copy-start(bf16[128,1536]{1,0:T(8,128)(2,1)} %copy-done.2) | copy-start | bytes 1179652
  142.4 6.9 %copy-start.5 = (bf16[128,1536]{1,0:T(8,128)(2,1)S(1)}, bf16[128,1536]{1,0:T(8,128)(2,1)}, u32[]{:S(2)}) copy-start(bf16[128,1536]{1,0:T(8,128)(2,1)} %copy-done.4) | copy-start | bytes 1179652
  150.0 2.9 %collective-permute-start.35 = (bf16[512,768]{1,0:T(8,128)(2,1)S(1)}, bf16[512,768]{1,0:T(8,128)(2,1)S(1)}, u32[]{:S(2)}, u32[]{:S(2)}) collective-permute-start(bf16[512,768]{1,0:T(8,128)(2,1)S(1)} %get-tuple-element.205.refs_1_), channel_id=1, source_target_pairs={{0,1},{1,0},{2,3},{3,2},{4,5},{5,4},{6,7},{7,6},{8,9},{9,8},{10,11... | collective-permute-start | bytes 2359304 | tf_op jit(solution)/shard_map/ppermute | solution.py:431
  156.0 2.6 %collective-permute-start.36 = (bf16[512,384]{1,0:T(8,128)(2,1)S(1)}, bf16[512,384]{1,0:T(8,128)(2,1)S(1)}, u32[]{:S(2)}, u32[]{:S(2)}) collective-permute-start(bf16[512,384]{1,0:T(8,128)(2,1)S(1)} %get-tuple-element.211.refs_1_), channel_id=1, source_target_pairs={{0,1},{1,0},{2,3},{3,2},{4,5},{5,4},{6,7},{7,6},{8,9},{9,8},{10,11... | collective-permute-start | bytes 1179656 | tf_op jit(solution)/shard_map/ppermute | solution.py:431
  161.5 2.1 %collective-permute-start.37 = (bf16[512,384]{1,0:T(8,128)(2,1)S(1)}, bf16[512,384]{1,0:T(8,128)(2,1)S(1)}, u32[]{:S(2)}, u32[]{:S(2)}) collective-permute-start(bf16[512,384]{1,0:T(8,128)(2,1)S(1)} %get-tuple-element.217.refs_1_), channel_id=1, source_target_pairs={{0,1},{1,0},{2,3},{3,2},{4,5},{5,4},{6,7},{7,6},{8,9},{9,8},{10,11... | collective-permute-start | bytes 1179656 | tf_op jit(solution)/shard_map/ppermute | solution.py:431
